TPU v7x, 32 devices: a whole 2x2x4 slice. The times are simulated.
32 devices in a mesh: groups: 2 (over x), adapter: 16 (over z, y, core).
Axes of the slice: x: 2, y: 2, z: 4, core: 2. Of those that a mesh axis runs over, the one named last changes fastest.
Arguments:
- activations: bfloat16 [4096, 8192], P(('groups', 'adapter')), parts along dimension 0, may hold values from -6 to 6
- cotangent: bfloat16 [4096, 1024], P(('groups', 'adapter')), parts along dimension 0, may hold values from -1.5 to 1.5
- family: int32 [4096], P(('groups', 'adapter')), parts along dimension 0, may hold values from 0 to 127, as said below
- value_weight: bfloat16 [8192, 1024], P('adapter'), may hold values from -0.1875 to 0.1875
- adapter_down: bfloat16 [8192, 8192], P(None, 'adapter'), may hold values from -0.0625 to 0.0625
- adapter_up: bfloat16 [8192, 1024], P('adapter'), may hold values from -0.1875 to 0.1875
Outputs:
- input_gradient: bfloat16 [4096, 8192], P(('groups', 'adapter')), parts along dimension 0
- grad_down: bfloat16 [16384, 8192], P('groups', 'adapter'), parts along dimension 0
- grad_up: bfloat16 [8192, 2048], P('adapter', 'groups'), parts along dimension 1
There are 2 independent parts, one for each index of `groups`. A program takes and returns all parts, laid end to end along the dimension named above; an argument that names none is the same for every part. Nothing has to cross between parts.
Inputs may be any that keep to these rules, and one draw needn't show every extreme that they name: Family f is owned by index f // 8 of adapter. Among the 128 tokens of one index of adapter, those whose families one index owns all have the same family, and there are at most 16 of them; in every draw one owner receives exactly 16 tokens from every index of adapter.
All inputs are finite; a program needn't handle non-finite values.
Results may differ from a plain program's by a relative error of at most 0.0085.
Values may be sent and summed in bfloat16 or wider, within the bound.
No kernel may reach another device: no remote copies, remote signals or barrier semaphores. Data moves between devices by JAX's collectives and lax.ppermute only.
A program may use at most 128 MiB of HBM per device.

v0:
```python
import jax
import jax.numpy as jnp
from jax import lax
from jax.sharding import PartitionSpec as P

ADAPTER_RANK = 64
FAM_DEV = 8


SCALE = 2.0


def local(activations, cotangent, family, value_weight, adapter_down, adapter_up):
    count = lax.axis_size("adapter")
    tok_rows = activations.shape[0]
    width = activations.shape[1]
    cap = max(2, (2 * tok_rows + count - 1) // count)
    token_slots = count * cap
    owner = family // FAM_DEV
    local_family = family % FAM_DEV
    owner_hits = (owner[:, None] == jnp.arange(count, dtype=jnp.int32)[None, :]).astype(jnp.int32)
    earlier = jnp.cumsum(owner_hits, axis=0) - owner_hits
    rank_within = jnp.sum(earlier * owner_hits, axis=1)
    token_position = owner * cap + rank_within
    token_at = (
        jnp.full((token_slots,), tok_rows, jnp.int32)
        .at[token_position]
        .set(jnp.arange(tok_rows, dtype=jnp.int32))
    )
    padded_x = jnp.concatenate([activations, jnp.zeros((1, width), jnp.bfloat16)], axis=0)
    padded_dy = jnp.concatenate(
        [cotangent, jnp.zeros((1, cotangent.shape[1]), jnp.bfloat16)], axis=0
    )
    padded_family = jnp.concatenate([local_family, jnp.zeros((1,), jnp.int32)], axis=0)
    send_x = padded_x[token_at]
    send_dy = padded_dy[token_at]
    send_family = padded_family[token_at]
    received_input, received_gradient, recv_family = (
        lax.all_to_all(send_x, "adapter", split_axis=0, concat_axis=0, tiled=True),
        lax.all_to_all(send_dy, "adapter", split_axis=0, concat_axis=0, tiled=True),
        lax.all_to_all(send_family, "adapter", split_axis=0, concat_axis=0, tiled=True),
    )
    total_columns = adapter_down.shape[1]
    column_family = jnp.arange(total_columns, dtype=jnp.int32) // ADAPTER_RANK
    selected_rows = (column_family[None, :] == recv_family[:, None]).astype(jnp.float32)
    low_rank_product = (
        jnp.dot(received_input, adapter_down, preferred_element_type=jnp.float32) * selected_rows
    ).astype(jnp.bfloat16)
    backward_rows = (
        lax.dot_general(
            received_gradient,
            adapter_up,
            (((1,), (1,)), ((), ())),
            preferred_element_type=jnp.float32,
        )
        * selected_rows
    ).astype(jnp.bfloat16)
    grad_down = (
        SCALE
        * lax.dot_general(
            received_input,
            backward_rows,
            (((0,), (0,)), ((), ())),
            preferred_element_type=jnp.float32,
        )
    ).astype(jnp.bfloat16)
    grad_up = (
        SCALE
        * lax.dot_general(
            low_rank_product,
            received_gradient,
            (((0,), (0,)), ((), ())),
            preferred_element_type=jnp.float32,
        )
    ).astype(jnp.bfloat16)
    adapter_rows = (
        SCALE
        * lax.dot_general(
            backward_rows,
            adapter_down,
            (((1,), (1,)), ((), ())),
            preferred_element_type=jnp.float32,
        )
    ).astype(jnp.bfloat16)
    returned_rows = lax.all_to_all(adapter_rows, "adapter", split_axis=0, concat_axis=0, tiled=True)
    adapter_part = returned_rows[token_position]
    frozen_part = lax.dot_general(
        cotangent,
        lax.all_gather(value_weight, "adapter", axis=0, tiled=True),
        (((1,), (1,)), ((), ())),
        preferred_element_type=jnp.float32,
    ).astype(jnp.bfloat16)
    input_gradient = (frozen_part.astype(jnp.float32) + adapter_part.astype(jnp.float32)).astype(
        jnp.bfloat16
    )
    return (input_gradient, grad_down, grad_up)


def solution(mesh):
    in_specs = (
        P(("groups", "adapter"), None),
        P(("groups", "adapter"), None),
        P(("groups", "adapter")),
        P("adapter", None),
        P(None, "adapter"),
        P("adapter", None),
    )
    out_specs = (P(("groups", "adapter"), None), P("groups", "adapter"), P("adapter", "groups"))
    return jax.shard_map(local, mesh=mesh, in_specs=in_specs, out_specs=out_specs, check_vma=False)
```

profile of v0, /device:TPU:15, one launch (start us, length us, event | category | flops | bytes accessed | tf_op | source)
XLA Modules:
  0.0 349.2 jit_solution(15760131832531693024)
XLA Ops:
  7.2 0.7 all-gather.2.cloned.1.call-update
  7.9 0.7 and_select_fusion.1
  9.0 1.0 scatter_custom_fusion
  10.1 1.9 gather_fusion
  12.0 0.7 all_to_all.30
  12.7 6.6 %all-to-all-start = ((s32[16,16,1]{1,2,0:T(1,128)}), s32[16,16,1]{1,2,0:T(1,128)S(1)}, u32[]{:S(2)}, u32[]{:S(2)}) async-start(s32[16,16,1]{1,2,0:T(1,128)} %bitcast), calls=%async_computation | async-start | bytes 16384 | tf_op jit(solution)/shard_map/all_to_all | solution.py:41
  19.3 1.0 concatenate.10
  20.3 2.0 gather_fusion.1
  22.2 0.8 all-to-all-done
  23.0 6.8 %all-to-all-start.1 = ((bf16[16,16,1024]{2,1,0:T(8,128)(2,1)}), bf16[16,16,1024]{2,1,0:T(8,128)(2,1)}, u32[]{:S(2)}, u32[]{:S(2)}) async-start(bf16[16,16,1024]{2,1,0:T(8,128)(2,1)} %bitcast.1), calls=%async_computation.1 | async-start | bytes 1048576 | tf_op jit(solution)/shard_map/all_to_all | solution.py:40
  29.8 1.8 concatenate.11
  31.6 5.2 %gather_fusion.3 = bf16[256,8192]{1,0:T(8,128)(2,1)} fusion(bf16[129,8192]{1,0:T(8,128)(2,1)S(1)} %concatenate.11, s32[1024]{0:T(1024)S(1)} %pad_clamp_fusion.1), kind=kCustom, calls=%fused_computation.3 | custom fusion | bytes 8389632 | tf_op jit(solution)/shard_map/gather | solution.py:35
  36.8 21.1 %all-to-all-done.1 = bf16[16,16,1024]{2,1,0:T(8,128)(2,1)} async-done(((bf16[16,16,1024]{2,1,0:T(8,128)(2,1)}), bf16[16,16,1024]{2,1,0:T(8,128)(2,1)}, u32[]{:S(2)}, u32[]{:S(2)}) %all-to-all-start.1) | async-done | bytes 524320 | tf_op jit(solution)/shard_map/all_to_all | solution.py:40
  57.9 5.2 %all-to-all-start.3 = ((bf16[16,16,8192]{2,1,0:T(8,128)(2,1)}), bf16[16,16,8192]{2,1,0:T(8,128)(2,1)}, u32[]{:S(2)}, u32[]{:S(2)}) async-start(bf16[16,16,8192]{2,1,0:T(8,128)(2,1)} %bitcast.19), calls=%async_computation.3 | async-start | bytes 8388608 | tf_op jit(solution)/shard_map/all_to_all | solution.py:39
  63.7 0.7 reduce.3
  64.5 1.5 fusion.5
  66.0 7.7 %fusion = bf16[256,8192]{1,0:T(8,128)(2,1)} fusion(bf16[256,512]{1,0:T(8,128)(2,1)S(1)} %fusion.5, bf16[8192,512]{1,0:T(8,128)(2,1)} %param.10), kind=kOutput, calls=%fused_computation.7 | convolution fusion | flops 2151677952 | bytes 12845056 | tf_op jit(solution)/shard_map/dot_general | solution.py:78
  73.7 152.4 %all-to-all-done.3 = bf16[16,16,8192]{2,1,0:T(8,128)(2,1)} async-done(((bf16[16,16,8192]{2,1,0:T(8,128)(2,1)}), bf16[16,16,8192]{2,1,0:T(8,128)(2,1)}, u32[]{:S(2)}, u32[]{:S(2)}) %all-to-all-start.3) | async-done | bytes 4194336 | tf_op jit(solution)/shard_map/all_to_all | solution.py:39
  226.1 4.7 %all-to-all-start.2 = ((bf16[16,16,8192]{2,1,0:T(8,128)(2,1)}), bf16[16,16,8192]{2,1,0:T(8,128)(2,1)}, u32[]{:S(2)}, u32[]{:S(2)}) async-start(bf16[16,16,8192]{2,1,0:T(8,128)(2,1)} %bitcast.20), calls=%async_computation.2 | async-start | bytes 8388608 | tf_op jit(solution)/shard_map/all_to_all | solution.py:85
  230.7 8.4 %multiply_convert_fusion.1 = bf16[512,1024]{1,0:T(8,128)(2,1)} fusion(bf16[256,1024]{1,0:T(8,128)(2,1)} %bitcast.2, bf16[256,8192]{1,0:T(8,128)(2,1)} %bitcast.6, bf16[8192,512]{1,0:T(8,128)(2,1)} %param.10, s32[512]{0:T(512)S(1)} %add_select_fusion, s32[256]{0:T(256)S(1)} %eq.34), kind=kOutput, calls=%fused_computation.12 | convolution fusion | flops 2417360896 | bytes 14158848 | tf_op jit(solution)/shard_map/dot_general | solution.py:69
  239.1 8.0 %multiply_convert_fusion = bf16[8192,512]{1,0:T(8,128)(2,1)} fusion(bf16[256,8192]{1,0:T(8,128)(2,1)} %bitcast.6, bf16[256,512]{1,0:T(8,128)(2,1)S(1)} %fusion.5), kind=kOutput, calls=%fused_computation.5 | convolution fusion | flops 2155872256 | bytes 12845056 | tf_op jit(solution)/shard_map/dot_general | solution.py:60
  247.1 76.0 %all-to-all-done.2 = bf16[16,16,8192]{2,1,0:T(8,128)(2,1)} async-done(((bf16[16,16,8192]{2,1,0:T(8,128)(2,1)}), bf16[16,16,8192]{2,1,0:T(8,128)(2,1)}, u32[]{:S(2)}, u32[]{:S(2)}) %all-to-all-start.2) | async-done | bytes 4194336 | tf_op jit(solution)/shard_map/all_to_all | solution.py:85
  323.1 6.5 %gather_fusion.2 = bf16[128,8192]{1,0:T(8,128)(2,1)S(1)} fusion(bf16[256,8192]{1,0:T(8,128)(2,1)} %bitcast.4, s32[1024]{0:T(1024)S(1)} %pad_clamp_fusion), kind=kCustom, calls=%fused_computation.2 | custom fusion | bytes 4194816 | tf_op jit(solution)/shard_map/gather | solution.py:86
  329.7 12.7 %fusion.3 = bf16[128,8192]{1,0:T(8,128)(2,1)} fusion(bf16[128,1024]{1,0:T(8,128)(2,1)S(1)} %copy-done.1, bf16[8192,1024]{1,0:T(8,128)(2,1)} %all-gather.2.cloned.1.call-done, bf16[128,8192]{1,0:T(8,128)(2,1)S(1)} %gather_fusion.2), kind=kOutput, calls=%fused_computation.11 | convolution fusion | flops 2152726528 | bytes 21233664 | tf_op jit(solution)/shard_map/dot_general | solution.py:87
  (18 shorter events, 1.1 us)
Async XLA Ops:
  7.2 57.3 %copy-start = (bf16[512,1024]{1,0:T(8,128)(2,1)S(1)}, bf16[512,1024]{1,0:T(8,128)(2,1)}, u32[]{:S(2)}) copy-start(bf16[512,1024]{1,0:T(8,128)(2,1)} %param.11) | copy-start | bytes 3145732
  7.2 322.5 %all-gather.2.cloned.1.call-start = ((), (), s32[]{:S(2)}) async-start(), calls=%async_computation.4 | async-start | bytes 17825792 | tf_op jit(solution)/shard_map/all_gather | solution.py:89
  12.7 10.3 %all-to-all-start = ((s32[16,16,1]{1,2,0:T(1,128)}), s32[16,16,1]{1,2,0:T(1,128)S(1)}, u32[]{:S(2)}, u32[]{:S(2)}) async-start(s32[16,16,1]{1,2,0:T(1,128)} %bitcast), calls=%async_computation | async-start | bytes 16384 | tf_op jit(solution)/shard_map/all_to_all | solution.py:41
  23.0 34.9 %all-to-all-start.1 = ((bf16[16,16,1024]{2,1,0:T(8,128)(2,1)}), bf16[16,16,1024]{2,1,0:T(8,128)(2,1)}, u32[]{:S(2)}, u32[]{:S(2)}) async-start(bf16[16,16,1024]{2,1,0:T(8,128)(2,1)} %bitcast.1), calls=%async_computation.1 | async-start | bytes 1048576 | tf_op jit(solution)/shard_map/all_to_all | solution.py:40
  57.9 168.1 %all-to-all-start.3 = ((bf16[16,16,8192]{2,1,0:T(8,128)(2,1)}), bf16[16,16,8192]{2,1,0:T(8,128)(2,1)}, u32[]{:S(2)}, u32[]{:S(2)}) async-start(bf16[16,16,8192]{2,1,0:T(8,128)(2,1)} %bitcast.19), calls=%async_computation.3 | async-start | bytes 8388608 | tf_op jit(solution)/shard_map/all_to_all | solution.py:39
  226.1 97.0 %all-to-all-start.2 = ((bf16[16,16,8192]{2,1,0:T(8,128)(2,1)}), bf16[16,16,8192]{2,1,0:T(8,128)(2,1)}, u32[]{:S(2)}, u32[]{:S(2)}) async-start(bf16[16,16,8192]{2,1,0:T(8,128)(2,1)} %bitcast.20), calls=%async_computation.2 | async-start | bytes 8388608 | tf_op jit(solution)/shard_map/all_to_all | solution.py:85
  323.1 6.6 %copy-start.1 = (bf16[128,1024]{1,0:T(8,128)(2,1)S(1)}, bf16[128,1024]{1,0:T(8,128)(2,1)}, u32[]{:S(2)}) copy-start(bf16[128,1024]{1,0:T(8,128)(2,1)} %param.7) | copy-start | bytes 786436
Sparse Core Ops, SparseCore 0:
  10.2 211.6 all-gather.1
where the time goes:
time: 350 us; the launch traced here: 349 us
  waiting for transfers between devices  251 us (72%)
  matrix products  38.3 us (11%)
  starting transfers between devices  23.2 us (7%)
  local copies, waits for them, and re-layouts  20.7 us (6%)
  between operations  14.2 us (4%)
    all_to_all x1, waiting for transfers between devices, local(): lax.all_to_all(send_x, 'adapter', split_axis=0, concat_axis=0, tiled=True)  152 us
    all_to_all x1, waiting for transfers between devices, local(): lax.all_to_all(adapter_rows, 'adapter', split_axis=0, concat_axis=0, tile...  76 us
    all_to_all x1, waiting for transfers between devices, local(): lax.all_to_all(send_dy, 'adapter', split_axis=0, concat_axis=0, tiled=True)  21.1 us
    dot_general x1, matrix products, local(): lax.dot_general(cotangent, lax.all_gather(value_weight, 'adapter', axis=0...  12.7 us
    dot_general x1, matrix products, local(): lax.dot_general(low_rank_product, received_gradient, (((0,), (0,)), ((),...  8.37 us
    dot_general x1, matrix products, local(): lax.dot_general(received_input, backward_rows, (((0,), (0,)), ((), ())),...  7.97 us
    dot_general x1, matrix products, local(): lax.dot_general(backward_rows, adapter_down, (((1,), (1,)), ((), ())), pr...  7.71 us
  transfers between devices with their start and end apart: 5, of which 4 were waited for; matrix products, arithmetic and copies ran while one was open for 14% of the time, Pallas kernels for 0%

commit v1 on v0

v1 whole, which is shorter than its diff:
```python
import functools

import jax
import jax.numpy as jnp
from jax import lax
from jax.experimental import pallas as pl
from jax.experimental.pallas import tpu as pltpu
from jax.sharding import PartitionSpec as P

ADAPTER_RANK = 64
FAM_DEV = 8
PLANE = 8
LANES = 128
BLOCK = 1024
VMEM = 60 << 20


SCALE = 2.0


def dot(a, b, dims):
    return lax.dot_general(a, b, (dims, ((), ())), preferred_element_type=jnp.float32)


def pack_kernel(cap, family_ref, dy_ref, out_ref, place_ref, back_place_ref):
    tok_rows, features = dy_ref.shape
    token_slots = out_ref.shape[0]
    square = (tok_rows, tok_rows)
    along = jnp.broadcast_to(family_ref[...], square)
    down = along.T
    same = (along // FAM_DEV) == (down // FAM_DEV)
    row = lax.broadcasted_iota(jnp.int32, square, 0)
    column = lax.broadcasted_iota(jnp.int32, square, 1)
    rank_down = jnp.sum((same & (column < row)).astype(jnp.int32), axis=1, keepdims=True)
    rank_along = jnp.sum((same & (row < column)).astype(jnp.int32), axis=0, keepdims=True)
    slot_down = (down[:, :1] // FAM_DEV) * cap + rank_down
    slot_along = (along[:1] // FAM_DEV) * cap + rank_along
    slots = lax.broadcasted_iota(jnp.int32, (token_slots, tok_rows), 0)
    place = jnp.where(slots == slot_along, 1.0, 0.0).astype(jnp.bfloat16)
    place_ref[...] = place
    slots = lax.broadcasted_iota(jnp.int32, (tok_rows, token_slots), 1)
    back_place_ref[...] = jnp.where(slots == slot_down, 1.0, 0.0).astype(jnp.bfloat16)
    out_ref[:, :features] = dot(place, dy_ref[...], ((1,), (0,))).astype(jnp.bfloat16)
    families = (down % FAM_DEV).astype(jnp.float32)[:, :LANES].astype(jnp.bfloat16)
    out_ref[:, features:] = dot(place, families, ((1,), (0,))).astype(jnp.bfloat16)


def pack(family, cotangent, cap, token_slots):
    tok_rows, features = cotangent.shape
    return pl.pallas_call(
        functools.partial(pack_kernel, cap),
        out_shape=[
            jax.ShapeDtypeStruct((token_slots, features + LANES), jnp.bfloat16),
            jax.ShapeDtypeStruct((token_slots, tok_rows), jnp.bfloat16),
            jax.ShapeDtypeStruct((tok_rows, token_slots), jnp.bfloat16),
        ],
        compiler_params=pltpu.CompilerParams(vmem_limit_bytes=VMEM),
    )(family.reshape(1, tok_rows), cotangent)


def own_columns(family_ref, columns):
    shape = (family_ref.shape[0], columns)
    column_family = lax.broadcasted_iota(jnp.int32, shape, 1) // ADAPTER_RANK
    return column_family == family_ref[:, :1].astype(jnp.int32)


def rows_kernel(dy_ref, family_ref, up_ref, down_ref, rows_ref, backward_ref):
    @pl.when(pl.program_id(0) == 0)
    def _():
        back = dot(dy_ref[...], up_ref[...], ((1,), (1,)))
        keep = own_columns(family_ref, back.shape[1])
        backward_ref[...] = jnp.where(keep, back, 0.0).astype(jnp.bfloat16)

    rows = dot(backward_ref[...], down_ref[...], ((1,), (1,)))
    rows_ref[...] = (SCALE * rows).astype(jnp.bfloat16)


def make_rows(received, adapter_up, adapter_down):
    token_slots = received.shape[0]
    columns, features = adapter_up.shape
    width = adapter_down.shape[0]
    return pl.pallas_call(
        rows_kernel,
        grid=(width // BLOCK,),
        in_specs=[
            pl.BlockSpec((token_slots, features), lambda j: (0, 0)),
            pl.BlockSpec((token_slots, LANES), lambda j: (0, features // LANES)),
            pl.BlockSpec((columns, features), lambda j: (0, 0)),
            pl.BlockSpec((BLOCK, columns), lambda j: (j, 0)),
        ],
        out_specs=[
            pl.BlockSpec((token_slots, BLOCK), lambda j: (0, j)),
            pl.BlockSpec((token_slots, columns), lambda j: (0, 0)),
        ],
        out_shape=[
            jax.ShapeDtypeStruct((token_slots, width), jnp.bfloat16),
            jax.ShapeDtypeStruct((token_slots, columns), jnp.bfloat16),
        ],
        compiler_params=pltpu.CompilerParams(vmem_limit_bytes=VMEM),
        cost_estimate=pl.CostEstimate(
            flops=2 * token_slots * columns * (width + features),
            bytes_accessed=2 * (columns + token_slots) * (width + features),
            transcendentals=0,
        ),
    )(received, received, adapter_up, adapter_down)


def grads_kernel(x_ref, dy_ref, family_ref, backward_ref, down_ref, grad_down_ref, grad_up_ref, low_ref):
    step = pl.program_id(0)

    @pl.when(step == 0)
    def _():
        low_ref[...] = jnp.zeros_like(low_ref)

    low_ref[...] += dot(x_ref[...], down_ref[...], ((1,), (0,)))
    grad_down = dot(x_ref[...], backward_ref[...], ((0,), (0,)))
    grad_down_ref[...] = (SCALE * grad_down).astype(jnp.bfloat16)

    @pl.when(step == pl.num_programs(0) - 1)
    def _():
        keep = own_columns(family_ref, low_ref.shape[1])
        low = jnp.where(keep, low_ref[...], 0.0).astype(jnp.bfloat16)
        grad_up = dot(low, dy_ref[...], ((0,), (0,)))
        grad_up_ref[...] = (SCALE * grad_up).astype(jnp.bfloat16)


def make_grads(received_input, received, backward_rows, adapter_up, adapter_down):
    token_slots = received.shape[0]
    columns, features = adapter_up.shape
    width = adapter_down.shape[0]
    return pl.pallas_call(
        grads_kernel,
        grid=(width // BLOCK,),
        in_specs=[
            pl.BlockSpec((token_slots, BLOCK), lambda j: (0, j)),
            pl.BlockSpec((token_slots, features), lambda j: (0, 0)),
            pl.BlockSpec((token_slots, LANES), lambda j: (0, features // LANES)),
            pl.BlockSpec((token_slots, columns), lambda j: (0, 0)),
            pl.BlockSpec((BLOCK, columns), lambda j: (j, 0)),
        ],
        out_specs=[
            pl.BlockSpec((BLOCK, columns), lambda j: (j, 0)),
            pl.BlockSpec((columns, features), lambda j: (0, 0)),
        ],
        out_shape=[
            jax.ShapeDtypeStruct((width, columns), jnp.bfloat16),
            jax.ShapeDtypeStruct((columns, features), jnp.bfloat16),
        ],
        scratch_shapes=[pltpu.VMEM((token_slots, columns), jnp.float32)],
        compiler_params=pltpu.CompilerParams(vmem_limit_bytes=VMEM),
        cost_estimate=pl.CostEstimate(
            flops=2 * token_slots * columns * (2 * width + features),
            bytes_accessed=2 * (2 * columns + token_slots) * (width + features),
            transcendentals=0,
        ),
    )(received_input, received, received, backward_rows, adapter_down)


def finish_kernel(share, groups, at_ref, place_ref, rows_ref, base_ref, out_ref):
    inner = PLANE // groups
    for layer in range(base_ref.shape[2] // share):
        for block in range(PLANE):
            start = (layer * PLANE + block) * share
            columns = slice(start, start + share)
            adapter_part = dot(place_ref[...], rows_ref[:, columns], ((1,), (0,)))
            inner_shift = lax.rem(at_ref[0] - block // groups + inner, inner)
            group_shift = lax.rem(at_ref[1] - block % groups + groups, groups)
            base = base_ref[inner_shift * groups + group_shift]
            base = base[:, layer * share : (layer + 1) * share].astype(jnp.float32)
            out_ref[:, columns] = (base + adapter_part).astype(jnp.bfloat16)


def finish(at, place, rows, base, deep, groups):
    tok_rows, token_slots = place.shape
    width = rows.shape[1]
    share = base.shape[2] // deep
    layers = max(1, LANES // share)
    steps = deep // layers
    return pl.pallas_call(
        functools.partial(finish_kernel, share, groups),
        grid_spec=pltpu.PrefetchScalarGridSpec(
            num_scalar_prefetch=1,
            grid=(steps,),
            in_specs=[
                pl.BlockSpec((tok_rows, token_slots), lambda z, _: (0, 0)),
                pl.BlockSpec((token_slots, width // steps), lambda z, _: (0, z)),
                pl.BlockSpec((PLANE, tok_rows, share * layers), lambda z, _: (0, 0, z)),
            ],
            out_specs=pl.BlockSpec((tok_rows, width // steps), lambda z, _: (0, z)),
        ),
        out_shape=jax.ShapeDtypeStruct((tok_rows, width), jnp.bfloat16),
        compiler_params=pltpu.CompilerParams(vmem_limit_bytes=VMEM),
        cost_estimate=pl.CostEstimate(
            flops=2 * tok_rows * token_slots * width,
            bytes_accessed=2 * width * (token_slots + 2 * tok_rows),
            transcendentals=0,
        ),
    )(at, place, rows, base)


def local(activations, cotangent, family, value_weight, adapter_down, adapter_up):
    count = lax.axis_size("adapter")
    groups = lax.axis_size("groups")
    inner = PLANE // groups
    deep = count // inner
    tok_rows, width = activations.shape
    cap = max(2, (2 * tok_rows + count - 1) // count)
    token_slots = count * cap
    me = lax.axis_index("adapter")
    my_group = lax.axis_index("groups")
    my_inner = lax.rem(me, inner)
    my_layer = me // inner

    def around_groups(block, shift):
        pairs = [(j, (j + shift) % groups) for j in range(groups)]
        return lax.ppermute(block, "groups", pairs)

    def around_plane(block, shift):
        pairs = [
            (line * inner + j, line * inner + (j + shift) % inner)
            for line in range(deep)
            for j in range(inner)
        ]
        return lax.ppermute(block, "adapter", pairs)

    def next_layer(block, step):
        pairs = [(j, j + step) for j in range(count) if 0 <= j + step < count]
        return lax.ppermute(block, "adapter", pairs)

    send, place, back_place = pack(family, cotangent, cap, token_slots)
    received = lax.all_to_all(send, "adapter", split_axis=0, concat_axis=0, tiled=True)

    share = value_weight.shape[0] // groups
    own_share = lax.dynamic_slice_in_dim(value_weight, my_group * share, share, 0)
    layers = [own_share]
    up = down = own_share
    for _ in range(deep - 1):
        up, down = next_layer(up, inner), next_layer(down, -inner)
        layers = [up] + layers + [down]

    send_x = dot(place, activations, ((1,), (0,))).astype(jnp.bfloat16)
    send_x, layers, cotangent = lax.optimization_barrier((send_x, layers, cotangent))
    received_input = lax.all_to_all(send_x, "adapter", split_axis=0, concat_axis=0, tiled=True)

    plane_weight = lax.dynamic_slice_in_dim(
        jnp.concatenate(layers, axis=0), (deep - 1 - my_layer) * share, deep * share, 0
    )
    plane_dy = [cotangent] + [around_groups(cotangent, -shift) for shift in range(1, groups)]
    plane_dy = jnp.stack(plane_dy)
    plane_dy = [plane_dy] + [around_plane(plane_dy, -shift) for shift in range(1, inner)]
    plane_dy = [jnp.concatenate([d[s] for d in plane_dy], axis=0) for s in range(groups)]

    adapter_rows, backward_rows = make_rows(received, adapter_up, adapter_down)
    blocks = [dot(block, plane_weight, ((1,), (1,))).astype(jnp.bfloat16) for block in plane_dy]
    blocks = blocks[:1] + [around_groups(block, s) for s, block in enumerate(blocks) if s]
    adapter_rows, received_input, blocks = lax.optimization_barrier(
        (adapter_rows, received_input, blocks)
    )
    returned_rows = lax.all_to_all(adapter_rows, "adapter", split_axis=0, concat_axis=0, tiled=True)
    base = []
    for shift in range(inner):
        for block in blocks:
            piece = block[shift * tok_rows : (shift + 1) * tok_rows]
            base.append(around_plane(piece, shift) if shift else piece)
    base = jnp.stack(base)
    grad_down, grad_up = make_grads(
        received_input, received, backward_rows, adapter_up, adapter_down
    )
    at = jnp.stack([my_inner, my_group]).astype(jnp.int32)
    input_gradient = finish(at, back_place, returned_rows, base, deep, groups)
    return (input_gradient, grad_down, grad_up)


def solution(mesh):
    in_specs = (
        P(("groups", "adapter"), None),
        P(("groups", "adapter"), None),
        P(("groups", "adapter")),
        P("adapter", None),
        P(None, "adapter"),
        P("adapter", None),
    )
    out_specs = (P(("groups", "adapter"), None), P("groups", "adapter"), P("adapter", "groups"))
    return jax.shard_map(local, mesh=mesh, in_specs=in_specs, out_specs=out_specs, check_vma=False)
```

time: 350 us -> 264 us (0.75)
  waiting for transfers between devices: 251 us -> 151 us
  Pallas kernels: 0 us -> 31.3 us
  matrix products: 38.3 us -> 10.3 us
  starting transfers between devices: 23.2 us -> 48 us
  between operations: 14.2 us -> 0.84 us
    all_to_all x1, waiting for transfers between devices: 152 us -> 13.7 us  [local(): lax.all_to_all(send_x, 'adapter', split_axis=0, concat_axis=0, tiled=True)]
    ppermute x0 -> x17, waiting for transfers between devices: none -> 98 us  [the longest x9 56.8 us: around_plane(): return lax.ppermute(block, 'adapter', pairs)]
    all_to_all x1, waiting for transfers between devices: 76 us -> 39.4 us  [local(): lax.all_to_all(adapter_rows, 'adapter', split_axis=0, concat_axis=0, tile...]
    pallas_call x0 -> x4, Pallas kernels: none -> 31.3 us  [the longest x1 13.2 us: make_grads(): pl.pallas_call(grads_kernel, grid=(width // BLOCK,), in_specs=[pl.BlockSp...]
    ppermute x0 -> x17, starting transfers between devices: none -> 29.7 us  [the longest x6 17.3 us: next_layer(): return lax.ppermute(block, 'adapter', pairs)]
    dot_general x5 -> x3, matrix products: 38.3 us -> 10.3 us  [dot(): lax.dot_general(a, b, (dims, ((), ())), preferred_element_type=jnp.float32)]
    all_to_all x2 -> x1, waiting for transfers between devices: 21.9 us -> 0.01 us  [local(): lax.all_to_all(send, 'adapter', split_axis=0, concat_axis=0, tiled=True)]
    gather x4 -> x0, local copies, waits for them, and re-layouts: 15.6 us -> none  [the longest x1 6.53 us: local(): adapter_part = returned_rows[token_position]]
  transfers between devices with their start and end apart: 5 -> 20, of which waited for: 4 -> 12; matrix products, arithmetic and copies ran while one was open for 14% -> 11% of each run, Pallas kernels for 0% -> 10%
where the time goes in v1:
time: 264 us; the launch traced here: 263 us
  waiting for transfers between devices  151 us (57%)
  starting transfers between devices  48 us (18%)
  Pallas kernels  31.3 us (12%)
  local copies, waits for them, and re-layouts  19.5 us (7%)
  matrix products  10.3 us (4%)
    ppermute x9, waiting for transfers between devices, around_plane(): return lax.ppermute(block, 'adapter', pairs)  56.8 us
    all_to_all x1, waiting for transfers between devices, local(): lax.all_to_all(adapter_rows, 'adapter', split_axis=0, concat_axis=0, tile...  39.4 us
    ppermute x6, waiting for transfers between devices, next_layer(): return lax.ppermute(block, 'adapter', pairs)  26.4 us
    ppermute x6, starting transfers between devices, next_layer(): return lax.ppermute(block, 'adapter', pairs)  17.3 us
    ppermute x2, waiting for transfers between devices, around_groups(): return lax.ppermute(block, 'groups', pairs)  14.9 us
    all_to_all x1, waiting for transfers between devices, local(): lax.all_to_all(send_x, 'adapter', split_axis=0, concat_axis=0, tiled=True)  13.7 us
    pallas_call x1, Pallas kernels, make_grads(): pl.pallas_call(grads_kernel, grid=(width // BLOCK,), in_specs=[pl.BlockSp...  13.2 us
    unnamed x33, local copies, waits for them, and re-layouts  12.8 us
  transfers between devices with their start and end apart: 20, of which 12 were waited for; matrix products, arithmetic and copies ran while one was open for 11% of the time, Pallas kernels for 10%

profile of v1, /device:TPU:15, one launch (start us, length us, event | category | flops | bytes accessed | tf_op | source)
XLA Modules:
  0.0 262.9 jit_solution(5818985220017157364)
XLA Ops:
  1.9 3.2 %collective-permute-start = (bf16[256,1024]{1,0:T(8,128)(2,1)S(1)}, bf16[256,1024]{1,0:T(8,128)(2,1)}, u32[]{:S(2)}, u32[]{:S(2)}) collective-permute-start(bf16[256,1024]{1,0:T(8,128)(2,1)S(1)} %constant_dynamic-slice_fusion), channel_id=1, source_target_pairs={{0,4},{1,5},{2,6},{3,7},{4,8},{5,9},{6,10},{7,11},{8,12},{9,13},{1... | collective-permute-start | bytes 1572872 | tf_op jit(solution)/shard_map/ppermute | solution.py:228
  5.1 2.9 %collective-permute-start.3 = (bf16[256,1024]{1,0:T(8,128)(2,1)S(1)}, bf16[256,1024]{1,0:T(8,128)(2,1)}, u32[]{:S(2)}, u32[]{:S(2)}) collective-permute-start(bf16[256,1024]{1,0:T(8,128)(2,1)S(1)} %constant_dynamic-slice_fusion), channel_id=1, source_target_pairs={{4,0},{5,1},{6,2},{7,3},{8,4},{9,5},{10,6},{11,7},{12,8},{13,9},{1... | collective-permute-start | bytes 1572872 | tf_op jit(solution)/shard_map/ppermute | solution.py:228
  10.2 7.1 %all-to-all-start = ((bf16[16,16,1152]{2,1,0:T(8,128)(2,1)}), bf16[16,16,1152]{2,1,0:T(8,128)(2,1)S(1)}, u32[]{:S(2)}, u32[]{:S(2)}) async-start(bf16[16,16,1152]{2,1,0:T(8,128)(2,1)} %bitcast.48), calls=%async_computation | async-start | bytes 1179648 | tf_op jit(solution)/shard_map/all_to_all | solution.py:231
  17.3 3.1 %collective-permute-start.1 = (bf16[256,1024]{1,0:T(8,128)(2,1)}, bf16[256,1024]{1,0:T(8,128)(2,1)S(1)}, u32[]{:S(2)}, u32[]{:S(2)}) collective-permute-start(bf16[256,1024]{1,0:T(8,128)(2,1)} %collective-permute-done), channel_id=1, source_target_pairs={{0,4},{1,5},{2,6},{3,7},{4,8},{5,9},{6,10},{7,11},{8,12},{9,13},{1... | collective-permute-start | bytes 1572872 | tf_op jit(solution)/shard_map/ppermute | solution.py:228
  22.7 18.9 %collective-permute-done.1 = bf16[256,1024]{1,0:T(8,128)(2,1)S(1)} collective-permute-done((bf16[256,1024]{1,0:T(8,128)(2,1)}, bf16[256,1024]{1,0:T(8,128)(2,1)S(1)}, u32[]{:S(2)}, u32[]{:S(2)}) %collective-permute-start.1) | collective-permute-done | bytes 524320 | tf_op jit(solution)/shard_map/ppermute | solution.py:228
  41.6 4.0 %collective-permute-start.2 = (bf16[256,1024]{1,0:T(8,128)(2,1)S(1)}, bf16[256,1024]{1,0:T(8,128)(2,1)S(1)}, u32[]{:S(2)}, u32[]{:S(2)}) collective-permute-start(bf16[256,1024]{1,0:T(8,128)(2,1)S(1)} %collective-permute-done.1), channel_id=1, source_target_pairs={{0,4},{1,5},{2,6},{3,7},{4,8},{5,9},{6,10},{7,11},{8,12},{9,13},{1... | collective-permute-start | bytes 1572872 | tf_op jit(solution)/shard_map/ppermute | solution.py:228
  47.5 4.1 %convolution_convert_fusion = bf16[256,8192]{1,0:T(8,128)(2,1)} fusion(bf16[256,128]{1,0:T(8,128)(2,1)} %get-tuple-element.26, bf16[128,8192]{1,0:T(8,128)(2,1)S(1)} %copy-done), kind=kOutput, calls=%fused_computation | convolution fusion | flops 538968064 | bytes 6356992 | tf_op jit(solution)/shard_map/dot_general | solution.py:22
  51.7 4.5 %collective-permute-done.2 = bf16[256,1024]{1,0:T(8,128)(2,1)S(1)} collective-permute-done((bf16[256,1024]{1,0:T(8,128)(2,1)S(1)}, bf16[256,1024]{1,0:T(8,128)(2,1)S(1)}, u32[]{:S(2)}, u32[]{:S(2)}) %collective-permute-start.2) | collective-permute-done | bytes 524320 | tf_op jit(solution)/shard_map/ppermute | solution.py:228
  57.0 2.9 %collective-permute-done.5 = bf16[256,1024]{1,0:T(8,128)(2,1)} collective-permute-done((bf16[256,1024]{1,0:T(8,128)(2,1)S(1)}, bf16[256,1024]{1,0:T(8,128)(2,1)}, u32[]{:S(2)}, u32[]{:S(2)}) %collective-permute-start.5) | collective-permute-done | bytes 524320 | tf_op jit(solution)/shard_map/ppermute | solution.py:228
  60.8 6.3 %all-to-all-start.1 = ((bf16[16,16,8192]{2,1,0:T(8,128)(2,1)}), bf16[16,16,8192]{2,1,0:T(8,128)(2,1)}, u32[]{:S(2)}, u32[]{:S(2)}) async-start(bf16[16,16,8192]{2,1,0:T(8,128)(2,1)} %bitcast.41), calls=%async_computation.1 | async-start | bytes 8388608 | tf_op jit(solution)/shard_map/all_to_all | solution.py:243
  69.6 5.2 %collective-permute-done.6 = bf16[128,1024]{1,0:T(8,128)(2,1)S(1)} collective-permute-done((bf16[128,1024]{1,0:T(8,128)(2,1)S(1)}, bf16[128,1024]{1,0:T(8,128)(2,1)S(1)}, u32[]{:S(2)}, u32[]{:S(2)}) %collective-permute-start.6) | collective-permute-done | bytes 262176 | tf_op jit(solution)/shard_map/ppermute | solution.py:216
  82.8 20.2 %collective-permute-done.7 = bf16[2,128,1024]{2,1,0:T(8,128)(2,1)S(1)} collective-permute-done((bf16[2,128,1024]{2,1,0:T(8,128)(2,1)S(1)}, bf16[2,128,1024]{2,1,0:T(8,128)(2,1)S(1)}, u32[]{:S(2)}, u32[]{:S(2)}) %collective-permute-start.7) | collective-permute-done | bytes 524320 | tf_op jit(solution)/shard_map/ppermute | solution.py:224
  103.1 15.9 %collective-permute-done.9 = bf16[2,128,1024]{2,1,0:T(8,128)(2,1)S(1)} collective-permute-done((bf16[2,128,1024]{2,1,0:T(8,128)(2,1)S(1)}, bf16[2,128,1024]{2,1,0:T(8,128)(2,1)S(1)}, u32[]{:S(2)}, u32[]{:S(2)}) %collective-permute-start.9) | collective-permute-done | bytes 524320 | tf_op jit(solution)/shard_map/ppermute | solution.py:224
  122.3 10.1 %shard_map.86 = (bf16[256,8192]{1,0:T(8,128)(2,1)}, bf16[256,512]{1,0:T(8,128)(2,1)}) custom-call(bf16[256,1152]{1,0:T(8,128)(2,1)} %bitcast.42, bf16[256,1152]{1,0:T(8,128)(2,1)} %bitcast.43, bf16[512,1024]{1,0:T(8,128)(2,1)} %up_ref.1, bf16[8192,512]{1,0:T(8,128)(2,1)} %down_ref.3), custom_call_target="tpu_custom_call" | custom-call | flops 2415919104 | bytes 14155776 | tf_op jit(solution)/shard_map/pallas_call | solution.py:82
  132.4 3.9 %fusion.4 = bf16[512,1024]{1,0:T(8,128)(2,1)} fusion(bf16[1792,1024]{1,0:T(8,128)(2,1)} %copy-done.9, s32[]{:T(128)S(6)} %select_n.13, bf16[128,1024]{1,0:T(8,128)(2,1)} %get-tuple-element.54, bf16[128,1024]{1,0:T(8,128)(2,1)S(1)} %get-tuple-element.52, bf16[128,1024]{1,0:T(8,128)(2,1)S(1)} %get-tuple-element.50, bf16[128,1024]{1,0:T(8,128)(2,1)S(1)} %copy-done.2), kind=kOutput, calls=%fused_computation.5 | convolution fusion | flops 1078460416 | bytes 4194308 | tf_op jit(solution)/shard_map/dot_general | solution.py:22
  136.3 9.6 %collective-permute-done.10 = bf16[512,1024]{1,0:T(8,128)(2,1)S(1)} collective-permute-done((bf16[512,1024]{1,0:T(8,128)(2,1)}, bf16[512,1024]{1,0:T(8,128)(2,1)S(1)}, u32[]{:S(2)}, u32[]{:S(2)}) %collective-permute-start.10) | collective-permute-done | bytes 1048608 | tf_op jit(solution)/shard_map/ppermute | solution.py:216
  146.0 13.7 %all-to-all-done.1 = bf16[16,16,8192]{2,1,0:T(8,128)(2,1)} async-done(((bf16[16,16,8192]{2,1,0:T(8,128)(2,1)}), bf16[16,16,8192]{2,1,0:T(8,128)(2,1)}, u32[]{:S(2)}, u32[]{:S(2)}) %all-to-all-start.1) | async-done | bytes 4194336 | tf_op jit(solution)/shard_map/all_to_all | solution.py:243
  159.7 4.9 %all-to-all-start.2 = ((bf16[16,16,8192]{2,1,0:T(8,128)(2,1)}), bf16[16,16,8192]{2,1,0:T(8,128)(2,1)}, u32[]{:S(2)}, u32[]{:S(2)}) async-start(bf16[16,16,8192]{2,1,0:T(8,128)(2,1)} %bitcast.46), calls=%async_computation.2 | async-start | bytes 8388608 | tf_op jit(solution)/shard_map/all_to_all | solution.py:259
  168.7 13.2 %shard_map.88 = (bf16[8192,512]{1,0:T(8,128)(2,1)}, bf16[512,1024]{1,0:T(8,128)(2,1)}) custom-call(bf16[256,8192]{1,0:T(8,128)(2,1)} %bitcast.6.x_ref, bf16[256,1152]{1,0:T(8,128)(2,1)} %bitcast.44, bf16[256,1152]{1,0:T(8,128)(2,1)} %bitcast.45, bf16[256,512]{1,0:T(8,128)(2,1)} %get-tuple-element.40.backward_ref, bf16[8192,512]{1,0:T(8,128)(2,1)} %down_ref.3), custom_call_target="tpu_custom_call" | custom-call | flops 4563402752 | bytes 23592960 | tf_op jit(solution)/shard_map/pallas_call | solution.py:131
  186.8 5.8 %collective-permute-start.16 = (bf16[128,1024]{1,0:T(8,128)(2,1)}, bf16[128,1024]{1,0:T(8,128)(2,1)S(1)}, u32[]{:S(2)}, u32[]{:S(2)}) collective-permute-start(bf16[128,1024]{1,0:T(8,128)(2,1)} %get-tuple-element.43), channel_id=1, source_target_pairs={{0,3},{1,0},{2,1},{3,2},{4,7},{5,4},{6,5},{7,6},{8,11},{9,8},{10,9... | collective-permute-start | bytes 786440 | tf_op jit(solution)/shard_map/ppermute | solution.py:224
  194.0 9.5 %collective-permute-done.13 = bf16[128,1024]{1,0:T(8,128)(2,1)S(1)} collective-permute-done((bf16[128,1024]{1,0:T(8,128)(2,1)}, bf16[128,1024]{1,0:T(8,128)(2,1)S(1)}, u32[]{:S(2)}, u32[]{:S(2)}) %collective-permute-start.13) | collective-permute-done | bytes 262176 | tf_op jit(solution)/shard_map/ppermute | solution.py:224
  204.3 10.5 %collective-permute-done.14 = bf16[128,1024]{1,0:T(8,128)(2,1)S(1)} collective-permute-done((bf16[128,1024]{1,0:T(8,128)(2,1)}, bf16[128,1024]{1,0:T(8,128)(2,1)S(1)}, u32[]{:S(2)}, u32[]{:S(2)}) %collective-permute-start.14) | collective-permute-done | bytes 262176 | tf_op jit(solution)/shard_map/ppermute | solution.py:224
  217.7 39.4 %all-to-all-done.2 = bf16[16,16,8192]{2,1,0:T(8,128)(2,1)} async-done(((bf16[16,16,8192]{2,1,0:T(8,128)(2,1)}), bf16[16,16,8192]{2,1,0:T(8,128)(2,1)}, u32[]{:S(2)}, u32[]{:S(2)}) %all-to-all-start.2) | async-done | bytes 4194336 | tf_op jit(solution)/shard_map/all_to_all | solution.py:259
  257.1 5.8 %shard_map.87 = bf16[128,8192]{1,0:T(8,128)(2,1)} custom-call(s32[2]{0:T(128)} %pad_add_fusion.at_ref, bf16[128,256]{1,0:T(8,128)(2,1)} %get-tuple-element.23.place_ref, bf16[256,8192]{1,0:T(8,128)(2,1)} %bitcast.16.rows_ref, bf16[8,128,1024]{2,1,0:T(8,128)(2,1)} %bitcast_dynamic-update-slice_fusion.base_ref), custom_call_target="tpu_custom_call" | custom-call | flops 536870912 | bytes 8388608 | tf_op jit(solution)/shard_map/pallas_call | solution.py:179
  (66 shorter events, 37.1 us)
Async XLA Ops:
  0.6 46.9 %copy-start = (bf16[128,8192]{1,0:T(8,128)(2,1)S(1)}, bf16[128,8192]{1,0:T(8,128)(2,1)}, u32[]{:S(2)}) copy-start(bf16[128,8192]{1,0:T(8,128)(2,1)} %param.6) | copy-start | bytes 6291460
  1.9 15.4 %collective-permute-start = (bf16[256,1024]{1,0:T(8,128)(2,1)S(1)}, bf16[256,1024]{1,0:T(8,128)(2,1)}, u32[]{:S(2)}, u32[]{:S(2)}) collective-permute-start(bf16[256,1024]{1,0:T(8,128)(2,1)S(1)} %constant_dynamic-slice_fusion), channel_id=1, source_target_pairs={{0,4},{1,5},{2,6},{3,7},{4,8},{5,9},{6,10},{7,11},{8,12},{9,13},{1... | collective-permute-start | bytes 1572872 | tf_op jit(solution)/shard_map/ppermute | solution.py:228
  5.1 15.3 %collective-permute-start.3 = (bf16[256,1024]{1,0:T(8,128)(2,1)S(1)}, bf16[256,1024]{1,0:T(8,128)(2,1)}, u32[]{:S(2)}, u32[]{:S(2)}) collective-permute-start(bf16[256,1024]{1,0:T(8,128)(2,1)S(1)} %constant_dynamic-slice_fusion), channel_id=1, source_target_pairs={{4,0},{5,1},{6,2},{7,3},{8,4},{9,5},{10,6},{11,7},{12,8},{13,9},{1... | collective-permute-start | bytes 1572872 | tf_op jit(solution)/shard_map/ppermute | solution.py:228
  10.2 49.7 %all-to-all-start = ((bf16[16,16,1152]{2,1,0:T(8,128)(2,1)}), bf16[16,16,1152]{2,1,0:T(8,128)(2,1)S(1)}, u32[]{:S(2)}, u32[]{:S(2)}) async-start(bf16[16,16,1152]{2,1,0:T(8,128)(2,1)} %bitcast.48), calls=%async_computation | async-start | bytes 1179648 | tf_op jit(solution)/shard_map/all_to_all | solution.py:231
  17.3 24.3 %collective-permute-start.1 = (bf16[256,1024]{1,0:T(8,128)(2,1)}, bf16[256,1024]{1,0:T(8,128)(2,1)S(1)}, u32[]{:S(2)}, u32[]{:S(2)}) collective-permute-start(bf16[256,1024]{1,0:T(8,128)(2,1)} %collective-permute-done), channel_id=1, source_target_pairs={{0,4},{1,5},{2,6},{3,7},{4,8},{5,9},{6,10},{7,11},{8,12},{9,13},{1... | collective-permute-start | bytes 1572872 | tf_op jit(solution)/shard_map/ppermute | solution.py:228
  20.4 25.2 %collective-permute-start.4 = (bf16[256,1024]{1,0:T(8,128)(2,1)}, bf16[256,1024]{1,0:T(8,128)(2,1)S(1)}, u32[]{:S(2)}, u32[]{:S(2)}) collective-permute-start(bf16[256,1024]{1,0:T(8,128)(2,1)} %collective-permute-done.3), channel_id=1, source_target_pairs={{4,0},{5,1},{6,2},{7,3},{8,4},{9,5},{10,6},{11,7},{12,8},{13,9},{1... | collective-permute-start | bytes 1572872 | tf_op jit(solution)/shard_map/ppermute | solution.py:228
  41.6 10.1 %copy-start.5 = (bf16[256,1024]{1,0:T(8,128)(2,1)}, bf16[256,1024]{1,0:T(8,128)(2,1)S(1)}, u32[]{:S(2)}) copy-start(bf16[256,1024]{1,0:T(8,128)(2,1)S(1)} %collective-permute-done.1) | copy-start | bytes 1572868
  41.6 14.6 %collective-permute-start.2 = (bf16[256,1024]{1,0:T(8,128)(2,1)S(1)}, bf16[256,1024]{1,0:T(8,128)(2,1)S(1)}, u32[]{:S(2)}, u32[]{:S(2)}) collective-permute-start(bf16[256,1024]{1,0:T(8,128)(2,1)S(1)} %collective-permute-done.1), channel_id=1, source_target_pairs={{0,4},{1,5},{2,6},{3,7},{4,8},{5,9},{6,10},{7,11},{8,12},{9,13},{1... | collective-permute-start | bytes 1572872 | tf_op jit(solution)/shard_map/ppermute | solution.py:228
  45.6 14.3 %collective-permute-start.5 = (bf16[256,1024]{1,0:T(8,128)(2,1)S(1)}, bf16[256,1024]{1,0:T(8,128)(2,1)}, u32[]{:S(2)}, u32[]{:S(2)}) collective-permute-start(bf16[256,1024]{1,0:T(8,128)(2,1)S(1)} %collective-permute-done.4), channel_id=1, source_target_pairs={{4,0},{5,1},{6,2},{7,3},{8,4},{9,5},{10,6},{11,7},{12,8},{13,9},{1... | collective-permute-start | bytes 1572872 | tf_op jit(solution)/shard_map/ppermute | solution.py:228
  60.8 98.9 %all-to-all-start.1 = ((bf16[16,16,8192]{2,1,0:T(8,128)(2,1)}), bf16[16,16,8192]{2,1,0:T(8,128)(2,1)}, u32[]{:S(2)}, u32[]{:S(2)}) async-start(bf16[16,16,8192]{2,1,0:T(8,128)(2,1)} %bitcast.41), calls=%async_computation.1 | async-start | bytes 8388608 | tf_op jit(solution)/shard_map/all_to_all | solution.py:243
  67.1 7.7 %collective-permute-start.6 = (bf16[128,1024]{1,0:T(8,128)(2,1)S(1)}, bf16[128,1024]{1,0:T(8,128)(2,1)S(1)}, u32[]{:S(2)}, u32[]{:S(2)}) collective-permute-start(bf16[128,1024]{1,0:T(8,128)(2,1)S(1)} %copy-done.2), channel_id=1, source_target_pairs={{0,16},{16,0},{1,17},{17,1},{2,18},{18,2},{3,19},{19,3},{4,20},{20... | collective-permute-start | bytes 786440 | tf_op jit(solution)/shard_map/ppermute | solution.py:216
  76.6 26.4 %collective-permute-start.7 = (bf16[2,128,1024]{2,1,0:T(8,128)(2,1)S(1)}, bf16[2,128,1024]{2,1,0:T(8,128)(2,1)S(1)}, u32[]{:S(2)}, u32[]{:S(2)}) collective-permute-start(bf16[2,128,1024]{2,1,0:T(8,128)(2,1)S(1)} %pad_maximum_fusion), channel_id=1, source_target_pairs={{0,3},{1,0},{2,1},{3,2},{4,7},{5,4},{6,5},{7,6},{8,11},{9,8},{10,9... | collective-permute-start | bytes 1572872 | tf_op jit(solution)/shard_map/ppermute | solution.py:224
  78.8 24.2 %collective-permute-start.8 = (bf16[2,128,1024]{2,1,0:T(8,128)(2,1)S(1)}, bf16[2,128,1024]{2,1,0:T(8,128)(2,1)S(1)}, u32[]{:S(2)}, u32[]{:S(2)}) collective-permute-start(bf16[2,128,1024]{2,1,0:T(8,128)(2,1)S(1)} %pad_maximum_fusion), channel_id=1, source_target_pairs={{0,2},{1,3},{2,0},{3,1},{4,6},{5,7},{6,4},{7,5},{8,10},{9,11},{10,... | collective-permute-start | bytes 1572872 | tf_op jit(solution)/shard_map/ppermute | solution.py:224
  80.3 39.4 %copy-start.8 = (bf16[128,1024]{1,0:T(8,128)(2,1)S(1)}, bf16[128,1024]{1,0:T(8,128)(2,1)}, u32[]{:S(2)}) copy-start(bf16[128,1024]{1,0:T(8,128)(2,1)} %copy-done.7) | copy-start | bytes 786436
  80.3 38.7 %collective-permute-start.9 = (bf16[2,128,1024]{2,1,0:T(8,128)(2,1)S(1)}, bf16[2,128,1024]{2,1,0:T(8,128)(2,1)S(1)}, u32[]{:S(2)}, u32[]{:S(2)}) collective-permute-start(bf16[2,128,1024]{2,1,0:T(8,128)(2,1)S(1)} %pad_maximum_fusion), channel_id=1, source_target_pairs={{0,1},{1,2},{2,3},{3,0},{4,5},{5,6},{6,7},{7,4},{8,9},{9,10},{10,1... | collective-permute-start | bytes 1572872 | tf_op jit(solution)/shard_map/ppermute | solution.py:224
  82.8 39.2 %copy-start.9 = (bf16[1792,1024]{1,0:T(8,128)(2,1)}, bf16[1792,1024]{1,0:T(8,128)(2,1)S(1)}, u32[]{:S(2)}) copy-start(bf16[1792,1024]{1,0:T(8,128)(2,1)S(1)} %constant_dynamic-update-slice_fusion) | copy-start | bytes 11010052
  122.0 24.0 %collective-permute-start.10 = (bf16[512,1024]{1,0:T(8,128)(2,1)}, bf16[512,1024]{1,0:T(8,128)(2,1)S(1)}, u32[]{:S(2)}, u32[]{:S(2)}) collective-permute-start(bf16[512,1024]{1,0:T(8,128)(2,1)} %fusion.7), channel_id=1, source_target_pairs={{0,16},{16,0},{1,17},{17,1},{2,18},{18,2},{3,19},{19,3},{4,20},{20... | collective-permute-start | bytes 3145736 | tf_op jit(solution)/shard_map/ppermute | solution.py:216
  159.7 97.4 %all-to-all-start.2 = ((bf16[16,16,8192]{2,1,0:T(8,128)(2,1)}), bf16[16,16,8192]{2,1,0:T(8,128)(2,1)}, u32[]{:S(2)}, u32[]{:S(2)}) async-start(bf16[16,16,8192]{2,1,0:T(8,128)(2,1)} %bitcast.46), calls=%async_computation.2 | async-start | bytes 8388608 | tf_op jit(solution)/shard_map/all_to_all | solution.py:259
  167.1 19.7 %collective-permute-start.11 = (bf16[128,1024]{1,0:T(8,128)(2,1)}, bf16[128,1024]{1,0:T(8,128)(2,1)S(1)}, u32[]{:S(2)}, u32[]{:S(2)}) collective-permute-start(bf16[128,1024]{1,0:T(8,128)(2,1)} %get-tuple-element.48), channel_id=1, source_target_pairs={{0,1},{1,2},{2,3},{3,0},{4,5},{5,6},{6,7},{7,4},{8,9},{9,10},{10,1... | collective-permute-start | bytes 786440 | tf_op jit(solution)/shard_map/ppermute | solution.py:224
  168.6 24.8 %collective-permute-start.12 = (bf16[128,1024]{1,0:T(8,128)(2,1)}, bf16[128,1024]{1,0:T(8,128)(2,1)S(1)}, u32[]{:S(2)}, u32[]{:S(2)}) collective-permute-start(bf16[128,1024]{1,0:T(8,128)(2,1)} %get-tuple-element.45), channel_id=1, source_target_pairs={{0,1},{1,2},{2,3},{3,0},{4,5},{5,6},{6,7},{7,4},{8,9},{9,10},{10,1... | collective-permute-start | bytes 786440 | tf_op jit(solution)/shard_map/ppermute | solution.py:224
  184.4 19.2 %collective-permute-start.13 = (bf16[128,1024]{1,0:T(8,128)(2,1)}, bf16[128,1024]{1,0:T(8,128)(2,1)S(1)}, u32[]{:S(2)}, u32[]{:S(2)}) collective-permute-start(bf16[128,1024]{1,0:T(8,128)(2,1)} %get-tuple-element.47), channel_id=1, source_target_pairs={{0,2},{1,3},{2,0},{3,1},{4,6},{5,7},{6,4},{7,5},{8,10},{9,11},{10,... | collective-permute-start | bytes 786440 | tf_op jit(solution)/shard_map/ppermute | solution.py:224
  185.6 29.2 %collective-permute-start.14 = (bf16[128,1024]{1,0:T(8,128)(2,1)}, bf16[128,1024]{1,0:T(8,128)(2,1)S(1)}, u32[]{:S(2)}, u32[]{:S(2)}) collective-permute-start(bf16[128,1024]{1,0:T(8,128)(2,1)} %get-tuple-element.44), channel_id=1, source_target_pairs={{0,2},{1,3},{2,0},{3,1},{4,6},{5,7},{6,4},{7,5},{8,10},{9,11},{10,... | collective-permute-start | bytes 786440 | tf_op jit(solution)/shard_map/ppermute | solution.py:224
  185.9 29.7 %collective-permute-start.15 = (bf16[128,1024]{1,0:T(8,128)(2,1)S(1)}, bf16[128,1024]{1,0:T(8,128)(2,1)S(1)}, u32[]{:S(2)}, u32[]{:S(2)}) collective-permute-start(bf16[128,1024]{1,0:T(8,128)(2,1)S(1)} %get-tuple-element.46), channel_id=1, source_target_pairs={{0,3},{1,0},{2,1},{3,2},{4,7},{5,4},{6,5},{7,6},{8,11},{9,8},{10,9... | collective-permute-start | bytes 786440 | tf_op jit(solution)/shard_map/ppermute | solution.py:224
  186.8 30.2 %collective-permute-start.16 = (bf16[128,1024]{1,0:T(8,128)(2,1)}, bf16[128,1024]{1,0:T(8,128)(2,1)S(1)}, u32[]{:S(2)}, u32[]{:S(2)}) collective-permute-start(bf16[128,1024]{1,0:T(8,128)(2,1)} %get-tuple-element.43), channel_id=1, source_target_pairs={{0,3},{1,0},{2,1},{3,2},{4,7},{5,4},{6,5},{7,6},{8,11},{9,8},{10,9... | collective-permute-start | bytes 786440 | tf_op jit(solution)/shard_map/ppermute | solution.py:224
  (6 other events, 20.3 us)

commit v2 on v1

--- a/solution.py
+++ b/solution.py
@@ -64,15 +64,43 @@
     return column_family == family_ref[:, :1].astype(jnp.int32)
 
 
-def rows_kernel(dy_ref, family_ref, up_ref, down_ref, rows_ref, backward_ref):
-    @pl.when(pl.program_id(0) == 0)
-    def _():
-        back = dot(dy_ref[...], up_ref[...], ((1,), (1,)))
-        keep = own_columns(family_ref, back.shape[1])
-        backward_ref[...] = jnp.where(keep, back, 0.0).astype(jnp.bfloat16)
-
-    rows = dot(backward_ref[...], down_ref[...], ((1,), (1,)))
-    rows_ref[...] = (SCALE * rows).astype(jnp.bfloat16)
+def rows_kernel(
+    received_ref, up_ref, down_ref, rows_ref, backward_ref, dy, families, up, down, rows, sems
+):
+    width, columns = down.shape
+    features = dy.shape[1]
+    steps = width // BLOCK
+    first = [
+        pltpu.make_async_copy(received_ref.at[:, pl.ds(0, features)], dy, sems.at[0]),
+        pltpu.make_async_copy(up_ref, up, sems.at[1]),
+        pltpu.make_async_copy(
+            received_ref.at[:, pl.ds(features, LANES)], families, sems.at[2]
+        ),
+    ]
+    loads, stores = [], []
+    for step in range(steps):
+        part = pl.ds(step * BLOCK, BLOCK)
+        loads.append(pltpu.make_async_copy(down_ref.at[part], down.at[part], sems.at[3 + step]))
+        stores.append(
+            pltpu.make_async_copy(
+                rows.at[:, part], rows_ref.at[:, part], sems.at[3 + steps + step]
+            )
+        )
+    for copy in first + loads:
+        copy.start()
+    for copy in first:
+        copy.wait()
+    back = dot(dy[...], up[...], ((1,), (1,)))
+    back = jnp.where(own_columns(families, columns), back, 0.0).astype(jnp.bfloat16)
+    backward_ref[...] = back
+    for step in range(steps):
+        part = pl.ds(step * BLOCK, BLOCK)
+        loads[step].wait()
+        product = dot(back, down[part], ((1,), (1,)))
+        rows[:, part] = (SCALE * product).astype(jnp.bfloat16)
+        stores[step].start()
+    for copy in stores:
+        copy.wait()
 
 
 def make_rows(received, adapter_up, adapter_down):
@@ -81,20 +109,22 @@
     width = adapter_down.shape[0]
     return pl.pallas_call(
         rows_kernel,
-        grid=(width // BLOCK,),
-        in_specs=[
-            pl.BlockSpec((token_slots, features), lambda j: (0, 0)),
-            pl.BlockSpec((token_slots, LANES), lambda j: (0, features // LANES)),
-            pl.BlockSpec((columns, features), lambda j: (0, 0)),
-            pl.BlockSpec((BLOCK, columns), lambda j: (j, 0)),
-        ],
+        in_specs=[pl.BlockSpec(memory_space=pl.ANY)] * 3,
         out_specs=[
-            pl.BlockSpec((token_slots, BLOCK), lambda j: (0, j)),
-            pl.BlockSpec((token_slots, columns), lambda j: (0, 0)),
+            pl.BlockSpec(memory_space=pl.ANY),
+            pl.BlockSpec(memory_space=pltpu.VMEM),
         ],
         out_shape=[
             jax.ShapeDtypeStruct((token_slots, width), jnp.bfloat16),
             jax.ShapeDtypeStruct((token_slots, columns), jnp.bfloat16),
+        ],
+        scratch_shapes=[
+            pltpu.VMEM((token_slots, features), jnp.bfloat16),
+            pltpu.VMEM((token_slots, LANES), jnp.bfloat16),
+            pltpu.VMEM((columns, features), jnp.bfloat16),
+            pltpu.VMEM((width, columns), jnp.bfloat16),
+            pltpu.VMEM((token_slots, width), jnp.bfloat16),
+            pltpu.SemaphoreType.DMA((3 + 2 * (width // BLOCK),)),
         ],
         compiler_params=pltpu.CompilerParams(vmem_limit_bytes=VMEM),
         cost_estimate=pl.CostEstimate(
@@ -102,7 +132,7 @@
             bytes_accessed=2 * (columns + token_slots) * (width + features),
             transcendentals=0,
         ),
-    )(received, received, adapter_up, adapter_down)
+    )(received, adapter_up, adapter_down)
 
 
 def grads_kernel(x_ref, dy_ref, family_ref, backward_ref, down_ref, grad_down_ref, grad_up_ref, low_ref):
@@ -156,39 +186,72 @@
     )(received_input, received, received, backward_rows, adapter_down)
 
 
-def finish_kernel(share, groups, at_ref, place_ref, rows_ref, base_ref, out_ref):
+def finish_kernel(
+    share, groups, at_ref, place_ref, rows_ref, base_ref, out_ref, rows, base, out, sems
+):
     inner = PLANE // groups
-    for layer in range(base_ref.shape[2] // share):
-        for block in range(PLANE):
-            start = (layer * PLANE + block) * share
-            columns = slice(start, start + share)
-            adapter_part = dot(place_ref[...], rows_ref[:, columns], ((1,), (0,)))
-            inner_shift = lax.rem(at_ref[0] - block // groups + inner, inner)
-            group_shift = lax.rem(at_ref[1] - block % groups + groups, groups)
-            base = base_ref[inner_shift * groups + group_shift]
-            base = base[:, layer * share : (layer + 1) * share].astype(jnp.float32)
-            out_ref[:, columns] = (base + adapter_part).astype(jnp.bfloat16)
+    wide = PLANE * share
+    layers = max(1, LANES // share)
+    steps = base.shape[2] // (layers * share)
+    loads, stores = [], []
+    for step in range(steps):
+        part = pl.ds(step * layers * wide, layers * wide)
+        side = pl.ds(step * layers * share, layers * share)
+        loads.append(
+            (
+                pltpu.make_async_copy(base_ref.at[:, :, side], base.at[:, :, side], sems.at[step]),
+                pltpu.make_async_copy(
+                    rows_ref.at[:, part], rows.at[:, part], sems.at[steps + step]
+                ),
+            )
+        )
+        stores.append(
+            pltpu.make_async_copy(
+                out.at[:, part], out_ref.at[:, part], sems.at[2 * steps + step]
+            )
+        )
+    for pair in loads:
+        for copy in pair:
+            copy.start()
+    for step in range(steps):
+        for copy in loads[step]:
+            copy.wait()
+        for layer in range(step * layers, (step + 1) * layers):
+            for block in range(PLANE):
+                columns = pl.ds((layer * PLANE + block) * share, share)
+                adapter_part = dot(place_ref[...], rows[:, columns], ((1,), (0,)))
+                inner_shift = lax.rem(at_ref[0] - block // groups + inner, inner)
+                group_shift = lax.rem(at_ref[1] - block % groups + groups, groups)
+                frozen_part = base[inner_shift * groups + group_shift]
+                frozen_part = frozen_part[:, layer * share : (layer + 1) * share]
+                total = frozen_part.astype(jnp.float32) + adapter_part
+                out[:, columns] = total.astype(jnp.bfloat16)
+        stores[step].start()
+    for copy in stores:
+        copy.wait()
 
 
 def finish(at, place, rows, base, deep, groups):
     tok_rows, token_slots = place.shape
     width = rows.shape[1]
     share = base.shape[2] // deep
-    layers = max(1, LANES // share)
-    steps = deep // layers
+    steps = deep // max(1, LANES // share)
     return pl.pallas_call(
         functools.partial(finish_kernel, share, groups),
-        grid_spec=pltpu.PrefetchScalarGridSpec(
-            num_scalar_prefetch=1,
-            grid=(steps,),
-            in_specs=[
-                pl.BlockSpec((tok_rows, token_slots), lambda z, _: (0, 0)),
-                pl.BlockSpec((token_slots, width // steps), lambda z, _: (0, z)),
-                pl.BlockSpec((PLANE, tok_rows, share * layers), lambda z, _: (0, 0, z)),
-            ],
-            out_specs=pl.BlockSpec((tok_rows, width // steps), lambda z, _: (0, z)),
-        ),
+        in_specs=[
+            pl.BlockSpec(memory_space=pltpu.SMEM),
+            pl.BlockSpec(memory_space=pltpu.VMEM),
+            pl.BlockSpec(memory_space=pl.ANY),
+            pl.BlockSpec(memory_space=pl.ANY),
+        ],
+        out_specs=pl.BlockSpec(memory_space=pl.ANY),
         out_shape=jax.ShapeDtypeStruct((tok_rows, width), jnp.bfloat16),
+        scratch_shapes=[
+            pltpu.VMEM(rows.shape, jnp.bfloat16),
+            pltpu.VMEM(base.shape, jnp.bfloat16),
+            pltpu.VMEM((tok_rows, width), jnp.bfloat16),
+            pltpu.SemaphoreType.DMA((3 * steps,)),
+        ],
         compiler_params=pltpu.CompilerParams(vmem_limit_bytes=VMEM),
         cost_estimate=pl.CostEstimate(
             flops=2 * tok_rows * token_slots * width,
@@ -211,6 +274,17 @@
     my_inner = lax.rem(me, inner)
     my_layer = me // inner
 
+    def next_layer(block, step):
+        pairs = [(j, j + step) for j in range(count) if 0 <= j + step < count]
+        return lax.ppermute(block, "adapter", pairs)
+
+    def send_layers(block, layers):
+        pairs = [(j * inner + at, k * inner + at) for j, k in layers for at in range(inner)]
+        return lax.ppermute(block, "adapter", pairs)
+
+    def pick(layer, *blocks):
+        return lax.select_n(layer, *blocks)
+
     def around_groups(block, shift):
         pairs = [(j, (j + shift) % groups) for j in range(groups)]
         return lax.ppermute(block, "groups", pairs)
@@ -223,40 +297,61 @@
         ]
         return lax.ppermute(block, "adapter", pairs)
 
-    def next_layer(block, step):
-        pairs = [(j, j + step) for j in range(count) if 0 <= j + step < count]
-        return lax.ppermute(block, "adapter", pairs)
+    share = value_weight.shape[0] // groups
+    own_share = lax.dynamic_slice_in_dim(value_weight, my_group * share, share, 0)
+    family, own_share = lax.optimization_barrier((family, own_share))
+    hops = [next_layer(own_share, inner), next_layer(own_share, -inner)]
+    if deep == 4:
+        hops.append(send_layers(own_share, ((0, 2), (3, 1))))
+    else:
+        for step in range(2, deep):
+            hops += [next_layer(own_share, step * inner), next_layer(own_share, -step * inner)]
 
     send, place, back_place = pack(family, cotangent, cap, token_slots)
     received = lax.all_to_all(send, "adapter", split_axis=0, concat_axis=0, tiled=True)
-
-    share = value_weight.shape[0] // groups
-    own_share = lax.dynamic_slice_in_dim(value_weight, my_group * share, share, 0)
-    layers = [own_share]
-    up = down = own_share
-    for _ in range(deep - 1):
-        up, down = next_layer(up, inner), next_layer(down, -inner)
-        layers = [up] + layers + [down]
-
     send_x = dot(place, activations, ((1,), (0,))).astype(jnp.bfloat16)
-    send_x, layers, cotangent = lax.optimization_barrier((send_x, layers, cotangent))
+    send_x, hops, cotangent = lax.optimization_barrier((send_x, hops, cotangent))
     received_input = lax.all_to_all(send_x, "adapter", split_axis=0, concat_axis=0, tiled=True)
 
-    plane_weight = lax.dynamic_slice_in_dim(
-        jnp.concatenate(layers, axis=0), (deep - 1 - my_layer) * share, deep * share, 0
-    )
     plane_dy = [cotangent] + [around_groups(cotangent, -shift) for shift in range(1, groups)]
     plane_dy = jnp.stack(plane_dy)
     plane_dy = [plane_dy] + [around_plane(plane_dy, -shift) for shift in range(1, inner)]
+    adapter_rows, backward_rows = make_rows(received, adapter_up, adapter_down)
+
+    below, above = hops[:2]
+    if deep == 4:
+        lower = my_layer < 2
+        over = hops[2]
+        pair = jnp.concatenate([jnp.where(lower, above, over), jnp.where(lower, over, below)], axis=0)
+        hops.append(send_layers(pair, ((1, 0), (2, 3))))
+    received_input, adapter_rows, plane_dy, hops = lax.optimization_barrier(
+        (received_input, adapter_rows, plane_dy, hops)
+    )
+    returned_rows = lax.all_to_all(adapter_rows, "adapter", split_axis=0, concat_axis=0, tiled=True)
+    if deep == 4:
+        below, above, over, pair = hops
+        first, second = pair[:share], pair[share:]
+        plane_weight = jnp.concatenate(
+            [
+                pick(my_layer, own_share, below, over, first),
+                pick(my_layer, above, own_share, below, second),
+                pick(my_layer, first, above, own_share, below),
+                pick(my_layer, second, over, above, own_share),
+            ],
+            axis=0,
+        )
+    else:
+        plane_weight = lax.dynamic_slice_in_dim(
+            jnp.concatenate(hops[0::2][::-1] + [own_share] + hops[1::2], axis=0),
+            (deep - 1 - my_layer) * share,
+            deep * share,
+            0,
+        )
     plane_dy = [jnp.concatenate([d[s] for d in plane_dy], axis=0) for s in range(groups)]
 
-    adapter_rows, backward_rows = make_rows(received, adapter_up, adapter_down)
     blocks = [dot(block, plane_weight, ((1,), (1,))).astype(jnp.bfloat16) for block in plane_dy]
     blocks = blocks[:1] + [around_groups(block, s) for s, block in enumerate(blocks) if s]
-    adapter_rows, received_input, blocks = lax.optimization_barrier(
-        (adapter_rows, received_input, blocks)
-    )
-    returned_rows = lax.all_to_all(adapter_rows, "adapter", split_axis=0, concat_axis=0, tiled=True)
+    received_input, blocks = lax.optimization_barrier((received_input, blocks))
     base = []
     for shift in range(inner):
         for block in blocks:

time: 264 us -> 251 us (0.951)
  starting transfers between devices: 48 us -> 35.1 us
  waiting for transfers between devices: 151 us -> 162 us
  local copies, waits for them, and re-layouts: 19.5 us -> 13.7 us
  matrix products: 10.3 us -> 6.66 us
  Pallas kernels: 31.3 us -> 28 us
  other arithmetic: 1.65 us -> 4.68 us
    ppermute x0 -> x2, waiting for transfers between devices: none -> 38.6 us  [send_layers(): return lax.ppermute(block, 'adapter', pairs)]
    all_to_all x1, waiting for transfers between devices: 39.4 us -> 12.5 us  [local(): lax.all_to_all(adapter_rows, 'adapter', split_axis=0, concat_axis=0, tile...]
    ppermute x2, waiting for transfers between devices: 14.9 us -> 29.2 us  [around_groups(): return lax.ppermute(block, 'groups', pairs)]
    ppermute x6 -> x2, starting transfers between devices: 17.3 us -> 5.3 us  [next_layer(): return lax.ppermute(block, 'adapter', pairs)]
    all_to_all x1, waiting for transfers between devices: 13.7 us -> 2.15 us  [local(): lax.all_to_all(send_x, 'adapter', split_axis=0, concat_axis=0, tiled=True)]
    unnamed x33 -> x27, local copies, waits for them, and re-layouts: 12.8 us -> 7.67 us
    ppermute x0 -> x2, starting transfers between devices: none -> 4.44 us  [send_layers(): return lax.ppermute(block, 'adapter', pairs)]
    ppermute x9, waiting for transfers between devices: 56.8 us -> 52.4 us  [around_plane(): return lax.ppermute(block, 'adapter', pairs)]
  transfers between devices with their start and end apart: 20 -> 18, of which waited for: 12 -> 13; matrix products, arithmetic and copies ran while one was open for 11% -> 9% of each run, Pallas kernels for 10% -> 8%
where the time goes in v2:
time: 251 us
  waiting for transfers between devices  162 us (65%)
  starting transfers between devices  35.1 us (14%)
  Pallas kernels  28 us (11%)
  local copies, waits for them, and re-layouts  13.7 us (5%)
  matrix products  6.66 us (3%)
  other arithmetic  4.68 us (2%)
    ppermute x9, waiting for transfers between devices, around_plane(): return lax.ppermute(block, 'adapter', pairs)  52.4 us
    ppermute x2, waiting for transfers between devices, send_layers(): return lax.ppermute(block, 'adapter', pairs)  38.6 us
    ppermute x2, waiting for transfers between devices, around_groups(): return lax.ppermute(block, 'groups', pairs)  29.2 us
    ppermute x2, waiting for transfers between devices, next_layer(): return lax.ppermute(block, 'adapter', pairs)  26.6 us
    pallas_call x1, Pallas kernels, make_grads(): pl.pallas_call(grads_kernel, grid=(width // BLOCK,), in_specs=[pl.BlockSp...  13.2 us
    all_to_all x1, waiting for transfers between devices, local(): lax.all_to_all(adapter_rows, 'adapter', split_axis=0, concat_axis=0, tile...  12.5 us
    unnamed x27, local copies, waits for them, and re-layouts  7.67 us
    ppermute x9, starting transfers between devices, around_plane(): return lax.ppermute(block, 'adapter', pairs)  7.57 us
  transfers between devices with their start and end apart: 18, of which 13 were waited for; matrix products, arithmetic and copies ran while one was open for 9% of the time, Pallas kernels for 8%

profile of v2, /device:TPU:15, one launch (start us, length us, event | category | flops | bytes accessed | tf_op | source)
XLA Modules:
  0.0 250.6 jit_solution(10363864733708801768)
XLA Ops:
  1.9 2.2 shard_map.85
  4.1 6.6 %all-to-all-start.1 = ((bf16[16,16,1152]{2,1,0:T(8,128)(2,1)}), bf16[16,16,1152]{2,1,0:T(8,128)(2,1)S(1)}, u32[]{:S(2)}, u32[]{:S(2)}) async-start(bf16[16,16,1152]{2,1,0:T(8,128)(2,1)} %bitcast.51), calls=%async_computation.1 | async-start | bytes 1179648 | tf_op jit(solution)/shard_map/all_to_all | solution.py:311
  10.7 3.1 %collective-permute-start = (bf16[256,1024]{1,0:T(8,128)(2,1)S(1)}, bf16[256,1024]{1,0:T(8,128)(2,1)S(1)}, u32[]{:S(2)}, u32[]{:S(2)}) collective-permute-start(bf16[256,1024]{1,0:T(8,128)(2,1)S(1)} %constant_dynamic-slice_fusion), channel_id=1, source_target_pairs={{0,4},{1,5},{2,6},{3,7},{4,8},{5,9},{6,10},{7,11},{8,12},{9,13},{1... | collective-permute-start | bytes 1572872 | tf_op jit(solution)/shard_map/ppermute | solution.py:279
  13.7 2.2 collective-permute-start.1
  17.3 4.1 %convolution_convert_fusion = bf16[256,8192]{1,0:T(8,128)(2,1)} fusion(bf16[256,128]{1,0:T(8,128)(2,1)} %get-tuple-element.32, bf16[128,8192]{1,0:T(8,128)(2,1)S(1)} %copy-done), kind=kOutput, calls=%fused_computation | convolution fusion | flops 538968064 | bytes 6356992 | tf_op jit(solution)/shard_map/dot_general | solution.py:22
  21.4 24.7 %collective-permute-done = bf16[256,1024]{1,0:T(8,128)(2,1)S(1)} collective-permute-done((bf16[256,1024]{1,0:T(8,128)(2,1)S(1)}, bf16[256,1024]{1,0:T(8,128)(2,1)S(1)}, u32[]{:S(2)}, u32[]{:S(2)}) %collective-permute-start) | collective-permute-done | bytes 524320 | tf_op jit(solution)/shard_map/ppermute | solution.py:279
  46.1 2.0 collective-permute-done.1
  49.7 5.4 %all-to-all-start = ((bf16[16,16,8192]{2,1,0:T(8,128)(2,1)}), bf16[16,16,8192]{2,1,0:T(8,128)(2,1)}, u32[]{:S(2)}, u32[]{:S(2)}) async-start(bf16[16,16,8192]{2,1,0:T(8,128)(2,1)} %bitcast.45), calls=%async_computation | async-start | bytes 8388608 | tf_op jit(solution)/shard_map/all_to_all | solution.py:314
  57.5 3.1 %collective-permute-start.7 = (bf16[512,1024]{1,0:T(8,128)(2,1)}, bf16[512,1024]{1,0:T(8,128)(2,1)}, u32[]{:S(2)}, u32[]{:S(2)}) collective-permute-start(bf16[512,1024]{1,0:T(8,128)(2,1)} %pad_maximum_fusion.1), channel_id=1, source_target_pairs={{4,0},{5,1},{6,2},{7,3},{8,12},{9,13},{10,14},{11,15},{20,16},{21,... | collective-permute-start | bytes 3145736 | tf_op jit(solution)/shard_map/ppermute | solution.py:283
  60.9 7.1 %collective-permute-done.3 = bf16[128,1024]{1,0:T(8,128)(2,1)S(1)} collective-permute-done((bf16[128,1024]{1,0:T(8,128)(2,1)S(1)}, bf16[128,1024]{1,0:T(8,128)(2,1)S(1)}, u32[]{:S(2)}, u32[]{:S(2)}) %collective-permute-start.3) | collective-permute-done | bytes 262176 | tf_op jit(solution)/shard_map/ppermute | solution.py:290
  71.2 7.4 %shard_map.86 = (bf16[256,8192]{1,0:T(8,128)(2,1)}, bf16[256,512]{1,0:T(8,128)(2,1)}) custom-call(bf16[256,1152]{1,0:T(8,128)(2,1)} %bitcast.47, bf16[512,1024]{1,0:T(8,128)(2,1)} %up_ref.1, bf16[8192,512]{1,0:T(8,128)(2,1)} %down_ref.3), custom_call_target="tpu_custom_call" | custom-call | flops 2415919104 | bytes 14155776 | tf_op jit(solution)/shard_map/pallas_call | solution.py:110
  78.6 12.5 %collective-permute-done.4 = bf16[2,128,1024]{2,1,0:T(8,128)(2,1)} collective-permute-done((bf16[2,128,1024]{2,1,0:T(8,128)(2,1)S(1)}, bf16[2,128,1024]{2,1,0:T(8,128)(2,1)}, u32[]{:S(2)}, u32[]{:S(2)}) %collective-permute-start.4) | collective-permute-done | bytes 524320 | tf_op jit(solution)/shard_map/ppermute | solution.py:298
  91.1 15.8 %collective-permute-done.6 = bf16[2,128,1024]{2,1,0:T(8,128)(2,1)} collective-permute-done((bf16[2,128,1024]{2,1,0:T(8,128)(2,1)S(1)}, bf16[2,128,1024]{2,1,0:T(8,128)(2,1)}, u32[]{:S(2)}, u32[]{:S(2)}) %collective-permute-start.6) | collective-permute-done | bytes 524320 | tf_op jit(solution)/shard_map/ppermute | solution.py:298
  107.0 38.6 %collective-permute-done.7 = bf16[512,1024]{1,0:T(8,128)(2,1)} collective-permute-done((bf16[512,1024]{1,0:T(8,128)(2,1)}, bf16[512,1024]{1,0:T(8,128)(2,1)}, u32[]{:S(2)}, u32[]{:S(2)}) %collective-permute-start.7) | collective-permute-done | bytes 1048608 | tf_op jit(solution)/shard_map/ppermute | solution.py:283
  145.5 2.2 all-to-all-done
  147.7 5.3 %all-to-all-start.2 = ((bf16[16,16,8192]{2,1,0:T(8,128)(2,1)}), bf16[16,16,8192]{2,1,0:T(8,128)(2,1)}, u32[]{:S(2)}, u32[]{:S(2)}) async-start(bf16[16,16,8192]{2,1,0:T(8,128)(2,1)} %bitcast.46), calls=%async_computation.2 | async-start | bytes 8388608 | tf_op jit(solution)/shard_map/all_to_all | solution.py:330
  160.5 22.2 %collective-permute-done.8 = bf16[512,1024]{1,0:T(8,128)(2,1)S(1)} collective-permute-done((bf16[512,1024]{1,0:T(8,128)(2,1)S(1)}, bf16[512,1024]{1,0:T(8,128)(2,1)S(1)}, u32[]{:S(2)}, u32[]{:S(2)}) %collective-permute-start.8) | collective-permute-done | bytes 1048608 | tf_op jit(solution)/shard_map/ppermute | solution.py:290
  185.8 13.2 %shard_map.88 = (bf16[8192,512]{1,0:T(8,128)(2,1)}, bf16[512,1024]{1,0:T(8,128)(2,1)}) custom-call(bf16[256,8192]{1,0:T(8,128)(2,1)} %bitcast.4.x_ref, bf16[256,1152]{1,0:T(8,128)(2,1)} %bitcast.48, bf16[256,1152]{1,0:T(8,128)(2,1)} %bitcast.49, bf16[256,512]{1,0:T(8,128)(2,1)} %get-tuple-element.54.backward_ref, bf16[8192,512]{1,0:T(8,128)(2,1)} %down_ref.3), custom_call_target="tpu_custom_call" | custom-call | flops 4563402752 | bytes 23592960 | tf_op jit(solution)/shard_map/pallas_call | solution.py:161
  206.0 8.8 %collective-permute-done.11 = bf16[128,1024]{1,0:T(8,128)(2,1)S(1)} collective-permute-done((bf16[128,1024]{1,0:T(8,128)(2,1)}, bf16[128,1024]{1,0:T(8,128)(2,1)S(1)}, u32[]{:S(2)}, u32[]{:S(2)}) %collective-permute-start.11) | collective-permute-done | bytes 262176 | tf_op jit(solution)/shard_map/ppermute | solution.py:298
  215.5 10.4 %collective-permute-done.12 = bf16[128,1024]{1,0:T(8,128)(2,1)S(1)} collective-permute-done((bf16[128,1024]{1,0:T(8,128)(2,1)}, bf16[128,1024]{1,0:T(8,128)(2,1)S(1)}, u32[]{:S(2)}, u32[]{:S(2)}) %collective-permute-start.12) | collective-permute-done | bytes 262176 | tf_op jit(solution)/shard_map/ppermute | solution.py:298
  226.7 2.7 %collective-permute-done.13 = bf16[128,1024]{1,0:T(8,128)(2,1)S(1)} collective-permute-done((bf16[128,1024]{1,0:T(8,128)(2,1)S(1)}, bf16[128,1024]{1,0:T(8,128)(2,1)S(1)}, u32[]{:S(2)}, u32[]{:S(2)}) %collective-permute-start.13) | collective-permute-done | bytes 262176 | tf_op jit(solution)/shard_map/ppermute | solution.py:298
  230.1 2.1 collective-permute-done.14
  232.9 12.5 %all-to-all-done.2 = bf16[16,16,8192]{2,1,0:T(8,128)(2,1)} async-done(((bf16[16,16,8192]{2,1,0:T(8,128)(2,1)}), bf16[16,16,8192]{2,1,0:T(8,128)(2,1)}, u32[]{:S(2)}, u32[]{:S(2)}) %all-to-all-start.2) | async-done | bytes 4194336 | tf_op jit(solution)/shard_map/all_to_all | solution.py:330
  245.5 5.1 %shard_map.87 = bf16[128,8192]{1,0:T(8,128)(2,1)} custom-call(s32[2]{0:T(128)} %pad_add_fusion.at_ref, bf16[128,256]{1,0:T(8,128)(2,1)} %get-tuple-element.31.place_ref, bf16[256,8192]{1,0:T(8,128)(2,1)} %bitcast.10.rows_ref, bf16[8,128,1024]{2,1,0:T(8,128)(2,1)} %bitcast_dynamic-update-slice_fusion.base_ref), custom_call_target="tpu_custom_call" | custom-call | flops 536870912 | bytes 8388608 | tf_op jit(solution)/shard_map/pallas_call | solution.py:239
  (57 shorter events, 30.4 us)
Async XLA Ops:
  0.6 16.6 %copy-start = (bf16[128,8192]{1,0:T(8,128)(2,1)S(1)}, bf16[128,8192]{1,0:T(8,128)(2,1)}, u32[]{:S(2)}) copy-start(bf16[128,8192]{1,0:T(8,128)(2,1)} %param.6) | copy-start | bytes 6291460
  4.1 44.7 %all-to-all-start.1 = ((bf16[16,16,1152]{2,1,0:T(8,128)(2,1)}), bf16[16,16,1152]{2,1,0:T(8,128)(2,1)S(1)}, u32[]{:S(2)}, u32[]{:S(2)}) async-start(bf16[16,16,1152]{2,1,0:T(8,128)(2,1)} %bitcast.51), calls=%async_computation.1 | async-start | bytes 1179648 | tf_op jit(solution)/shard_map/all_to_all | solution.py:311
  10.7 35.4 %collective-permute-start = (bf16[256,1024]{1,0:T(8,128)(2,1)S(1)}, bf16[256,1024]{1,0:T(8,128)(2,1)S(1)}, u32[]{:S(2)}, u32[]{:S(2)}) collective-permute-start(bf16[256,1024]{1,0:T(8,128)(2,1)S(1)} %constant_dynamic-slice_fusion), channel_id=1, source_target_pairs={{0,4},{1,5},{2,6},{3,7},{4,8},{5,9},{6,10},{7,11},{8,12},{9,13},{1... | collective-permute-start | bytes 1572872 | tf_op jit(solution)/shard_map/ppermute | solution.py:279
  13.7 34.3 %collective-permute-start.1 = (bf16[256,1024]{1,0:T(8,128)(2,1)S(1)}, bf16[256,1024]{1,0:T(8,128)(2,1)S(1)}, u32[]{:S(2)}, u32[]{:S(2)}) collective-permute-start(bf16[256,1024]{1,0:T(8,128)(2,1)S(1)} %constant_dynamic-slice_fusion), channel_id=1, source_target_pairs={{4,0},{5,1},{6,2},{7,3},{8,4},{9,5},{10,6},{11,7},{12,8},{13,9},{1... | collective-permute-start | bytes 1572872 | tf_op jit(solution)/shard_map/ppermute | solution.py:279
  16.0 32.9 %collective-permute-start.2 = (bf16[256,1024]{1,0:T(8,128)(2,1)S(1)}, bf16[256,1024]{1,0:T(8,128)(2,1)}, u32[]{:S(2)}, u32[]{:S(2)}) collective-permute-start(bf16[256,1024]{1,0:T(8,128)(2,1)S(1)} %constant_dynamic-slice_fusion), channel_id=1, source_target_pairs={{0,8},{1,9},{2,10},{3,11},{12,4},{13,5},{14,6},{15,7},{16,24},{17,... | collective-permute-start | bytes 1572872 | tf_op jit(solution)/shard_map/ppermute | solution.py:283
  49.7 98.0 %all-to-all-start = ((bf16[16,16,8192]{2,1,0:T(8,128)(2,1)}), bf16[16,16,8192]{2,1,0:T(8,128)(2,1)}, u32[]{:S(2)}, u32[]{:S(2)}) async-start(bf16[16,16,8192]{2,1,0:T(8,128)(2,1)} %bitcast.45), calls=%async_computation | async-start | bytes 8388608 | tf_op jit(solution)/shard_map/all_to_all | solution.py:314
  55.1 5.5 %copy-start.7 = (bf16[128,1024]{1,0:T(8,128)(2,1)S(1)}, bf16[128,1024]{1,0:T(8,128)(2,1)}, u32[]{:S(2)}) copy-start(bf16[128,1024]{1,0:T(8,128)(2,1)} %dy_ref.1) | copy-start | bytes 786436
  57.5 88.1 %collective-permute-start.7 = (bf16[512,1024]{1,0:T(8,128)(2,1)}, bf16[512,1024]{1,0:T(8,128)(2,1)}, u32[]{:S(2)}, u32[]{:S(2)}) collective-permute-start(bf16[512,1024]{1,0:T(8,128)(2,1)} %pad_maximum_fusion.1), channel_id=1, source_target_pairs={{4,0},{5,1},{6,2},{7,3},{8,12},{9,13},{10,14},{11,15},{20,16},{21,... | collective-permute-start | bytes 3145736 | tf_op jit(solution)/shard_map/ppermute | solution.py:283
  60.6 7.3 %collective-permute-start.3 = (bf16[128,1024]{1,0:T(8,128)(2,1)S(1)}, bf16[128,1024]{1,0:T(8,128)(2,1)S(1)}, u32[]{:S(2)}, u32[]{:S(2)}) collective-permute-start(bf16[128,1024]{1,0:T(8,128)(2,1)S(1)} %copy-done.7), channel_id=1, source_target_pairs={{0,16},{16,0},{1,17},{17,1},{2,18},{18,2},{3,19},{19,3},{4,20},{20... | collective-permute-start | bytes 786440 | tf_op jit(solution)/shard_map/ppermute | solution.py:290
  68.0 23.1 %collective-permute-start.4 = (bf16[2,128,1024]{2,1,0:T(8,128)(2,1)S(1)}, bf16[2,128,1024]{2,1,0:T(8,128)(2,1)}, u32[]{:S(2)}, u32[]{:S(2)}) collective-permute-start(bf16[2,128,1024]{2,1,0:T(8,128)(2,1)S(1)} %pad_maximum_fusion.2), channel_id=1, source_target_pairs={{0,3},{1,0},{2,1},{3,2},{4,7},{5,4},{6,5},{7,6},{8,11},{9,8},{10,9... | collective-permute-start | bytes 1572872 | tf_op jit(solution)/shard_map/ppermute | solution.py:298
  69.5 21.7 %collective-permute-start.5 = (bf16[2,128,1024]{2,1,0:T(8,128)(2,1)S(1)}, bf16[2,128,1024]{2,1,0:T(8,128)(2,1)S(1)}, u32[]{:S(2)}, u32[]{:S(2)}) collective-permute-start(bf16[2,128,1024]{2,1,0:T(8,128)(2,1)S(1)} %pad_maximum_fusion.2), channel_id=1, source_target_pairs={{0,2},{1,3},{2,0},{3,1},{4,6},{5,7},{6,4},{7,5},{8,10},{9,11},{10,... | collective-permute-start | bytes 1572872 | tf_op jit(solution)/shard_map/ppermute | solution.py:298
  69.5 37.4 %collective-permute-start.6 = (bf16[2,128,1024]{2,1,0:T(8,128)(2,1)S(1)}, bf16[2,128,1024]{2,1,0:T(8,128)(2,1)}, u32[]{:S(2)}, u32[]{:S(2)}) collective-permute-start(bf16[2,128,1024]{2,1,0:T(8,128)(2,1)S(1)} %pad_maximum_fusion.2), channel_id=1, source_target_pairs={{0,1},{1,2},{2,3},{3,0},{4,5},{5,6},{6,7},{7,4},{8,9},{9,10},{10,1... | collective-permute-start | bytes 1572872 | tf_op jit(solution)/shard_map/ppermute | solution.py:298
  91.1 15.8 %copy-start.8 = (bf16[2,128,1024]{2,1,0:T(8,128)(2,1)}, bf16[2,128,1024]{2,1,0:T(8,128)(2,1)S(1)}, u32[]{:S(2)}) copy-start(bf16[2,128,1024]{2,1,0:T(8,128)(2,1)S(1)} %collective-permute-done.5) | copy-start | bytes 1572868
  147.7 97.8 %all-to-all-start.2 = ((bf16[16,16,8192]{2,1,0:T(8,128)(2,1)}), bf16[16,16,8192]{2,1,0:T(8,128)(2,1)}, u32[]{:S(2)}, u32[]{:S(2)}) async-start(bf16[16,16,8192]{2,1,0:T(8,128)(2,1)} %bitcast.46), calls=%async_computation.2 | async-start | bytes 8388608 | tf_op jit(solution)/shard_map/all_to_all | solution.py:330
  153.0 2.4 copy-start.3
  153.0 2.4 copy-start.5
  158.3 24.4 %collective-permute-start.8 = (bf16[512,1024]{1,0:T(8,128)(2,1)S(1)}, bf16[512,1024]{1,0:T(8,128)(2,1)S(1)}, u32[]{:S(2)}, u32[]{:S(2)}) collective-permute-start(bf16[512,1024]{1,0:T(8,128)(2,1)S(1)} %convolution_convert_fusion.1), channel_id=1, source_target_pairs={{0,16},{16,0},{1,17},{17,1},{2,18},{18,2},{3,19},{19,3},{4,20},{20... | collective-permute-start | bytes 3145736 | tf_op jit(solution)/shard_map/ppermute | solution.py:290
  160.5 22.2 %copy-start.6 = (bf16[512,1024]{1,0:T(8,128)(2,1)}, bf16[512,1024]{1,0:T(8,128)(2,1)S(1)}, u32[]{:S(2)}) copy-start(bf16[512,1024]{1,0:T(8,128)(2,1)S(1)} %convolution_convert_fusion.2) | copy-start | bytes 3145732
  183.6 20.5 %collective-permute-start.9 = (bf16[128,1024]{1,0:T(8,128)(2,1)}, bf16[128,1024]{1,0:T(8,128)(2,1)S(1)}, u32[]{:S(2)}, u32[]{:S(2)}) collective-permute-start(bf16[128,1024]{1,0:T(8,128)(2,1)} %get-tuple-element.66), channel_id=1, source_target_pairs={{0,1},{1,2},{2,3},{3,0},{4,5},{5,6},{6,7},{7,4},{8,9},{9,10},{10,1... | collective-permute-start | bytes 786440 | tf_op jit(solution)/shard_map/ppermute | solution.py:298
  185.8 19.4 %collective-permute-start.10 = (bf16[128,1024]{1,0:T(8,128)(2,1)}, bf16[128,1024]{1,0:T(8,128)(2,1)S(1)}, u32[]{:S(2)}, u32[]{:S(2)}) collective-permute-start(bf16[128,1024]{1,0:T(8,128)(2,1)} %get-tuple-element.63), channel_id=1, source_target_pairs={{0,1},{1,2},{2,3},{3,0},{4,5},{5,6},{6,7},{7,4},{8,9},{9,10},{10,1... | collective-permute-start | bytes 786440 | tf_op jit(solution)/shard_map/ppermute | solution.py:298
  201.5 13.3 %collective-permute-start.11 = (bf16[128,1024]{1,0:T(8,128)(2,1)}, bf16[128,1024]{1,0:T(8,128)(2,1)S(1)}, u32[]{:S(2)}, u32[]{:S(2)}) collective-permute-start(bf16[128,1024]{1,0:T(8,128)(2,1)} %get-tuple-element.65), channel_id=1, source_target_pairs={{0,2},{1,3},{2,0},{3,1},{4,6},{5,7},{6,4},{7,5},{8,10},{9,11},{10,... | collective-permute-start | bytes 786440 | tf_op jit(solution)/shard_map/ppermute | solution.py:298
  202.7 23.3 %collective-permute-start.12 = (bf16[128,1024]{1,0:T(8,128)(2,1)}, bf16[128,1024]{1,0:T(8,128)(2,1)S(1)}, u32[]{:S(2)}, u32[]{:S(2)}) collective-permute-start(bf16[128,1024]{1,0:T(8,128)(2,1)} %get-tuple-element.62), channel_id=1, source_target_pairs={{0,2},{1,3},{2,0},{3,1},{4,6},{5,7},{6,4},{7,5},{8,10},{9,11},{10,... | collective-permute-start | bytes 786440 | tf_op jit(solution)/shard_map/ppermute | solution.py:298
  203.0 26.4 %collective-permute-start.13 = (bf16[128,1024]{1,0:T(8,128)(2,1)S(1)}, bf16[128,1024]{1,0:T(8,128)(2,1)S(1)}, u32[]{:S(2)}, u32[]{:S(2)}) collective-permute-start(bf16[128,1024]{1,0:T(8,128)(2,1)S(1)} %get-tuple-element.64), channel_id=1, source_target_pairs={{0,3},{1,0},{2,1},{3,2},{4,7},{5,4},{6,5},{7,6},{8,11},{9,8},{10,9... | collective-permute-start | bytes 786440 | tf_op jit(solution)/shard_map/ppermute | solution.py:298
  204.0 28.2 %collective-permute-start.14 = (bf16[128,1024]{1,0:T(8,128)(2,1)}, bf16[128,1024]{1,0:T(8,128)(2,1)S(1)}, u32[]{:S(2)}, u32[]{:S(2)}) collective-permute-start(bf16[128,1024]{1,0:T(8,128)(2,1)} %get-tuple-element.61), channel_id=1, source_target_pairs={{0,3},{1,0},{2,1},{3,2},{4,7},{5,4},{6,5},{7,6},{8,11},{9,8},{10,9... | collective-permute-start | bytes 786440 | tf_op jit(solution)/shard_map/ppermute | solution.py:298
  (4 other events, 4.9 us)

commit v3 on v2

--- a/solution.py
+++ b/solution.py
@@ -309,21 +309,23 @@
 
     send, place, back_place = pack(family, cotangent, cap, token_slots)
     received = lax.all_to_all(send, "adapter", split_axis=0, concat_axis=0, tiled=True)
-    send_x = dot(place, activations, ((1,), (0,))).astype(jnp.bfloat16)
-    send_x, hops, cotangent = lax.optimization_barrier((send_x, hops, cotangent))
-    received_input = lax.all_to_all(send_x, "adapter", split_axis=0, concat_axis=0, tiled=True)
-
-    plane_dy = [cotangent] + [around_groups(cotangent, -shift) for shift in range(1, groups)]
-    plane_dy = jnp.stack(plane_dy)
-    plane_dy = [plane_dy] + [around_plane(plane_dy, -shift) for shift in range(1, inner)]
-    adapter_rows, backward_rows = make_rows(received, adapter_up, adapter_down)
-
     below, above = hops[:2]
     if deep == 4:
         lower = my_layer < 2
         over = hops[2]
         pair = jnp.concatenate([jnp.where(lower, above, over), jnp.where(lower, over, below)], axis=0)
-        hops.append(send_layers(pair, ((1, 0), (2, 3))))
+        hops.append(pair)
+    place, hops, cotangent = lax.optimization_barrier((place, hops, cotangent))
+    send_x = dot(place, activations, ((1,), (0,))).astype(jnp.bfloat16)
+    received_input = lax.all_to_all(send_x, "adapter", split_axis=0, concat_axis=0, tiled=True)
+
+    plane_dy = [cotangent] + [around_groups(cotangent, -shift) for shift in range(1, groups)]
+    plane_dy = jnp.stack(plane_dy)
+    plane_dy = [plane_dy] + [around_plane(plane_dy, -shift) for shift in range(1, inner)]
+    adapter_rows, backward_rows = make_rows(received, adapter_up, adapter_down)
+
+    if deep == 4:
+        hops[3] = send_layers(hops[3], ((1, 0), (2, 3)))
     received_input, adapter_rows, plane_dy, hops = lax.optimization_barrier(
         (received_input, adapter_rows, plane_dy, hops)
     )

time: 251 us -> 247 us (0.984)
  waiting for transfers between devices: 162 us -> 156 us
    ppermute x2, waiting for transfers between devices: 26.6 us -> 0.01 us  [next_layer(): return lax.ppermute(block, 'adapter', pairs)]
    ppermute x2, waiting for transfers between devices: 38.6 us -> 50.1 us  [send_layers(): return lax.ppermute(block, 'adapter', pairs)]
    all_to_all x1, waiting for transfers between devices: 0.01 us -> 7.85 us  [local(): lax.all_to_all(send, 'adapter', split_axis=0, concat_axis=0, tiled=True)]
    unnamed x27 -> x21, local copies, waits for them, and re-layouts: 7.67 us -> 6.84 us
  transfers between devices with their start and end apart: 18 -> 18, of which waited for: 13 -> 13; matrix products, arithmetic and copies ran while one was open for 9% -> 9% of each run, Pallas kernels for 8% -> 9%
where the time goes in v3:
time: 247 us; the launch traced here: 246 us
  waiting for transfers between devices  156 us (63%)
  starting transfers between devices  37.2 us (15%)
  Pallas kernels  28 us (11%)
  local copies, waits for them, and re-layouts  12.9 us (5%)
  matrix products  5.83 us (2%)
  other arithmetic  4.92 us (2%)
    ppermute x9, waiting for transfers between devices, around_plane(): return lax.ppermute(block, 'adapter', pairs)  54.8 us
    ppermute x2, waiting for transfers between devices, send_layers(): return lax.ppermute(block, 'adapter', pairs)  50.1 us
    ppermute x2, waiting for transfers between devices, around_groups(): return lax.ppermute(block, 'groups', pairs)  29.2 us
    pallas_call x1, Pallas kernels, make_grads(): pl.pallas_call(grads_kernel, grid=(width // BLOCK,), in_specs=[pl.BlockSp...  13.2 us
    all_to_all x1, waiting for transfers between devices, local(): lax.all_to_all(adapter_rows, 'adapter', split_axis=0, concat_axis=0, tile...  12.3 us
    all_to_all x1, starting transfers between devices, local(): lax.all_to_all(send, 'adapter', split_axis=0, concat_axis=0, tiled=True)  8.85 us
    all_to_all x1, waiting for transfers between devices, local(): lax.all_to_all(send, 'adapter', split_axis=0, concat_axis=0, tiled=True)  7.85 us
    ppermute x9, starting transfers between devices, around_plane(): return lax.ppermute(block, 'adapter', pairs)  7.57 us
  transfers between devices with their start and end apart: 18, of which 13 were waited for; matrix products, arithmetic and copies ran while one was open for 9% of the time, Pallas kernels for 9%

profile of v3, /device:TPU:15, one launch (start us, length us, event | category | flops | bytes accessed | tf_op | source)
XLA Modules:
  0.0 246.1 jit_solution(1603614016567920394)
XLA Ops:
  1.9 3.2 %collective-permute-start = (bf16[256,1024]{1,0:T(8,128)(2,1)S(1)}, bf16[256,1024]{1,0:T(8,128)(2,1)}, u32[]{:S(2)}, u32[]{:S(2)}) collective-permute-start(bf16[256,1024]{1,0:T(8,128)(2,1)S(1)} %constant_dynamic-slice_fusion), channel_id=1, source_target_pairs={{0,4},{1,5},{2,6},{3,7},{4,8},{5,9},{6,10},{7,11},{8,12},{9,13},{1... | collective-permute-start | bytes 1572872 | tf_op jit(solution)/shard_map/ppermute | solution.py:279
  5.1 2.9 %collective-permute-start.1 = (bf16[256,1024]{1,0:T(8,128)(2,1)S(1)}, bf16[256,1024]{1,0:T(8,128)(2,1)}, u32[]{:S(2)}, u32[]{:S(2)}) collective-permute-start(bf16[256,1024]{1,0:T(8,128)(2,1)S(1)} %constant_dynamic-slice_fusion), channel_id=1, source_target_pairs={{4,0},{5,1},{6,2},{7,3},{8,4},{9,5},{10,6},{11,7},{12,8},{13,9},{1... | collective-permute-start | bytes 1572872 | tf_op jit(solution)/shard_map/ppermute | solution.py:279
  9.3 2.2 shard_map.85
  11.5 8.9 %all-to-all-start.1 = ((bf16[16,16,1152]{2,1,0:T(8,128)(2,1)}), bf16[16,16,1152]{2,1,0:T(8,128)(2,1)S(1)}, u32[]{:S(2)}, u32[]{:S(2)}) async-start(bf16[16,16,1152]{2,1,0:T(8,128)(2,1)} %bitcast.51), calls=%async_computation.1 | async-start | bytes 1179648 | tf_op jit(solution)/shard_map/all_to_all | solution.py:311
  20.4 11.5 %collective-permute-done.2 = bf16[256,1024]{1,0:T(8,128)(2,1)} collective-permute-done((bf16[256,1024]{1,0:T(8,128)(2,1)S(1)}, bf16[256,1024]{1,0:T(8,128)(2,1)}, u32[]{:S(2)}, u32[]{:S(2)}) %collective-permute-start.2) | collective-permute-done | bytes 524320 | tf_op jit(solution)/shard_map/ppermute | solution.py:283
  34.2 3.3 %convolution_convert_fusion = bf16[256,8192]{1,0:T(8,128)(2,1)} fusion(bf16[256,128]{1,0:T(8,128)(2,1)S(1)} %copy-done.6, bf16[128,8192]{1,0:T(8,128)(2,1)S(1)} %copy-done), kind=kOutput, calls=%fused_computation | convolution fusion | flops 538968064 | bytes 6356992 | tf_op jit(solution)/shard_map/dot_general | solution.py:22
  37.5 7.9 %all-to-all-done.1 = bf16[16,16,1152]{2,1,0:T(8,128)(2,1)S(1)} async-done(((bf16[16,16,1152]{2,1,0:T(8,128)(2,1)}), bf16[16,16,1152]{2,1,0:T(8,128)(2,1)S(1)}, u32[]{:S(2)}, u32[]{:S(2)}) %all-to-all-start.1) | async-done | bytes 589856 | tf_op jit(solution)/shard_map/all_to_all | solution.py:311
  46.1 4.4 %all-to-all-start = ((bf16[16,16,8192]{2,1,0:T(8,128)(2,1)}), bf16[16,16,8192]{2,1,0:T(8,128)(2,1)}, u32[]{:S(2)}, u32[]{:S(2)}) async-start(bf16[16,16,8192]{2,1,0:T(8,128)(2,1)} %bitcast.45), calls=%async_computation | async-start | bytes 8388608 | tf_op jit(solution)/shard_map/all_to_all | solution.py:320
  50.6 3.0 %collective-permute-start.7 = (bf16[512,1024]{1,0:T(8,128)(2,1)}, bf16[512,1024]{1,0:T(8,128)(2,1)}, u32[]{:S(2)}, u32[]{:S(2)}) collective-permute-start(bf16[512,1024]{1,0:T(8,128)(2,1)} %pad_maximum_fusion.1), channel_id=1, source_target_pairs={{4,0},{5,1},{6,2},{7,3},{8,12},{9,13},{10,14},{11,15},{20,16},{21,... | collective-permute-start | bytes 3145736 | tf_op jit(solution)/shard_map/ppermute | solution.py:283
  53.9 7.1 %collective-permute-done.3 = bf16[128,1024]{1,0:T(8,128)(2,1)S(1)} collective-permute-done((bf16[128,1024]{1,0:T(8,128)(2,1)S(1)}, bf16[128,1024]{1,0:T(8,128)(2,1)S(1)}, u32[]{:S(2)}, u32[]{:S(2)}) %collective-permute-start.3) | collective-permute-done | bytes 262176 | tf_op jit(solution)/shard_map/ppermute | solution.py:290
  64.1 7.4 %shard_map.86 = (bf16[256,8192]{1,0:T(8,128)(2,1)}, bf16[256,512]{1,0:T(8,128)(2,1)}) custom-call(bf16[256,1152]{1,0:T(8,128)(2,1)} %bitcast.47, bf16[512,1024]{1,0:T(8,128)(2,1)} %up_ref.1, bf16[8192,512]{1,0:T(8,128)(2,1)} %down_ref.3), custom_call_target="tpu_custom_call" | custom-call | flops 2415919104 | bytes 14155776 | tf_op jit(solution)/shard_map/pallas_call | solution.py:110
  71.6 15.1 %collective-permute-done.4 = bf16[2,128,1024]{2,1,0:T(8,128)(2,1)} collective-permute-done((bf16[2,128,1024]{2,1,0:T(8,128)(2,1)S(1)}, bf16[2,128,1024]{2,1,0:T(8,128)(2,1)}, u32[]{:S(2)}, u32[]{:S(2)}) %collective-permute-start.4) | collective-permute-done | bytes 524320 | tf_op jit(solution)/shard_map/ppermute | solution.py:298
  86.7 15.6 %collective-permute-done.6 = bf16[2,128,1024]{2,1,0:T(8,128)(2,1)} collective-permute-done((bf16[2,128,1024]{2,1,0:T(8,128)(2,1)S(1)}, bf16[2,128,1024]{2,1,0:T(8,128)(2,1)}, u32[]{:S(2)}, u32[]{:S(2)}) %collective-permute-start.6) | collective-permute-done | bytes 524320 | tf_op jit(solution)/shard_map/ppermute | solution.py:298
  102.3 38.6 %collective-permute-done.7 = bf16[512,1024]{1,0:T(8,128)(2,1)} collective-permute-done((bf16[512,1024]{1,0:T(8,128)(2,1)}, bf16[512,1024]{1,0:T(8,128)(2,1)}, u32[]{:S(2)}, u32[]{:S(2)}) %collective-permute-start.7) | collective-permute-done | bytes 1048608 | tf_op jit(solution)/shard_map/ppermute | solution.py:283
  140.9 2.2 all-to-all-done
  143.1 5.4 %all-to-all-start.2 = ((bf16[16,16,8192]{2,1,0:T(8,128)(2,1)}), bf16[16,16,8192]{2,1,0:T(8,128)(2,1)}, u32[]{:S(2)}, u32[]{:S(2)}) async-start(bf16[16,16,8192]{2,1,0:T(8,128)(2,1)} %bitcast.46), calls=%async_computation.2 | async-start | bytes 8388608 | tf_op jit(solution)/shard_map/all_to_all | solution.py:332
  156.2 22.2 %collective-permute-done.8 = bf16[512,1024]{1,0:T(8,128)(2,1)S(1)} collective-permute-done((bf16[512,1024]{1,0:T(8,128)(2,1)S(1)}, bf16[512,1024]{1,0:T(8,128)(2,1)S(1)}, u32[]{:S(2)}, u32[]{:S(2)}) %collective-permute-start.8) | collective-permute-done | bytes 1048608 | tf_op jit(solution)/shard_map/ppermute | solution.py:290
  181.6 13.2 %shard_map.88 = (bf16[8192,512]{1,0:T(8,128)(2,1)}, bf16[512,1024]{1,0:T(8,128)(2,1)}) custom-call(bf16[256,8192]{1,0:T(8,128)(2,1)} %bitcast.4.x_ref, bf16[256,1152]{1,0:T(8,128)(2,1)} %bitcast.48, bf16[256,1152]{1,0:T(8,128)(2,1)} %bitcast.49, bf16[256,512]{1,0:T(8,128)(2,1)} %get-tuple-element.56.backward_ref, bf16[8192,512]{1,0:T(8,128)(2,1)} %down_ref.3), custom_call_target="tpu_custom_call" | custom-call | flops 4563402752 | bytes 23592960 | tf_op jit(solution)/shard_map/pallas_call | solution.py:161
  201.7 8.8 %collective-permute-done.11 = bf16[128,1024]{1,0:T(8,128)(2,1)S(1)} collective-permute-done((bf16[128,1024]{1,0:T(8,128)(2,1)}, bf16[128,1024]{1,0:T(8,128)(2,1)S(1)}, u32[]{:S(2)}, u32[]{:S(2)}) %collective-permute-start.11) | collective-permute-done | bytes 262176 | tf_op jit(solution)/shard_map/ppermute | solution.py:298
  211.3 10.4 %collective-permute-done.12 = bf16[128,1024]{1,0:T(8,128)(2,1)S(1)} collective-permute-done((bf16[128,1024]{1,0:T(8,128)(2,1)}, bf16[128,1024]{1,0:T(8,128)(2,1)S(1)}, u32[]{:S(2)}, u32[]{:S(2)}) %collective-permute-start.12) | collective-permute-done | bytes 262176 | tf_op jit(solution)/shard_map/ppermute | solution.py:298
  222.4 2.7 %collective-permute-done.13 = bf16[128,1024]{1,0:T(8,128)(2,1)S(1)} collective-permute-done((bf16[128,1024]{1,0:T(8,128)(2,1)S(1)}, bf16[128,1024]{1,0:T(8,128)(2,1)S(1)}, u32[]{:S(2)}, u32[]{:S(2)}) %collective-permute-start.13) | collective-permute-done | bytes 262176 | tf_op jit(solution)/shard_map/ppermute | solution.py:298
  225.9 2.1 collective-permute-done.14
  228.7 12.3 %all-to-all-done.2 = bf16[16,16,8192]{2,1,0:T(8,128)(2,1)} async-done(((bf16[16,16,8192]{2,1,0:T(8,128)(2,1)}), bf16[16,16,8192]{2,1,0:T(8,128)(2,1)}, u32[]{:S(2)}, u32[]{:S(2)}) %all-to-all-start.2) | async-done | bytes 4194336 | tf_op jit(solution)/shard_map/all_to_all | solution.py:332
  241.0 5.1 %shard_map.87 = bf16[128,8192]{1,0:T(8,128)(2,1)} custom-call(s32[2]{0:T(128)} %pad_add_fusion.at_ref, bf16[128,256]{1,0:T(8,128)(2,1)} %get-tuple-element.32.place_ref, bf16[256,8192]{1,0:T(8,128)(2,1)} %bitcast.10.rows_ref, bf16[8,128,1024]{2,1,0:T(8,128)(2,1)} %bitcast_dynamic-update-slice_fusion.base_ref), custom_call_target="tpu_custom_call" | custom-call | flops 536870912 | bytes 8388608 | tf_op jit(solution)/shard_map/pallas_call | solution.py:239
  (51 shorter events, 29.8 us)
Async XLA Ops:
  0.6 33.6 %copy-start = (bf16[128,8192]{1,0:T(8,128)(2,1)S(1)}, bf16[128,8192]{1,0:T(8,128)(2,1)}, u32[]{:S(2)}) copy-start(bf16[128,8192]{1,0:T(8,128)(2,1)} %param.6) | copy-start | bytes 6291460
  1.9 18.5 %collective-permute-start = (bf16[256,1024]{1,0:T(8,128)(2,1)S(1)}, bf16[256,1024]{1,0:T(8,128)(2,1)}, u32[]{:S(2)}, u32[]{:S(2)}) collective-permute-start(bf16[256,1024]{1,0:T(8,128)(2,1)S(1)} %constant_dynamic-slice_fusion), channel_id=1, source_target_pairs={{0,4},{1,5},{2,6},{3,7},{4,8},{5,9},{6,10},{7,11},{8,12},{9,13},{1... | collective-permute-start | bytes 1572872 | tf_op jit(solution)/shard_map/ppermute | solution.py:279
  5.1 15.3 %collective-permute-start.1 = (bf16[256,1024]{1,0:T(8,128)(2,1)S(1)}, bf16[256,1024]{1,0:T(8,128)(2,1)}, u32[]{:S(2)}, u32[]{:S(2)}) collective-permute-start(bf16[256,1024]{1,0:T(8,128)(2,1)S(1)} %constant_dynamic-slice_fusion), channel_id=1, source_target_pairs={{4,0},{5,1},{6,2},{7,3},{8,4},{9,5},{10,6},{11,7},{12,8},{13,9},{1... | collective-permute-start | bytes 1572872 | tf_op jit(solution)/shard_map/ppermute | solution.py:279
  8.0 23.9 %collective-permute-start.2 = (bf16[256,1024]{1,0:T(8,128)(2,1)S(1)}, bf16[256,1024]{1,0:T(8,128)(2,1)}, u32[]{:S(2)}, u32[]{:S(2)}) collective-permute-start(bf16[256,1024]{1,0:T(8,128)(2,1)S(1)} %constant_dynamic-slice_fusion), channel_id=1, source_target_pairs={{0,8},{1,9},{2,10},{3,11},{12,4},{13,5},{14,6},{15,7},{16,24},{17,... | collective-permute-start | bytes 1572872 | tf_op jit(solution)/shard_map/ppermute | solution.py:283
  11.5 33.8 %all-to-all-start.1 = ((bf16[16,16,1152]{2,1,0:T(8,128)(2,1)}), bf16[16,16,1152]{2,1,0:T(8,128)(2,1)S(1)}, u32[]{:S(2)}, u32[]{:S(2)}) async-start(bf16[16,16,1152]{2,1,0:T(8,128)(2,1)} %bitcast.51), calls=%async_computation.1 | async-start | bytes 1179648 | tf_op jit(solution)/shard_map/all_to_all | solution.py:311
  20.4 13.8 %copy-start.6 = (bf16[256,128]{1,0:T(8,128)(2,1)S(1)}, bf16[256,128]{1,0:T(8,128)(2,1)}, u32[]{:S(2)}) copy-start(bf16[256,128]{1,0:T(8,128)(2,1)} %get-tuple-element.35) | copy-start | bytes 196612
  45.3 8.3 %copy-start.3 = (bf16[128,1024]{1,0:T(8,128)(2,1)S(1)}, bf16[128,1024]{1,0:T(8,128)(2,1)}, u32[]{:S(2)}) copy-start(bf16[128,1024]{1,0:T(8,128)(2,1)} %dy_ref.1) | copy-start | bytes 786436
  46.1 97.0 %all-to-all-start = ((bf16[16,16,8192]{2,1,0:T(8,128)(2,1)}), bf16[16,16,8192]{2,1,0:T(8,128)(2,1)}, u32[]{:S(2)}, u32[]{:S(2)}) async-start(bf16[16,16,8192]{2,1,0:T(8,128)(2,1)} %bitcast.45), calls=%async_computation | async-start | bytes 8388608 | tf_op jit(solution)/shard_map/all_to_all | solution.py:320
  50.6 90.3 %collective-permute-start.7 = (bf16[512,1024]{1,0:T(8,128)(2,1)}, bf16[512,1024]{1,0:T(8,128)(2,1)}, u32[]{:S(2)}, u32[]{:S(2)}) collective-permute-start(bf16[512,1024]{1,0:T(8,128)(2,1)} %pad_maximum_fusion.1), channel_id=1, source_target_pairs={{4,0},{5,1},{6,2},{7,3},{8,12},{9,13},{10,14},{11,15},{20,16},{21,... | collective-permute-start | bytes 3145736 | tf_op jit(solution)/shard_map/ppermute | solution.py:283
  53.6 7.3 %collective-permute-start.3 = (bf16[128,1024]{1,0:T(8,128)(2,1)S(1)}, bf16[128,1024]{1,0:T(8,128)(2,1)S(1)}, u32[]{:S(2)}, u32[]{:S(2)}) collective-permute-start(bf16[128,1024]{1,0:T(8,128)(2,1)S(1)} %copy-done.3), channel_id=1, source_target_pairs={{0,16},{16,0},{1,17},{17,1},{2,18},{18,2},{3,19},{19,3},{4,20},{20... | collective-permute-start | bytes 786440 | tf_op jit(solution)/shard_map/ppermute | solution.py:290
  61.0 25.7 %collective-permute-start.4 = (bf16[2,128,1024]{2,1,0:T(8,128)(2,1)S(1)}, bf16[2,128,1024]{2,1,0:T(8,128)(2,1)}, u32[]{:S(2)}, u32[]{:S(2)}) collective-permute-start(bf16[2,128,1024]{2,1,0:T(8,128)(2,1)S(1)} %pad_maximum_fusion.2), channel_id=1, source_target_pairs={{0,3},{1,0},{2,1},{3,2},{4,7},{5,4},{6,5},{7,6},{8,11},{9,8},{10,9... | collective-permute-start | bytes 1572872 | tf_op jit(solution)/shard_map/ppermute | solution.py:298
  62.4 24.3 %collective-permute-start.5 = (bf16[2,128,1024]{2,1,0:T(8,128)(2,1)S(1)}, bf16[2,128,1024]{2,1,0:T(8,128)(2,1)S(1)}, u32[]{:S(2)}, u32[]{:S(2)}) collective-permute-start(bf16[2,128,1024]{2,1,0:T(8,128)(2,1)S(1)} %pad_maximum_fusion.2), channel_id=1, source_target_pairs={{0,2},{1,3},{2,0},{3,1},{4,6},{5,7},{6,4},{7,5},{8,10},{9,11},{10,... | collective-permute-start | bytes 1572872 | tf_op jit(solution)/shard_map/ppermute | solution.py:298
  62.6 39.7 %collective-permute-start.6 = (bf16[2,128,1024]{2,1,0:T(8,128)(2,1)S(1)}, bf16[2,128,1024]{2,1,0:T(8,128)(2,1)}, u32[]{:S(2)}, u32[]{:S(2)}) collective-permute-start(bf16[2,128,1024]{2,1,0:T(8,128)(2,1)S(1)} %pad_maximum_fusion.2), channel_id=1, source_target_pairs={{0,1},{1,2},{2,3},{3,0},{4,5},{5,6},{6,7},{7,4},{8,9},{9,10},{10,1... | collective-permute-start | bytes 1572872 | tf_op jit(solution)/shard_map/ppermute | solution.py:298
  86.7 15.6 %copy-start.4 = (bf16[2,128,1024]{2,1,0:T(8,128)(2,1)}, bf16[2,128,1024]{2,1,0:T(8,128)(2,1)S(1)}, u32[]{:S(2)}) copy-start(bf16[2,128,1024]{2,1,0:T(8,128)(2,1)S(1)} %collective-permute-done.5) | copy-start | bytes 1572868
  143.1 97.9 %all-to-all-start.2 = ((bf16[16,16,8192]{2,1,0:T(8,128)(2,1)}), bf16[16,16,8192]{2,1,0:T(8,128)(2,1)}, u32[]{:S(2)}, u32[]{:S(2)}) async-start(bf16[16,16,8192]{2,1,0:T(8,128)(2,1)} %bitcast.46), calls=%async_computation.2 | async-start | bytes 8388608 | tf_op jit(solution)/shard_map/all_to_all | solution.py:332
  148.5 1.2 copy-start.5
  154.0 24.4 %collective-permute-start.8 = (bf16[512,1024]{1,0:T(8,128)(2,1)S(1)}, bf16[512,1024]{1,0:T(8,128)(2,1)S(1)}, u32[]{:S(2)}, u32[]{:S(2)}) collective-permute-start(bf16[512,1024]{1,0:T(8,128)(2,1)S(1)} %convolution_convert_fusion.1), channel_id=1, source_target_pairs={{0,16},{16,0},{1,17},{17,1},{2,18},{18,2},{3,19},{19,3},{4,20},{20... | collective-permute-start | bytes 3145736 | tf_op jit(solution)/shard_map/ppermute | solution.py:290
  156.2 22.2 %copy-start.2 = (bf16[512,1024]{1,0:T(8,128)(2,1)}, bf16[512,1024]{1,0:T(8,128)(2,1)S(1)}, u32[]{:S(2)}) copy-start(bf16[512,1024]{1,0:T(8,128)(2,1)S(1)} %convolution_convert_fusion.2) | copy-start | bytes 3145732
  179.3 20.5 %collective-permute-start.9 = (bf16[128,1024]{1,0:T(8,128)(2,1)}, bf16[128,1024]{1,0:T(8,128)(2,1)S(1)}, u32[]{:S(2)}, u32[]{:S(2)}) collective-permute-start(bf16[128,1024]{1,0:T(8,128)(2,1)} %get-tuple-element.68), channel_id=1, source_target_pairs={{0,1},{1,2},{2,3},{3,0},{4,5},{5,6},{6,7},{7,4},{8,9},{9,10},{10,1... | collective-permute-start | bytes 786440 | tf_op jit(solution)/shard_map/ppermute | solution.py:298
  181.6 19.4 %collective-permute-start.10 = (bf16[128,1024]{1,0:T(8,128)(2,1)}, bf16[128,1024]{1,0:T(8,128)(2,1)S(1)}, u32[]{:S(2)}, u32[]{:S(2)}) collective-permute-start(bf16[128,1024]{1,0:T(8,128)(2,1)} %get-tuple-element.65), channel_id=1, source_target_pairs={{0,1},{1,2},{2,3},{3,0},{4,5},{5,6},{6,7},{7,4},{8,9},{9,10},{10,1... | collective-permute-start | bytes 786440 | tf_op jit(solution)/shard_map/ppermute | solution.py:298
  197.2 13.3 %collective-permute-start.11 = (bf16[128,1024]{1,0:T(8,128)(2,1)}, bf16[128,1024]{1,0:T(8,128)(2,1)S(1)}, u32[]{:S(2)}, u32[]{:S(2)}) collective-permute-start(bf16[128,1024]{1,0:T(8,128)(2,1)} %get-tuple-element.67), channel_id=1, source_target_pairs={{0,2},{1,3},{2,0},{3,1},{4,6},{5,7},{6,4},{7,5},{8,10},{9,11},{10,... | collective-permute-start | bytes 786440 | tf_op jit(solution)/shard_map/ppermute | solution.py:298
  198.4 23.2 %collective-permute-start.12 = (bf16[128,1024]{1,0:T(8,128)(2,1)}, bf16[128,1024]{1,0:T(8,128)(2,1)S(1)}, u32[]{:S(2)}, u32[]{:S(2)}) collective-permute-start(bf16[128,1024]{1,0:T(8,128)(2,1)} %get-tuple-element.64), channel_id=1, source_target_pairs={{0,2},{1,3},{2,0},{3,1},{4,6},{5,7},{6,4},{7,5},{8,10},{9,11},{10,... | collective-permute-start | bytes 786440 | tf_op jit(solution)/shard_map/ppermute | solution.py:298
  198.7 26.4 %collective-permute-start.13 = (bf16[128,1024]{1,0:T(8,128)(2,1)S(1)}, bf16[128,1024]{1,0:T(8,128)(2,1)S(1)}, u32[]{:S(2)}, u32[]{:S(2)}) collective-permute-start(bf16[128,1024]{1,0:T(8,128)(2,1)S(1)} %get-tuple-element.66), channel_id=1, source_target_pairs={{0,3},{1,0},{2,1},{3,2},{4,7},{5,4},{6,5},{7,6},{8,11},{9,8},{10,9... | collective-permute-start | bytes 786440 | tf_op jit(solution)/shard_map/ppermute | solution.py:298
  199.8 28.2 %collective-permute-start.14 = (bf16[128,1024]{1,0:T(8,128)(2,1)}, bf16[128,1024]{1,0:T(8,128)(2,1)S(1)}, u32[]{:S(2)}, u32[]{:S(2)}) collective-permute-start(bf16[128,1024]{1,0:T(8,128)(2,1)} %get-tuple-element.63), channel_id=1, source_target_pairs={{0,3},{1,0},{2,1},{3,2},{4,7},{5,4},{6,5},{7,6},{8,11},{9,8},{10,9... | collective-permute-start | bytes 786440 | tf_op jit(solution)/shard_map/ppermute | solution.py:298
  (1 other events, 0.8 us)

commit v4 on v3

--- a/solution.py
+++ b/solution.py
@@ -13,6 +13,7 @@
 LANES = 128
 BLOCK = 1024
 VMEM = 60 << 20
+PAIR_FLOPS = 100_000_000_000
 
 
 SCALE = 2.0
@@ -56,6 +57,32 @@
         ],
         compiler_params=pltpu.CompilerParams(vmem_limit_bytes=VMEM),
     )(family.reshape(1, tok_rows), cotangent)
+
+
+def pack_x_kernel(place_ref, x_ref, out_ref):
+    out_ref[...] = dot(place_ref[...], x_ref[...], ((1,), (0,))).astype(jnp.bfloat16)
+
+
+def pack_x(place, activations):
+    token_slots, tok_rows = place.shape
+    width = activations.shape[1]
+    columns = 2 * BLOCK
+    return pl.pallas_call(
+        pack_x_kernel,
+        grid=(width // columns,),
+        in_specs=[
+            pl.BlockSpec((token_slots, tok_rows), lambda j: (0, 0)),
+            pl.BlockSpec((tok_rows, columns), lambda j: (0, j)),
+        ],
+        out_specs=pl.BlockSpec((token_slots, columns), lambda j: (0, j)),
+        out_shape=jax.ShapeDtypeStruct((token_slots, width), jnp.bfloat16),
+        compiler_params=pltpu.CompilerParams(vmem_limit_bytes=VMEM),
+        cost_estimate=pl.CostEstimate(
+            flops=2 * tok_rows * token_slots * width,
+            bytes_accessed=2 * width * (token_slots + tok_rows),
+            transcendentals=0,
+        ),
+    )(place, activations)
 
 
 def own_columns(family_ref, columns):
@@ -261,6 +288,34 @@
     )(at, place, rows, base)
 
 
+def pair_kernel(layer_ref, below_ref, above_ref, over_ref, out_ref):
+    share = below_ref.shape[0]
+
+    @pl.when(layer_ref[0] < 2)
+    def _():
+        out_ref[:share] = above_ref[...]
+        out_ref[share:] = over_ref[...]
+
+    @pl.when(layer_ref[0] >= 2)
+    def _():
+        out_ref[:share] = over_ref[...]
+        out_ref[share:] = below_ref[...]
+
+
+def make_pair(layer, below, above, over):
+    share, features = below.shape
+    whole = pl.BlockSpec(memory_space=pltpu.VMEM)
+    return pl.pallas_call(
+        pair_kernel,
+        in_specs=[pl.BlockSpec(memory_space=pltpu.SMEM), whole, whole, whole],
+        out_specs=whole,
+        out_shape=jax.ShapeDtypeStruct((2 * share, features), jnp.bfloat16),
+        cost_estimate=pl.CostEstimate(
+            flops=PAIR_FLOPS, bytes_accessed=10 * share * features, transcendentals=0
+        ),
+    )(layer[None], below, above, over)
+
+
 def local(activations, cotangent, family, value_weight, adapter_down, adapter_up):
     count = lax.axis_size("adapter")
     groups = lax.axis_size("groups")
@@ -301,22 +356,18 @@
     own_share = lax.dynamic_slice_in_dim(value_weight, my_group * share, share, 0)
     family, own_share = lax.optimization_barrier((family, own_share))
     hops = [next_layer(own_share, inner), next_layer(own_share, -inner)]
+    if deep > 4:
+        for step in range(2, deep):
+            hops += [next_layer(own_share, step * inner), next_layer(own_share, -step * inner)]
+
+    send, place, back_place = pack(family, cotangent, cap, token_slots)
+    received = lax.all_to_all(send, "adapter", split_axis=0, concat_axis=0, tiled=True)
+    send_x = pack_x(place, activations)
+    received, own_share, cotangent, send_x = lax.optimization_barrier(
+        (received, own_share, cotangent, send_x)
+    )
     if deep == 4:
         hops.append(send_layers(own_share, ((0, 2), (3, 1))))
-    else:
-        for step in range(2, deep):
-            hops += [next_layer(own_share, step * inner), next_layer(own_share, -step * inner)]
-
-    send, place, back_place = pack(family, cotangent, cap, token_slots)
-    received = lax.all_to_all(send, "adapter", split_axis=0, concat_axis=0, tiled=True)
-    below, above = hops[:2]
-    if deep == 4:
-        lower = my_layer < 2
-        over = hops[2]
-        pair = jnp.concatenate([jnp.where(lower, above, over), jnp.where(lower, over, below)], axis=0)
-        hops.append(pair)
-    place, hops, cotangent = lax.optimization_barrier((place, hops, cotangent))
-    send_x = dot(place, activations, ((1,), (0,))).astype(jnp.bfloat16)
     received_input = lax.all_to_all(send_x, "adapter", split_axis=0, concat_axis=0, tiled=True)
 
     plane_dy = [cotangent] + [around_groups(cotangent, -shift) for shift in range(1, groups)]
@@ -325,7 +376,7 @@
     adapter_rows, backward_rows = make_rows(received, adapter_up, adapter_down)
 
     if deep == 4:
-        hops[3] = send_layers(hops[3], ((1, 0), (2, 3)))
+        hops.append(send_layers(make_pair(my_layer, *hops), ((1, 0), (2, 3))))
     received_input, adapter_rows, plane_dy, hops = lax.optimization_barrier(
         (received_input, adapter_rows, plane_dy, hops)
     )
@@ -353,13 +404,13 @@
 
     blocks = [dot(block, plane_weight, ((1,), (1,))).astype(jnp.bfloat16) for block in plane_dy]
     blocks = blocks[:1] + [around_groups(block, s) for s, block in enumerate(blocks) if s]
-    received_input, blocks = lax.optimization_barrier((received_input, blocks))
     base = []
     for shift in range(inner):
         for block in blocks:
             piece = block[shift * tok_rows : (shift + 1) * tok_rows]
             base.append(around_plane(piece, shift) if shift else piece)
     base = jnp.stack(base)
+    received_input, base = lax.optimization_barrier((received_input, base))
     grad_down, grad_up = make_grads(
         received_input, received, backward_rows, adapter_up, adapter_down
     )

time: 247 us -> 243 us (0.984)
  local copies, waits for them, and re-layouts: 12.9 us -> 3.93 us
  Pallas kernels: 28 us -> 36.1 us
  starting transfers between devices: 37.2 us -> 42.2 us
  matrix products: 5.83 us -> 2.57 us
  other arithmetic: 4.92 us -> 1.99 us
    ppermute x2, waiting for transfers between devices: 50.1 us -> 0.01 us  [send_layers(): return lax.ppermute(block, 'adapter', pairs)]
    ppermute x2, waiting for transfers between devices: 0.01 us -> 28.6 us  [next_layer(): return lax.ppermute(block, 'adapter', pairs)]
    all_to_all x1, waiting for transfers between devices: 2.17 us -> 15.9 us  [local(): lax.all_to_all(send_x, 'adapter', split_axis=0, concat_axis=0, tiled=True)]
    all_to_all x1, waiting for transfers between devices: 12.3 us -> 26.1 us  [local(): lax.all_to_all(adapter_rows, 'adapter', split_axis=0, concat_axis=0, tile...]
    pallas_call x0 -> x2, Pallas kernels: none -> 7.35 us  [the longest x1 4.91 us: pack_x(): pl.pallas_call(pack_x_kernel, grid=(width // columns,), in_specs=[pl.Bloc...]
    ppermute x9, starting transfers between devices: 7.57 us -> 12.7 us  [around_plane(): return lax.ppermute(block, 'adapter', pairs)]
    unnamed x21 -> x27, local copies, waits for them, and re-layouts: 6.84 us -> 2.3 us
    all_to_all x1, starting transfers between devices: 4.44 us -> 8.53 us  [local(): lax.all_to_all(send_x, 'adapter', split_axis=0, concat_axis=0, tiled=True)]
  transfers between devices with their start and end apart: 18 -> 18, of which waited for: 13 -> 12; matrix products, arithmetic and copies ran while one was open for 9% -> 3% of each run, Pallas kernels for 9% -> 12%
where the time goes in v4:
time: 243 us; the launch traced here: 242 us
  waiting for transfers between devices  154 us (63%)
  starting transfers between devices  42.2 us (17%)
  Pallas kernels  36.1 us (15%)
  local copies, waits for them, and re-layouts  3.93 us (2%)
  matrix products  2.57 us (1%)
    ppermute x9, waiting for transfers between devices, around_plane(): return lax.ppermute(block, 'adapter', pairs)  51.7 us
    ppermute x2, waiting for transfers between devices, next_layer(): return lax.ppermute(block, 'adapter', pairs)  28.6 us
    ppermute x2, waiting for transfers between devices, around_groups(): return lax.ppermute(block, 'groups', pairs)  26.3 us
    all_to_all x1, waiting for transfers between devices, local(): lax.all_to_all(adapter_rows, 'adapter', split_axis=0, concat_axis=0, tile...  26.1 us
    all_to_all x1, waiting for transfers between devices, local(): lax.all_to_all(send_x, 'adapter', split_axis=0, concat_axis=0, tiled=True)  15.9 us
    pallas_call x1, Pallas kernels, make_grads(): pl.pallas_call(grads_kernel, grid=(width // BLOCK,), in_specs=[pl.BlockSp...  14 us
    ppermute x9, starting transfers between devices, around_plane(): return lax.ppermute(block, 'adapter', pairs)  12.7 us
    all_to_all x1, starting transfers between devices, local(): lax.all_to_all(send_x, 'adapter', split_axis=0, concat_axis=0, tiled=True)  8.53 us
  transfers between devices with their start and end apart: 18, of which 12 were waited for; matrix products, arithmetic and copies ran while one was open for 3% of the time, Pallas kernels for 12%

profile of v4, /device:TPU:15, one launch (start us, length us, event | category | flops | bytes accessed | tf_op | source)
XLA Modules:
  0.0 241.9 jit_solution(15154543801138940375)
XLA Ops:
  1.9 2.2 shard_map.85
  4.1 6.6 %all-to-all-start = ((bf16[16,16,1152]{2,1,0:T(8,128)(2,1)}), bf16[16,16,1152]{2,1,0:T(8,128)(2,1)S(1)}, u32[]{:S(2)}, u32[]{:S(2)}) async-start(bf16[16,16,1152]{2,1,0:T(8,128)(2,1)} %bitcast.54), calls=%async_computation | async-start | bytes 1179648 | tf_op jit(solution)/shard_map/all_to_all | solution.py:364
  10.7 3.1 %collective-permute-start.4 = (bf16[256,1024]{1,0:T(8,128)(2,1)S(1)}, bf16[256,1024]{1,0:T(8,128)(2,1)S(1)}, u32[]{:S(2)}, u32[]{:S(2)}) collective-permute-start(bf16[256,1024]{1,0:T(8,128)(2,1)S(1)} %constant_dynamic-slice_fusion), channel_id=1, source_target_pairs={{0,4},{1,5},{2,6},{3,7},{4,8},{5,9},{6,10},{7,11},{8,12},{9,13},{1... | collective-permute-start | bytes 1572872 | tf_op jit(solution)/shard_map/ppermute | solution.py:334
  13.8 2.2 collective-permute-start.5
  16.0 4.9 %shard_map.86 = bf16[256,8192]{1,0:T(8,128)(2,1)} custom-call(bf16[256,128]{1,0:T(8,128)(2,1)} %get-tuple-element.32.place_ref, bf16[128,8192]{1,0:T(8,128)(2,1)} %x_ref.1), custom_call_target="tpu_custom_call" | custom-call | flops 536870912 | bytes 6291456 | tf_op jit(solution)/shard_map/pallas_call | solution.py:70
  20.9 5.6 %all-to-all-done = bf16[16,16,1152]{2,1,0:T(8,128)(2,1)S(1)} async-done(((bf16[16,16,1152]{2,1,0:T(8,128)(2,1)}), bf16[16,16,1152]{2,1,0:T(8,128)(2,1)S(1)}, u32[]{:S(2)}, u32[]{:S(2)}) %all-to-all-start) | async-done | bytes 589856 | tf_op jit(solution)/shard_map/all_to_all | solution.py:364
  27.8 8.5 %all-to-all-start.1 = ((bf16[16,16,8192]{2,1,0:T(8,128)(2,1)}), bf16[16,16,8192]{2,1,0:T(8,128)(2,1)}, u32[]{:S(2)}, u32[]{:S(2)}) async-start(bf16[16,16,8192]{2,1,0:T(8,128)(2,1)} %bitcast.48), calls=%async_computation.1 | async-start | bytes 8388608 | tf_op jit(solution)/shard_map/all_to_all | solution.py:371
  36.4 9.7 %collective-permute-done.4.below_ref = bf16[256,1024]{1,0:T(8,128)(2,1)S(1)} collective-permute-done((bf16[256,1024]{1,0:T(8,128)(2,1)S(1)}, bf16[256,1024]{1,0:T(8,128)(2,1)S(1)}, u32[]{:S(2)}, u32[]{:S(2)}) %collective-permute-start.4) | collective-permute-done | bytes 524320 | tf_op jit(solution)/shard_map/ppermute | solution.py:334
  46.1 18.9 %collective-permute-done.5.above_ref = bf16[256,1024]{1,0:T(8,128)(2,1)S(1)} collective-permute-done((bf16[256,1024]{1,0:T(8,128)(2,1)S(1)}, bf16[256,1024]{1,0:T(8,128)(2,1)S(1)}, u32[]{:S(2)}, u32[]{:S(2)}) %collective-permute-start.5) | collective-permute-done | bytes 524320 | tf_op jit(solution)/shard_map/ppermute | solution.py:334
  65.8 2.4 %shard_map.88 = bf16[512,1024]{1,0:T(8,128)(2,1)} custom-call(s32[1]{0:T(128)} %bitcast.9.layer_ref, bf16[256,1024]{1,0:T(8,128)(2,1)} %copy-done.4, bf16[256,1024]{1,0:T(8,128)(2,1)} %copy-done.6, bf16[256,1024]{1,0:T(8,128)(2,1)} %collective-permute-done.6.over_ref), custom_call_target="tpu_custom_call" | custom-call | flops 99999997952 | bytes 2621440 | tf_op jit(solution)/shard_map/pallas_call | solution.py:308
  69.9 6.3 %collective-permute-done = bf16[128,1024]{1,0:T(8,128)(2,1)S(1)} collective-permute-done((bf16[128,1024]{1,0:T(8,128)(2,1)S(1)}, bf16[128,1024]{1,0:T(8,128)(2,1)S(1)}, u32[]{:S(2)}, u32[]{:S(2)}) %collective-permute-start) | collective-permute-done | bytes 262176 | tf_op jit(solution)/shard_map/ppermute | solution.py:345
  78.5 5.8 %collective-permute-start.2 = (bf16[2,128,1024]{2,1,0:T(8,128)(2,1)S(1)}, bf16[2,128,1024]{2,1,0:T(8,128)(2,1)}, u32[]{:S(2)}, u32[]{:S(2)}) collective-permute-start(bf16[2,128,1024]{2,1,0:T(8,128)(2,1)S(1)} %pad_maximum_fusion.1), channel_id=1, source_target_pairs={{0,2},{1,3},{2,0},{3,1},{4,6},{5,7},{6,4},{7,5},{8,10},{9,11},{10,... | collective-permute-start | bytes 1572872 | tf_op jit(solution)/shard_map/ppermute | solution.py:353
  84.3 7.4 %shard_map.87 = (bf16[256,8192]{1,0:T(8,128)(2,1)}, bf16[256,512]{1,0:T(8,128)(2,1)}) custom-call(bf16[256,1152]{1,0:T(8,128)(2,1)} %bitcast.50, bf16[512,1024]{1,0:T(8,128)(2,1)} %up_ref.1, bf16[8192,512]{1,0:T(8,128)(2,1)} %down_ref.3), custom_call_target="tpu_custom_call" | custom-call | flops 2415919104 | bytes 14155776 | tf_op jit(solution)/shard_map/pallas_call | solution.py:137
  91.7 14.7 %collective-permute-done.1 = bf16[2,128,1024]{2,1,0:T(8,128)(2,1)S(1)} collective-permute-done((bf16[2,128,1024]{2,1,0:T(8,128)(2,1)S(1)}, bf16[2,128,1024]{2,1,0:T(8,128)(2,1)S(1)}, u32[]{:S(2)}, u32[]{:S(2)}) %collective-permute-start.1) | collective-permute-done | bytes 524320 | tf_op jit(solution)/shard_map/ppermute | solution.py:353
  106.3 6.4 %collective-permute-done.2 = bf16[2,128,1024]{2,1,0:T(8,128)(2,1)} collective-permute-done((bf16[2,128,1024]{2,1,0:T(8,128)(2,1)S(1)}, bf16[2,128,1024]{2,1,0:T(8,128)(2,1)}, u32[]{:S(2)}, u32[]{:S(2)}) %collective-permute-start.2) | collective-permute-done | bytes 524320 | tf_op jit(solution)/shard_map/ppermute | solution.py:353
  112.7 9.8 %collective-permute-done.3 = bf16[2,128,1024]{2,1,0:T(8,128)(2,1)} collective-permute-done((bf16[2,128,1024]{2,1,0:T(8,128)(2,1)S(1)}, bf16[2,128,1024]{2,1,0:T(8,128)(2,1)}, u32[]{:S(2)}, u32[]{:S(2)}) %collective-permute-start.3) | collective-permute-done | bytes 524320 | tf_op jit(solution)/shard_map/ppermute | solution.py:353
  122.5 15.9 %all-to-all-done.1 = bf16[16,16,8192]{2,1,0:T(8,128)(2,1)} async-done(((bf16[16,16,8192]{2,1,0:T(8,128)(2,1)}), bf16[16,16,8192]{2,1,0:T(8,128)(2,1)}, u32[]{:S(2)}, u32[]{:S(2)}) %all-to-all-start.1) | async-done | bytes 4194336 | tf_op jit(solution)/shard_map/all_to_all | solution.py:371
  138.4 5.9 %all-to-all-start.2 = ((bf16[16,16,8192]{2,1,0:T(8,128)(2,1)}), bf16[16,16,8192]{2,1,0:T(8,128)(2,1)}, u32[]{:S(2)}, u32[]{:S(2)}) async-start(bf16[16,16,8192]{2,1,0:T(8,128)(2,1)} %bitcast.49), calls=%async_computation.2 | async-start | bytes 8388608 | tf_op jit(solution)/shard_map/all_to_all | solution.py:383
  152.9 20.0 %collective-permute-done.8 = bf16[512,1024]{1,0:T(8,128)(2,1)S(1)} collective-permute-done((bf16[512,1024]{1,0:T(8,128)(2,1)S(1)}, bf16[512,1024]{1,0:T(8,128)(2,1)S(1)}, u32[]{:S(2)}, u32[]{:S(2)}) %collective-permute-start.8) | collective-permute-done | bytes 1048608 | tf_op jit(solution)/shard_map/ppermute | solution.py:345
  175.8 9.7 %collective-permute-done.10 = bf16[128,1024]{1,0:T(8,128)(2,1)S(1)} collective-permute-done((bf16[128,1024]{1,0:T(8,128)(2,1)S(1)}, bf16[128,1024]{1,0:T(8,128)(2,1)S(1)}, u32[]{:S(2)}, u32[]{:S(2)}) %collective-permute-start.10) | collective-permute-done | bytes 262176 | tf_op jit(solution)/shard_map/ppermute | solution.py:353
  185.5 11.2 %collective-permute-done.12 = bf16[128,1024]{1,0:T(8,128)(2,1)S(1)} collective-permute-done((bf16[128,1024]{1,0:T(8,128)(2,1)S(1)}, bf16[128,1024]{1,0:T(8,128)(2,1)S(1)}, u32[]{:S(2)}, u32[]{:S(2)}) %collective-permute-start.12) | collective-permute-done | bytes 262176 | tf_op jit(solution)/shard_map/ppermute | solution.py:353
  196.8 14.0 %shard_map.90 = (bf16[8192,512]{1,0:T(8,128)(2,1)}, bf16[512,1024]{1,0:T(8,128)(2,1)}) custom-call(bf16[256,8192]{1,0:T(8,128)(2,1)} %bitcast.6.x_ref, bf16[256,1152]{1,0:T(8,128)(2,1)} %bitcast.51, bf16[256,1152]{1,0:T(8,128)(2,1)} %bitcast.52, bf16[256,512]{1,0:T(8,128)(2,1)} %get-tuple-element.50.backward_ref, bf16[8192,512]{1,0:T(8,128)(2,1)} %down_ref.3), custom_call_target="tpu_custom_call" | custom-call | flops 4563402752 | bytes 23592960 | tf_op jit(solution)/shard_map/pallas_call | solution.py:188
  210.8 26.1 %all-to-all-done.2 = bf16[16,16,8192]{2,1,0:T(8,128)(2,1)} async-done(((bf16[16,16,8192]{2,1,0:T(8,128)(2,1)}), bf16[16,16,8192]{2,1,0:T(8,128)(2,1)}, u32[]{:S(2)}, u32[]{:S(2)}) %all-to-all-start.2) | async-done | bytes 4194336 | tf_op jit(solution)/shard_map/all_to_all | solution.py:383
  236.8 5.1 %shard_map.89 = bf16[128,8192]{1,0:T(8,128)(2,1)} custom-call(s32[2]{0:T(128)} %pad_add_fusion.at_ref, bf16[128,256]{1,0:T(8,128)(2,1)} %get-tuple-element.29.place_ref, bf16[256,8192]{1,0:T(8,128)(2,1)} %bitcast.11.rows_ref, bf16[8,128,1024]{2,1,0:T(8,128)(2,1)} %copy-done.1), custom_call_target="tpu_custom_call" | custom-call | flops 536870912 | bytes 8388608 | tf_op jit(solution)/shard_map/pallas_call | solution.py:266
  (56 shorter events, 18.7 us)
Async XLA Ops:
  4.1 22.4 %all-to-all-start = ((bf16[16,16,1152]{2,1,0:T(8,128)(2,1)}), bf16[16,16,1152]{2,1,0:T(8,128)(2,1)S(1)}, u32[]{:S(2)}, u32[]{:S(2)}) async-start(bf16[16,16,1152]{2,1,0:T(8,128)(2,1)} %bitcast.54), calls=%async_computation | async-start | bytes 1179648 | tf_op jit(solution)/shard_map/all_to_all | solution.py:364
  10.7 35.4 %collective-permute-start.4 = (bf16[256,1024]{1,0:T(8,128)(2,1)S(1)}, bf16[256,1024]{1,0:T(8,128)(2,1)S(1)}, u32[]{:S(2)}, u32[]{:S(2)}) collective-permute-start(bf16[256,1024]{1,0:T(8,128)(2,1)S(1)} %constant_dynamic-slice_fusion), channel_id=1, source_target_pairs={{0,4},{1,5},{2,6},{3,7},{4,8},{5,9},{6,10},{7,11},{8,12},{9,13},{1... | collective-permute-start | bytes 1572872 | tf_op jit(solution)/shard_map/ppermute | solution.py:334
  13.8 51.2 %collective-permute-start.5 = (bf16[256,1024]{1,0:T(8,128)(2,1)S(1)}, bf16[256,1024]{1,0:T(8,128)(2,1)S(1)}, u32[]{:S(2)}, u32[]{:S(2)}) collective-permute-start(bf16[256,1024]{1,0:T(8,128)(2,1)S(1)} %constant_dynamic-slice_fusion), channel_id=1, source_target_pairs={{4,0},{5,1},{6,2},{7,3},{8,4},{9,5},{10,6},{11,7},{12,8},{13,9},{1... | collective-permute-start | bytes 1572872 | tf_op jit(solution)/shard_map/ppermute | solution.py:334
  26.5 38.5 %collective-permute-start.6 = (bf16[256,1024]{1,0:T(8,128)(2,1)S(1)}, bf16[256,1024]{1,0:T(8,128)(2,1)}, u32[]{:S(2)}, u32[]{:S(2)}) collective-permute-start(bf16[256,1024]{1,0:T(8,128)(2,1)S(1)} %constant_dynamic-slice_fusion), channel_id=1, source_target_pairs={{0,8},{1,9},{2,10},{3,11},{12,4},{13,5},{14,6},{15,7},{16,24},{17,... | collective-permute-start | bytes 1572872 | tf_op jit(solution)/shard_map/ppermute | solution.py:338
  27.8 110.6 %all-to-all-start.1 = ((bf16[16,16,8192]{2,1,0:T(8,128)(2,1)}), bf16[16,16,8192]{2,1,0:T(8,128)(2,1)}, u32[]{:S(2)}, u32[]{:S(2)}) async-start(bf16[16,16,8192]{2,1,0:T(8,128)(2,1)} %bitcast.48), calls=%async_computation.1 | async-start | bytes 8388608 | tf_op jit(solution)/shard_map/all_to_all | solution.py:371
  46.1 19.7 %copy-start.4 = (bf16[256,1024]{1,0:T(8,128)(2,1)}, bf16[256,1024]{1,0:T(8,128)(2,1)S(1)}, u32[]{:S(2)}) copy-start(bf16[256,1024]{1,0:T(8,128)(2,1)S(1)} %collective-permute-done.4.below_ref) | copy-start | bytes 1572868
  65.8 3.8 %copy-start.3 = (bf16[128,1024]{1,0:T(8,128)(2,1)S(1)}, bf16[128,1024]{1,0:T(8,128)(2,1)}, u32[]{:S(2)}) copy-start(bf16[128,1024]{1,0:T(8,128)(2,1)} %dy_ref.1) | copy-start | bytes 786436
  68.2 54.3 %collective-permute-start.7 = (bf16[512,1024]{1,0:T(8,128)(2,1)}, bf16[512,1024]{1,0:T(8,128)(2,1)S(1)}, u32[]{:S(2)}, u32[]{:S(2)}) collective-permute-start(bf16[512,1024]{1,0:T(8,128)(2,1)} %shard_map.88), channel_id=1, source_target_pairs={{4,0},{5,1},{6,2},{7,3},{8,12},{9,13},{10,14},{11,15},{20,16},{21,... | collective-permute-start | bytes 3145736 | tf_op jit(solution)/shard_map/ppermute | solution.py:338
  69.6 6.6 %collective-permute-start = (bf16[128,1024]{1,0:T(8,128)(2,1)S(1)}, bf16[128,1024]{1,0:T(8,128)(2,1)S(1)}, u32[]{:S(2)}, u32[]{:S(2)}) collective-permute-start(bf16[128,1024]{1,0:T(8,128)(2,1)S(1)} %copy-done.3), channel_id=1, source_target_pairs={{0,16},{16,0},{1,17},{17,1},{2,18},{18,2},{3,19},{19,3},{4,20},{20... | collective-permute-start | bytes 786440 | tf_op jit(solution)/shard_map/ppermute | solution.py:345
  76.3 30.1 %collective-permute-start.1 = (bf16[2,128,1024]{2,1,0:T(8,128)(2,1)S(1)}, bf16[2,128,1024]{2,1,0:T(8,128)(2,1)S(1)}, u32[]{:S(2)}, u32[]{:S(2)}) collective-permute-start(bf16[2,128,1024]{2,1,0:T(8,128)(2,1)S(1)} %pad_maximum_fusion.1), channel_id=1, source_target_pairs={{0,3},{1,0},{2,1},{3,2},{4,7},{5,4},{6,5},{7,6},{8,11},{9,8},{10,9... | collective-permute-start | bytes 1572872 | tf_op jit(solution)/shard_map/ppermute | solution.py:353
  78.5 34.2 %collective-permute-start.2 = (bf16[2,128,1024]{2,1,0:T(8,128)(2,1)S(1)}, bf16[2,128,1024]{2,1,0:T(8,128)(2,1)}, u32[]{:S(2)}, u32[]{:S(2)}) collective-permute-start(bf16[2,128,1024]{2,1,0:T(8,128)(2,1)S(1)} %pad_maximum_fusion.1), channel_id=1, source_target_pairs={{0,2},{1,3},{2,0},{3,1},{4,6},{5,7},{6,4},{7,5},{8,10},{9,11},{10,... | collective-permute-start | bytes 1572872 | tf_op jit(solution)/shard_map/ppermute | solution.py:353
  84.2 38.2 %collective-permute-start.3 = (bf16[2,128,1024]{2,1,0:T(8,128)(2,1)S(1)}, bf16[2,128,1024]{2,1,0:T(8,128)(2,1)}, u32[]{:S(2)}, u32[]{:S(2)}) collective-permute-start(bf16[2,128,1024]{2,1,0:T(8,128)(2,1)S(1)} %pad_maximum_fusion.1), channel_id=1, source_target_pairs={{0,1},{1,2},{2,3},{3,0},{4,5},{5,6},{6,7},{7,4},{8,9},{9,10},{10,1... | collective-permute-start | bytes 1572872 | tf_op jit(solution)/shard_map/ppermute | solution.py:353
  106.3 16.1 %copy-start.8 = (bf16[2,128,1024]{2,1,0:T(8,128)(2,1)}, bf16[2,128,1024]{2,1,0:T(8,128)(2,1)S(1)}, u32[]{:S(2)}) copy-start(bf16[2,128,1024]{2,1,0:T(8,128)(2,1)S(1)} %collective-permute-done.1) | copy-start | bytes 1572868
  138.4 98.4 %all-to-all-start.2 = ((bf16[16,16,8192]{2,1,0:T(8,128)(2,1)}), bf16[16,16,8192]{2,1,0:T(8,128)(2,1)}, u32[]{:S(2)}, u32[]{:S(2)}) async-start(bf16[16,16,8192]{2,1,0:T(8,128)(2,1)} %bitcast.49), calls=%async_computation.2 | async-start | bytes 8388608 | tf_op jit(solution)/shard_map/all_to_all | solution.py:383
  144.3 1.5 copy-start.5
  144.3 1.7 copy-start.7
  148.5 24.4 %collective-permute-start.8 = (bf16[512,1024]{1,0:T(8,128)(2,1)S(1)}, bf16[512,1024]{1,0:T(8,128)(2,1)S(1)}, u32[]{:S(2)}, u32[]{:S(2)}) collective-permute-start(bf16[512,1024]{1,0:T(8,128)(2,1)S(1)} %convolution_convert_fusion), channel_id=1, source_target_pairs={{0,16},{16,0},{1,17},{17,1},{2,18},{18,2},{3,19},{19,3},{4,20},{20... | collective-permute-start | bytes 3145736 | tf_op jit(solution)/shard_map/ppermute | solution.py:345
  150.9 24.8 %collective-permute-start.9 = (bf16[128,1024]{1,0:T(8,128)(2,1)S(1)}, bf16[128,1024]{1,0:T(8,128)(2,1)S(1)}, u32[]{:S(2)}, u32[]{:S(2)}) collective-permute-start(bf16[128,1024]{1,0:T(8,128)(2,1)S(1)} %get-tuple-element.62), channel_id=1, source_target_pairs={{0,1},{1,2},{2,3},{3,0},{4,5},{5,6},{6,7},{7,4},{8,9},{9,10},{10,1... | collective-permute-start | bytes 786440 | tf_op jit(solution)/shard_map/ppermute | solution.py:353
  151.7 33.7 %collective-permute-start.11 = (bf16[128,1024]{1,0:T(8,128)(2,1)S(1)}, bf16[128,1024]{1,0:T(8,128)(2,1)S(1)}, u32[]{:S(2)}, u32[]{:S(2)}) collective-permute-start(bf16[128,1024]{1,0:T(8,128)(2,1)S(1)} %get-tuple-element.61), channel_id=1, source_target_pairs={{0,2},{1,3},{2,0},{3,1},{4,6},{5,7},{6,4},{7,5},{8,10},{9,11},{10,... | collective-permute-start | bytes 786440 | tf_op jit(solution)/shard_map/ppermute | solution.py:353
  152.9 43.8 %collective-permute-start.13 = (bf16[128,1024]{1,0:T(8,128)(2,1)S(1)}, bf16[128,1024]{1,0:T(8,128)(2,1)S(1)}, u32[]{:S(2)}, u32[]{:S(2)}) collective-permute-start(bf16[128,1024]{1,0:T(8,128)(2,1)S(1)} %get-tuple-element.60), channel_id=1, source_target_pairs={{0,3},{1,0},{2,1},{3,2},{4,7},{5,4},{6,5},{7,6},{8,11},{9,8},{10,9... | collective-permute-start | bytes 786440 | tf_op jit(solution)/shard_map/ppermute | solution.py:353
  173.0 12.4 %collective-permute-start.10 = (bf16[128,1024]{1,0:T(8,128)(2,1)S(1)}, bf16[128,1024]{1,0:T(8,128)(2,1)S(1)}, u32[]{:S(2)}, u32[]{:S(2)}) collective-permute-start(bf16[128,1024]{1,0:T(8,128)(2,1)S(1)} %get-tuple-element.59), channel_id=1, source_target_pairs={{0,1},{1,2},{2,3},{3,0},{4,5},{5,6},{6,7},{7,4},{8,9},{9,10},{10,1... | collective-permute-start | bytes 786440 | tf_op jit(solution)/shard_map/ppermute | solution.py:353
  174.4 22.2 %collective-permute-start.12 = (bf16[128,1024]{1,0:T(8,128)(2,1)S(1)}, bf16[128,1024]{1,0:T(8,128)(2,1)S(1)}, u32[]{:S(2)}, u32[]{:S(2)}) collective-permute-start(bf16[128,1024]{1,0:T(8,128)(2,1)S(1)} %get-tuple-element.58), channel_id=1, source_target_pairs={{0,2},{1,3},{2,0},{3,1},{4,6},{5,7},{6,4},{7,5},{8,10},{9,11},{10,... | collective-permute-start | bytes 786440 | tf_op jit(solution)/shard_map/ppermute | solution.py:353
  175.7 21.0 %collective-permute-start.14 = (bf16[128,1024]{1,0:T(8,128)(2,1)S(1)}, bf16[128,1024]{1,0:T(8,128)(2,1)S(1)}, u32[]{:S(2)}, u32[]{:S(2)}) collective-permute-start(bf16[128,1024]{1,0:T(8,128)(2,1)S(1)} %get-tuple-element.57), channel_id=1, source_target_pairs={{0,3},{1,0},{2,1},{3,2},{4,7},{5,4},{6,5},{7,6},{8,11},{9,8},{10,9... | collective-permute-start | bytes 786440 | tf_op jit(solution)/shard_map/ppermute | solution.py:353
  196.7 14.0 %copy-start.1 = (bf16[8,128,1024]{2,1,0:T(8,128)(2,1)}, bf16[8,128,1024]{2,1,0:T(8,128)(2,1)S(1)}, u32[]{:S(2)}) copy-start(bf16[8,128,1024]{2,1,0:T(8,128)(2,1)S(1)} %bitcast_dynamic-update-slice_fusion.base_ref) | copy-start | bytes 6291460
  (4 other events, 4.7 us)

commit v5 on v4

--- a/solution.py
+++ b/solution.py
@@ -204,7 +204,7 @@
             jax.ShapeDtypeStruct((columns, features), jnp.bfloat16),
         ],
         scratch_shapes=[pltpu.VMEM((token_slots, columns), jnp.float32)],
-        compiler_params=pltpu.CompilerParams(vmem_limit_bytes=VMEM),
+        compiler_params=pltpu.CompilerParams(vmem_limit_bytes=VMEM // 2),
         cost_estimate=pl.CostEstimate(
             flops=2 * token_slots * columns * (2 * width + features),
             bytes_accessed=2 * (2 * columns + token_slots) * (width + features),
@@ -214,7 +214,7 @@
 
 
 def finish_kernel(
-    share, groups, at_ref, place_ref, rows_ref, base_ref, out_ref, rows, base, out, sems
+    share, groups, at_ref, place_ref, rows_ref, base, out_ref, rows, out, sems
 ):
     inner = PLANE // groups
     wide = PLANE * share
@@ -223,26 +223,18 @@
     loads, stores = [], []
     for step in range(steps):
         part = pl.ds(step * layers * wide, layers * wide)
-        side = pl.ds(step * layers * share, layers * share)
         loads.append(
-            (
-                pltpu.make_async_copy(base_ref.at[:, :, side], base.at[:, :, side], sems.at[step]),
-                pltpu.make_async_copy(
-                    rows_ref.at[:, part], rows.at[:, part], sems.at[steps + step]
-                ),
-            )
+            pltpu.make_async_copy(rows_ref.at[:, part], rows.at[:, part], sems.at[step])
         )
         stores.append(
             pltpu.make_async_copy(
-                out.at[:, part], out_ref.at[:, part], sems.at[2 * steps + step]
+                out.at[:, part], out_ref.at[:, part], sems.at[steps + step]
             )
         )
-    for pair in loads:
-        for copy in pair:
-            copy.start()
+    for copy in loads:
+        copy.start()
     for step in range(steps):
-        for copy in loads[step]:
-            copy.wait()
+        loads[step].wait()
         for layer in range(step * layers, (step + 1) * layers):
             for block in range(PLANE):
                 columns = pl.ds((layer * PLANE + block) * share, share)
@@ -269,17 +261,16 @@
             pl.BlockSpec(memory_space=pltpu.SMEM),
             pl.BlockSpec(memory_space=pltpu.VMEM),
             pl.BlockSpec(memory_space=pl.ANY),
-            pl.BlockSpec(memory_space=pl.ANY),
+            pl.BlockSpec(memory_space=pltpu.VMEM),
         ],
         out_specs=pl.BlockSpec(memory_space=pl.ANY),
         out_shape=jax.ShapeDtypeStruct((tok_rows, width), jnp.bfloat16),
         scratch_shapes=[
             pltpu.VMEM(rows.shape, jnp.bfloat16),
-            pltpu.VMEM(base.shape, jnp.bfloat16),
             pltpu.VMEM((tok_rows, width), jnp.bfloat16),
-            pltpu.SemaphoreType.DMA((3 * steps,)),
-        ],
-        compiler_params=pltpu.CompilerParams(vmem_limit_bytes=VMEM),
+            pltpu.SemaphoreType.DMA((2 * steps,)),
+        ],
+        compiler_params=pltpu.CompilerParams(vmem_limit_bytes=VMEM // 2),
         cost_estimate=pl.CostEstimate(
             flops=2 * tok_rows * token_slots * width,
             bytes_accessed=2 * width * (token_slots + 2 * tok_rows),

time: 243 us -> 242 us (level)
  Pallas kernels: 36.1 us -> 31.9 us
  waiting for transfers between devices: 154 us -> 158 us
    pallas_call x1, Pallas kernels: 14 us -> 11 us  [make_grads(): pl.pallas_call(grads_kernel, grid=(width // BLOCK,), in_specs=[pl.BlockSp...]
    all_to_all x1, waiting for transfers between devices: 26.1 us -> 29.1 us  [local(): lax.all_to_all(adapter_rows, 'adapter', split_axis=0, concat_axis=0, tile...]
  transfers between devices with their start and end apart: 18 -> 18, of which waited for: 12 -> 12; matrix products, arithmetic and copies ran while one was open for 3% -> 2% of each run, Pallas kernels for 12% -> 11%
where the time goes in v5:
time: 242 us; the launch traced here: 241 us
  waiting for transfers between devices  158 us (65%)
  starting transfers between devices  42.2 us (17%)
  Pallas kernels  31.9 us (13%)
  local copies, waits for them, and re-layouts  3.96 us (2%)
  matrix products  2.57 us (1%)
    ppermute x9, waiting for transfers between devices, around_plane(): return lax.ppermute(block, 'adapter', pairs)  51.6 us
    all_to_all x1, waiting for transfers between devices, local(): lax.all_to_all(adapter_rows, 'adapter', split_axis=0, concat_axis=0, tile...  29.1 us
    ppermute x2, waiting for transfers between devices, next_layer(): return lax.ppermute(block, 'adapter', pairs)  28.6 us
    ppermute x2, waiting for transfers between devices, around_groups(): return lax.ppermute(block, 'groups', pairs)  26.9 us
    all_to_all x1, waiting for transfers between devices, local(): lax.all_to_all(send_x, 'adapter', split_axis=0, concat_axis=0, tiled=True)  15.9 us
    ppermute x9, starting transfers between devices, around_plane(): return lax.ppermute(block, 'adapter', pairs)  12.7 us
    pallas_call x1, Pallas kernels, make_grads(): pl.pallas_call(grads_kernel, grid=(width // BLOCK,), in_specs=[pl.BlockSp...  11 us
    all_to_all x1, starting transfers between devices, local(): lax.all_to_all(send_x, 'adapter', split_axis=0, concat_axis=0, tiled=True)  8.53 us
  transfers between devices with their start and end apart: 18, of which 12 were waited for; matrix products, arithmetic and copies ran while one was open for 2% of the time, Pallas kernels for 11%

profile of v5, /device:TPU:15, one launch (start us, length us, event | category | flops | bytes accessed | tf_op | source)
XLA Modules:
  0.0 240.8 jit_solution(14756727703159986854)
XLA Ops:
  1.9 2.2 shard_map.85
  4.1 6.6 %all-to-all-start = ((bf16[16,16,1152]{2,1,0:T(8,128)(2,1)}), bf16[16,16,1152]{2,1,0:T(8,128)(2,1)S(1)}, u32[]{:S(2)}, u32[]{:S(2)}) async-start(bf16[16,16,1152]{2,1,0:T(8,128)(2,1)} %bitcast.56), calls=%async_computation | async-start | bytes 1179648 | tf_op jit(solution)/shard_map/all_to_all | solution.py:355
  10.7 3.1 %collective-permute-start.4 = (bf16[256,1024]{1,0:T(8,128)(2,1)S(1)}, bf16[256,1024]{1,0:T(8,128)(2,1)S(1)}, u32[]{:S(2)}, u32[]{:S(2)}) collective-permute-start(bf16[256,1024]{1,0:T(8,128)(2,1)S(1)} %constant_dynamic-slice_fusion), channel_id=1, source_target_pairs={{0,4},{1,5},{2,6},{3,7},{4,8},{5,9},{6,10},{7,11},{8,12},{9,13},{1... | collective-permute-start | bytes 1572872 | tf_op jit(solution)/shard_map/ppermute | solution.py:325
  13.8 2.2 collective-permute-start.5
  16.0 4.9 %shard_map.86 = bf16[256,8192]{1,0:T(8,128)(2,1)} custom-call(bf16[256,128]{1,0:T(8,128)(2,1)} %get-tuple-element.32.place_ref, bf16[128,8192]{1,0:T(8,128)(2,1)} %x_ref.1), custom_call_target="tpu_custom_call" | custom-call | flops 536870912 | bytes 6291456 | tf_op jit(solution)/shard_map/pallas_call | solution.py:70
  20.9 5.6 %all-to-all-done = bf16[16,16,1152]{2,1,0:T(8,128)(2,1)S(1)} async-done(((bf16[16,16,1152]{2,1,0:T(8,128)(2,1)}), bf16[16,16,1152]{2,1,0:T(8,128)(2,1)S(1)}, u32[]{:S(2)}, u32[]{:S(2)}) %all-to-all-start) | async-done | bytes 589856 | tf_op jit(solution)/shard_map/all_to_all | solution.py:355
  27.8 8.5 %all-to-all-start.1 = ((bf16[16,16,8192]{2,1,0:T(8,128)(2,1)}), bf16[16,16,8192]{2,1,0:T(8,128)(2,1)}, u32[]{:S(2)}, u32[]{:S(2)}) async-start(bf16[16,16,8192]{2,1,0:T(8,128)(2,1)} %bitcast.53), calls=%async_computation.1 | async-start | bytes 8388608 | tf_op jit(solution)/shard_map/all_to_all | solution.py:362
  36.4 9.7 %collective-permute-done.4.below_ref = bf16[256,1024]{1,0:T(8,128)(2,1)S(1)} collective-permute-done((bf16[256,1024]{1,0:T(8,128)(2,1)S(1)}, bf16[256,1024]{1,0:T(8,128)(2,1)S(1)}, u32[]{:S(2)}, u32[]{:S(2)}) %collective-permute-start.4) | collective-permute-done | bytes 524320 | tf_op jit(solution)/shard_map/ppermute | solution.py:325
  46.1 18.9 %collective-permute-done.5.above_ref = bf16[256,1024]{1,0:T(8,128)(2,1)S(1)} collective-permute-done((bf16[256,1024]{1,0:T(8,128)(2,1)S(1)}, bf16[256,1024]{1,0:T(8,128)(2,1)S(1)}, u32[]{:S(2)}, u32[]{:S(2)}) %collective-permute-start.5) | collective-permute-done | bytes 524320 | tf_op jit(solution)/shard_map/ppermute | solution.py:325
  65.8 2.4 %shard_map.88 = bf16[512,1024]{1,0:T(8,128)(2,1)} custom-call(s32[1]{0:T(128)} %bitcast.9.layer_ref, bf16[256,1024]{1,0:T(8,128)(2,1)} %copy-done.6, bf16[256,1024]{1,0:T(8,128)(2,1)} %copy-done.8, bf16[256,1024]{1,0:T(8,128)(2,1)} %collective-permute-done.6.over_ref), custom_call_target="tpu_custom_call" | custom-call | flops 99999997952 | bytes 2621440 | tf_op jit(solution)/shard_map/pallas_call | solution.py:299
  69.9 6.3 %collective-permute-done = bf16[128,1024]{1,0:T(8,128)(2,1)S(1)} collective-permute-done((bf16[128,1024]{1,0:T(8,128)(2,1)S(1)}, bf16[128,1024]{1,0:T(8,128)(2,1)S(1)}, u32[]{:S(2)}, u32[]{:S(2)}) %collective-permute-start) | collective-permute-done | bytes 262176 | tf_op jit(solution)/shard_map/ppermute | solution.py:336
  78.5 5.8 %collective-permute-start.2 = (bf16[2,128,1024]{2,1,0:T(8,128)(2,1)S(1)}, bf16[2,128,1024]{2,1,0:T(8,128)(2,1)}, u32[]{:S(2)}, u32[]{:S(2)}) collective-permute-start(bf16[2,128,1024]{2,1,0:T(8,128)(2,1)S(1)} %pad_maximum_fusion.1), channel_id=1, source_target_pairs={{0,2},{1,3},{2,0},{3,1},{4,6},{5,7},{6,4},{7,5},{8,10},{9,11},{10,... | collective-permute-start | bytes 1572872 | tf_op jit(solution)/shard_map/ppermute | solution.py:344
  84.3 7.4 %shard_map.87 = (bf16[256,8192]{1,0:T(8,128)(2,1)}, bf16[256,512]{1,0:T(8,128)(2,1)}) custom-call(bf16[256,1152]{1,0:T(8,128)(2,1)} %bitcast.50, bf16[512,1024]{1,0:T(8,128)(2,1)} %up_ref.1, bf16[8192,512]{1,0:T(8,128)(2,1)} %down_ref.3), custom_call_target="tpu_custom_call" | custom-call | flops 2415919104 | bytes 14155776 | tf_op jit(solution)/shard_map/pallas_call | solution.py:137
  91.7 14.7 %collective-permute-done.1 = bf16[2,128,1024]{2,1,0:T(8,128)(2,1)S(1)} collective-permute-done((bf16[2,128,1024]{2,1,0:T(8,128)(2,1)S(1)}, bf16[2,128,1024]{2,1,0:T(8,128)(2,1)S(1)}, u32[]{:S(2)}, u32[]{:S(2)}) %collective-permute-start.1) | collective-permute-done | bytes 524320 | tf_op jit(solution)/shard_map/ppermute | solution.py:344
  106.3 6.4 %collective-permute-done.2 = bf16[2,128,1024]{2,1,0:T(8,128)(2,1)} collective-permute-done((bf16[2,128,1024]{2,1,0:T(8,128)(2,1)S(1)}, bf16[2,128,1024]{2,1,0:T(8,128)(2,1)}, u32[]{:S(2)}, u32[]{:S(2)}) %collective-permute-start.2) | collective-permute-done | bytes 524320 | tf_op jit(solution)/shard_map/ppermute | solution.py:344
  112.7 9.8 %collective-permute-done.3 = bf16[2,128,1024]{2,1,0:T(8,128)(2,1)} collective-permute-done((bf16[2,128,1024]{2,1,0:T(8,128)(2,1)S(1)}, bf16[2,128,1024]{2,1,0:T(8,128)(2,1)}, u32[]{:S(2)}, u32[]{:S(2)}) %collective-permute-start.3) | collective-permute-done | bytes 524320 | tf_op jit(solution)/shard_map/ppermute | solution.py:344
  122.5 15.9 %all-to-all-done.1 = bf16[16,16,8192]{2,1,0:T(8,128)(2,1)} async-done(((bf16[16,16,8192]{2,1,0:T(8,128)(2,1)}), bf16[16,16,8192]{2,1,0:T(8,128)(2,1)}, u32[]{:S(2)}, u32[]{:S(2)}) %all-to-all-start.1) | async-done | bytes 4194336 | tf_op jit(solution)/shard_map/all_to_all | solution.py:362
  138.4 5.9 %all-to-all-start.2 = ((bf16[16,16,8192]{2,1,0:T(8,128)(2,1)}), bf16[16,16,8192]{2,1,0:T(8,128)(2,1)}, u32[]{:S(2)}, u32[]{:S(2)}) async-start(bf16[16,16,8192]{2,1,0:T(8,128)(2,1)} %bitcast.54), calls=%async_computation.2 | async-start | bytes 8388608 | tf_op jit(solution)/shard_map/all_to_all | solution.py:374
  152.4 20.6 %collective-permute-done.8 = bf16[512,1024]{1,0:T(8,128)(2,1)S(1)} collective-permute-done((bf16[512,1024]{1,0:T(8,128)(2,1)S(1)}, bf16[512,1024]{1,0:T(8,128)(2,1)S(1)}, u32[]{:S(2)}, u32[]{:S(2)}) %collective-permute-start.8) | collective-permute-done | bytes 1048608 | tf_op jit(solution)/shard_map/ppermute | solution.py:336
  175.8 9.6 %collective-permute-done.10 = bf16[128,1024]{1,0:T(8,128)(2,1)S(1)} collective-permute-done((bf16[128,1024]{1,0:T(8,128)(2,1)S(1)}, bf16[128,1024]{1,0:T(8,128)(2,1)S(1)}, u32[]{:S(2)}, u32[]{:S(2)}) %collective-permute-start.10) | collective-permute-done | bytes 262176 | tf_op jit(solution)/shard_map/ppermute | solution.py:344
  185.5 11.2 %collective-permute-done.12 = bf16[128,1024]{1,0:T(8,128)(2,1)S(1)} collective-permute-done((bf16[128,1024]{1,0:T(8,128)(2,1)S(1)}, bf16[128,1024]{1,0:T(8,128)(2,1)S(1)}, u32[]{:S(2)}, u32[]{:S(2)}) %collective-permute-start.12) | collective-permute-done | bytes 262176 | tf_op jit(solution)/shard_map/ppermute | solution.py:344
  196.8 11.0 %shard_map.90 = (bf16[8192,512]{1,0:T(8,128)(2,1)}, bf16[512,1024]{1,0:T(8,128)(2,1)}) custom-call(bf16[256,8192]{1,0:T(8,128)(2,1)} %bitcast.6.x_ref, bf16[256,1152]{1,0:T(8,128)(2,1)S(1)} %bitcast.51, bf16[256,1152]{1,0:T(8,128)(2,1)S(1)} %bitcast.52, bf16[256,512]{1,0:T(8,128)(2,1)S(1)} %copy-done.4, bf16[8192,512]{1,0:T(8,128)(2,1)S(1)} %bitcast.49), custom_call_target="tpu_custom_call" | custom-call | flops 4563402752 | bytes 23592960 | tf_op jit(solution)/shard_map/pallas_call | solution.py:188
  207.8 29.1 %all-to-all-done.2 = bf16[16,16,8192]{2,1,0:T(8,128)(2,1)} async-done(((bf16[16,16,8192]{2,1,0:T(8,128)(2,1)}), bf16[16,16,8192]{2,1,0:T(8,128)(2,1)}, u32[]{:S(2)}, u32[]{:S(2)}) %all-to-all-start.2) | async-done | bytes 4194336 | tf_op jit(solution)/shard_map/all_to_all | solution.py:374
  236.9 4.0 %shard_map.89 = bf16[128,8192]{1,0:T(8,128)(2,1)} custom-call(s32[2]{0:T(128)S(1)} %pad_add_fusion.at_ref, bf16[128,256]{1,0:T(8,128)(2,1)S(1)} %copy-done.3, bf16[256,8192]{1,0:T(8,128)(2,1)} %bitcast.11.rows_ref, bf16[8,128,1024]{2,1,0:T(8,128)(2,1)S(1)} %bitcast_dynamic-update-slice_fusion.base), custom_call_target="tpu_custom_call" | custom-call | flops 536870912 | bytes 8388608 | tf_op jit(solution)/shard_map/pallas_call | solution.py:258
  (65 shorter events, 18.1 us)
Async XLA Ops:
  4.1 22.4 %all-to-all-start = ((bf16[16,16,1152]{2,1,0:T(8,128)(2,1)}), bf16[16,16,1152]{2,1,0:T(8,128)(2,1)S(1)}, u32[]{:S(2)}, u32[]{:S(2)}) async-start(bf16[16,16,1152]{2,1,0:T(8,128)(2,1)} %bitcast.56), calls=%async_computation | async-start | bytes 1179648 | tf_op jit(solution)/shard_map/all_to_all | solution.py:355
  10.7 35.4 %collective-permute-start.4 = (bf16[256,1024]{1,0:T(8,128)(2,1)S(1)}, bf16[256,1024]{1,0:T(8,128)(2,1)S(1)}, u32[]{:S(2)}, u32[]{:S(2)}) collective-permute-start(bf16[256,1024]{1,0:T(8,128)(2,1)S(1)} %constant_dynamic-slice_fusion), channel_id=1, source_target_pairs={{0,4},{1,5},{2,6},{3,7},{4,8},{5,9},{6,10},{7,11},{8,12},{9,13},{1... | collective-permute-start | bytes 1572872 | tf_op jit(solution)/shard_map/ppermute | solution.py:325
  13.8 51.2 %collective-permute-start.5 = (bf16[256,1024]{1,0:T(8,128)(2,1)S(1)}, bf16[256,1024]{1,0:T(8,128)(2,1)S(1)}, u32[]{:S(2)}, u32[]{:S(2)}) collective-permute-start(bf16[256,1024]{1,0:T(8,128)(2,1)S(1)} %constant_dynamic-slice_fusion), channel_id=1, source_target_pairs={{4,0},{5,1},{6,2},{7,3},{8,4},{9,5},{10,6},{11,7},{12,8},{13,9},{1... | collective-permute-start | bytes 1572872 | tf_op jit(solution)/shard_map/ppermute | solution.py:325
  26.5 38.5 %collective-permute-start.6 = (bf16[256,1024]{1,0:T(8,128)(2,1)S(1)}, bf16[256,1024]{1,0:T(8,128)(2,1)}, u32[]{:S(2)}, u32[]{:S(2)}) collective-permute-start(bf16[256,1024]{1,0:T(8,128)(2,1)S(1)} %constant_dynamic-slice_fusion), channel_id=1, source_target_pairs={{0,8},{1,9},{2,10},{3,11},{12,4},{13,5},{14,6},{15,7},{16,24},{17,... | collective-permute-start | bytes 1572872 | tf_op jit(solution)/shard_map/ppermute | solution.py:329
  27.8 110.6 %all-to-all-start.1 = ((bf16[16,16,8192]{2,1,0:T(8,128)(2,1)}), bf16[16,16,8192]{2,1,0:T(8,128)(2,1)}, u32[]{:S(2)}, u32[]{:S(2)}) async-start(bf16[16,16,8192]{2,1,0:T(8,128)(2,1)} %bitcast.53), calls=%async_computation.1 | async-start | bytes 8388608 | tf_op jit(solution)/shard_map/all_to_all | solution.py:362
  46.1 19.7 %copy-start.6 = (bf16[256,1024]{1,0:T(8,128)(2,1)}, bf16[256,1024]{1,0:T(8,128)(2,1)S(1)}, u32[]{:S(2)}) copy-start(bf16[256,1024]{1,0:T(8,128)(2,1)S(1)} %collective-permute-done.4.below_ref) | copy-start | bytes 1572868
  68.2 54.3 %collective-permute-start.7 = (bf16[512,1024]{1,0:T(8,128)(2,1)}, bf16[512,1024]{1,0:T(8,128)(2,1)S(1)}, u32[]{:S(2)}, u32[]{:S(2)}) collective-permute-start(bf16[512,1024]{1,0:T(8,128)(2,1)} %shard_map.88), channel_id=1, source_target_pairs={{4,0},{5,1},{6,2},{7,3},{8,12},{9,13},{10,14},{11,15},{20,16},{21,... | collective-permute-start | bytes 3145736 | tf_op jit(solution)/shard_map/ppermute | solution.py:329
  69.6 6.6 %collective-permute-start = (bf16[128,1024]{1,0:T(8,128)(2,1)S(1)}, bf16[128,1024]{1,0:T(8,128)(2,1)S(1)}, u32[]{:S(2)}, u32[]{:S(2)}) collective-permute-start(bf16[128,1024]{1,0:T(8,128)(2,1)S(1)} %copy-done.5), channel_id=1, source_target_pairs={{0,16},{16,0},{1,17},{17,1},{2,18},{18,2},{3,19},{19,3},{4,20},{20... | collective-permute-start | bytes 786440 | tf_op jit(solution)/shard_map/ppermute | solution.py:336
  76.3 30.1 %collective-permute-start.1 = (bf16[2,128,1024]{2,1,0:T(8,128)(2,1)S(1)}, bf16[2,128,1024]{2,1,0:T(8,128)(2,1)S(1)}, u32[]{:S(2)}, u32[]{:S(2)}) collective-permute-start(bf16[2,128,1024]{2,1,0:T(8,128)(2,1)S(1)} %pad_maximum_fusion.1), channel_id=1, source_target_pairs={{0,3},{1,0},{2,1},{3,2},{4,7},{5,4},{6,5},{7,6},{8,11},{9,8},{10,9... | collective-permute-start | bytes 1572872 | tf_op jit(solution)/shard_map/ppermute | solution.py:344
  78.5 34.2 %collective-permute-start.2 = (bf16[2,128,1024]{2,1,0:T(8,128)(2,1)S(1)}, bf16[2,128,1024]{2,1,0:T(8,128)(2,1)}, u32[]{:S(2)}, u32[]{:S(2)}) collective-permute-start(bf16[2,128,1024]{2,1,0:T(8,128)(2,1)S(1)} %pad_maximum_fusion.1), channel_id=1, source_target_pairs={{0,2},{1,3},{2,0},{3,1},{4,6},{5,7},{6,4},{7,5},{8,10},{9,11},{10,... | collective-permute-start | bytes 1572872 | tf_op jit(solution)/shard_map/ppermute | solution.py:344
  84.3 38.2 %collective-permute-start.3 = (bf16[2,128,1024]{2,1,0:T(8,128)(2,1)S(1)}, bf16[2,128,1024]{2,1,0:T(8,128)(2,1)}, u32[]{:S(2)}, u32[]{:S(2)}) collective-permute-start(bf16[2,128,1024]{2,1,0:T(8,128)(2,1)S(1)} %pad_maximum_fusion.1), channel_id=1, source_target_pairs={{0,1},{1,2},{2,3},{3,0},{4,5},{5,6},{6,7},{7,4},{8,9},{9,10},{10,1... | collective-permute-start | bytes 1572872 | tf_op jit(solution)/shard_map/ppermute | solution.py:344
  138.4 98.4 %all-to-all-start.2 = ((bf16[16,16,8192]{2,1,0:T(8,128)(2,1)}), bf16[16,16,8192]{2,1,0:T(8,128)(2,1)}, u32[]{:S(2)}, u32[]{:S(2)}) async-start(bf16[16,16,8192]{2,1,0:T(8,128)(2,1)} %bitcast.54), calls=%async_computation.2 | async-start | bytes 8388608 | tf_op jit(solution)/shard_map/all_to_all | solution.py:374
  148.5 24.4 %collective-permute-start.8 = (bf16[512,1024]{1,0:T(8,128)(2,1)S(1)}, bf16[512,1024]{1,0:T(8,128)(2,1)S(1)}, u32[]{:S(2)}, u32[]{:S(2)}) collective-permute-start(bf16[512,1024]{1,0:T(8,128)(2,1)S(1)} %convolution_convert_fusion), channel_id=1, source_target_pairs={{0,16},{16,0},{1,17},{17,1},{2,18},{18,2},{3,19},{19,3},{4,20},{20... | collective-permute-start | bytes 3145736 | tf_op jit(solution)/shard_map/ppermute | solution.py:336
  148.9 47.8 %slice-start = ((s8[8388608]{0:T(1024)(128)(4,1)}), s8[4194304]{0:T(1024)(128)(4,1)S(1)}, s32[]{:S(2)}) async-start(s8[8388608]{0:T(1024)(128)(4,1)} %bitcast.48), calls=%async_computation.3 | async-start | bytes 8388608
  148.9 47.8 %slice-start.1 = ((s8[8388608]{0:T(1024)(128)(4,1)}), s8[4194304]{0:T(1024)(128)(4,1)S(1)}, s32[]{:S(2)}) async-start(s8[8388608]{0:T(1024)(128)(4,1)} %bitcast.48), calls=%async_computation.4 | async-start | bytes 8388608
  150.3 25.4 %collective-permute-start.9 = (bf16[128,1024]{1,0:T(8,128)(2,1)S(1)}, bf16[128,1024]{1,0:T(8,128)(2,1)S(1)}, u32[]{:S(2)}, u32[]{:S(2)}) collective-permute-start(bf16[128,1024]{1,0:T(8,128)(2,1)S(1)} %get-tuple-element.62), channel_id=1, source_target_pairs={{0,1},{1,2},{2,3},{3,0},{4,5},{5,6},{6,7},{7,4},{8,9},{9,10},{10,1... | collective-permute-start | bytes 786440 | tf_op jit(solution)/shard_map/ppermute | solution.py:344
  151.1 34.3 %collective-permute-start.11 = (bf16[128,1024]{1,0:T(8,128)(2,1)S(1)}, bf16[128,1024]{1,0:T(8,128)(2,1)S(1)}, u32[]{:S(2)}, u32[]{:S(2)}) collective-permute-start(bf16[128,1024]{1,0:T(8,128)(2,1)S(1)} %get-tuple-element.61), channel_id=1, source_target_pairs={{0,2},{1,3},{2,0},{3,1},{4,6},{5,7},{6,4},{7,5},{8,10},{9,11},{10,... | collective-permute-start | bytes 786440 | tf_op jit(solution)/shard_map/ppermute | solution.py:344
  152.3 44.3 %collective-permute-start.13 = (bf16[128,1024]{1,0:T(8,128)(2,1)S(1)}, bf16[128,1024]{1,0:T(8,128)(2,1)S(1)}, u32[]{:S(2)}, u32[]{:S(2)}) collective-permute-start(bf16[128,1024]{1,0:T(8,128)(2,1)S(1)} %get-tuple-element.60), channel_id=1, source_target_pairs={{0,3},{1,0},{2,1},{3,2},{4,7},{5,4},{6,5},{7,6},{8,11},{9,8},{10,9... | collective-permute-start | bytes 786440 | tf_op jit(solution)/shard_map/ppermute | solution.py:344
  173.0 23.7 %copy-start.2 = (bf16[16,16,1152]{2,1,0:T(8,128)(2,1)S(1)}, bf16[16,16,1152]{2,1,0:T(8,128)(2,1)}, u32[]{:S(2)}) copy-start(bf16[16,16,1152]{2,1,0:T(8,128)(2,1)} %copy-done.1) | copy-start | bytes 1769476
  173.1 23.7 %copy-start.4 = (bf16[256,512]{1,0:T(8,128)(2,1)S(1)}, bf16[256,512]{1,0:T(8,128)(2,1)}, u32[]{:S(2)}) copy-start(bf16[256,512]{1,0:T(8,128)(2,1)} %get-tuple-element.50.backward_ref) | copy-start | bytes 786436
  173.1 12.4 %collective-permute-start.10 = (bf16[128,1024]{1,0:T(8,128)(2,1)S(1)}, bf16[128,1024]{1,0:T(8,128)(2,1)S(1)}, u32[]{:S(2)}, u32[]{:S(2)}) collective-permute-start(bf16[128,1024]{1,0:T(8,128)(2,1)S(1)} %get-tuple-element.59), channel_id=1, source_target_pairs={{0,1},{1,2},{2,3},{3,0},{4,5},{5,6},{6,7},{7,4},{8,9},{9,10},{10,1... | collective-permute-start | bytes 786440 | tf_op jit(solution)/shard_map/ppermute | solution.py:344
  174.5 22.2 %collective-permute-start.12 = (bf16[128,1024]{1,0:T(8,128)(2,1)S(1)}, bf16[128,1024]{1,0:T(8,128)(2,1)S(1)}, u32[]{:S(2)}, u32[]{:S(2)}) collective-permute-start(bf16[128,1024]{1,0:T(8,128)(2,1)S(1)} %get-tuple-element.58), channel_id=1, source_target_pairs={{0,2},{1,3},{2,0},{3,1},{4,6},{5,7},{6,4},{7,5},{8,10},{9,11},{10,... | collective-permute-start | bytes 786440 | tf_op jit(solution)/shard_map/ppermute | solution.py:344
  175.7 21.0 %collective-permute-start.14 = (bf16[128,1024]{1,0:T(8,128)(2,1)S(1)}, bf16[128,1024]{1,0:T(8,128)(2,1)S(1)}, u32[]{:S(2)}, u32[]{:S(2)}) collective-permute-start(bf16[128,1024]{1,0:T(8,128)(2,1)S(1)} %get-tuple-element.57), channel_id=1, source_target_pairs={{0,3},{1,0},{2,1},{3,2},{4,7},{5,4},{6,5},{7,6},{8,11},{9,8},{10,9... | collective-permute-start | bytes 786440 | tf_op jit(solution)/shard_map/ppermute | solution.py:344
  196.8 40.1 %copy-start.3 = (bf16[128,256]{1,0:T(8,128)(2,1)S(1)}, bf16[128,256]{1,0:T(8,128)(2,1)}, u32[]{:S(2)}) copy-start(bf16[128,256]{1,0:T(8,128)(2,1)} %get-tuple-element.29.place_ref) | copy-start | bytes 196612
  (8 other events, 27.9 us)

commit v6 on v5

--- a/solution.py
+++ b/solution.py
@@ -13,7 +13,7 @@
 LANES = 128
 BLOCK = 1024
 VMEM = 60 << 20
-PAIR_FLOPS = 100_000_000_000
+EARLY_FLOPS = 100_000_000_000
 
 
 SCALE = 2.0
@@ -63,18 +63,18 @@
     out_ref[...] = dot(place_ref[...], x_ref[...], ((1,), (0,))).astype(jnp.bfloat16)
 
 
-def pack_x(place, activations):
+def pack_x(place, activations, columns):
     token_slots, tok_rows = place.shape
-    width = activations.shape[1]
-    columns = 2 * BLOCK
+    width = activations.shape[1] if columns is None else columns
+    step = width // 2
     return pl.pallas_call(
         pack_x_kernel,
-        grid=(width // columns,),
+        grid=(2,),
         in_specs=[
             pl.BlockSpec((token_slots, tok_rows), lambda j: (0, 0)),
-            pl.BlockSpec((tok_rows, columns), lambda j: (0, j)),
-        ],
-        out_specs=pl.BlockSpec((token_slots, columns), lambda j: (0, j)),
+            pl.BlockSpec((tok_rows, step), lambda j: (0, j)),
+        ],
+        out_specs=pl.BlockSpec((token_slots, step), lambda j: (0, j)),
         out_shape=jax.ShapeDtypeStruct((token_slots, width), jnp.bfloat16),
         compiler_params=pltpu.CompilerParams(vmem_limit_bytes=VMEM),
         cost_estimate=pl.CostEstimate(
@@ -162,15 +162,19 @@
     )(received, adapter_up, adapter_down)
 
 
-def grads_kernel(x_ref, dy_ref, family_ref, backward_ref, down_ref, grad_down_ref, grad_up_ref, low_ref):
+def grads_kernel(pieces, *refs):
+    dy_ref, family_ref, backward_ref, down_ref, grad_down_ref, grad_up_ref, low_ref = refs[pieces:]
     step = pl.program_id(0)
+    x = refs[0][...]
+    if pieces == 2:
+        x = jnp.where(step < pl.num_programs(0) - 1, x, refs[1][...])
 
     @pl.when(step == 0)
     def _():
         low_ref[...] = jnp.zeros_like(low_ref)
 
-    low_ref[...] += dot(x_ref[...], down_ref[...], ((1,), (0,)))
-    grad_down = dot(x_ref[...], backward_ref[...], ((0,), (0,)))
+    low_ref[...] += dot(x, down_ref[...], ((1,), (0,)))
+    grad_down = dot(x, backward_ref[...], ((0,), (0,)))
     grad_down_ref[...] = (SCALE * grad_down).astype(jnp.bfloat16)
 
     @pl.when(step == pl.num_programs(0) - 1)
@@ -181,15 +185,17 @@
         grad_up_ref[...] = (SCALE * grad_up).astype(jnp.bfloat16)
 
 
-def make_grads(received_input, received, backward_rows, adapter_up, adapter_down):
+def make_grads(xs, received, backward_rows, adapter_up, adapter_down):
     token_slots = received.shape[0]
     columns, features = adapter_up.shape
     width = adapter_down.shape[0]
-    return pl.pallas_call(
-        grads_kernel,
+    blocks = xs[0].shape[1] // BLOCK
+    return pl.pallas_call(
+        functools.partial(grads_kernel, len(xs)),
         grid=(width // BLOCK,),
         in_specs=[
-            pl.BlockSpec((token_slots, BLOCK), lambda j: (0, j)),
+            pl.BlockSpec((token_slots, BLOCK), lambda j: (0, jnp.minimum(j, blocks - 1))),
+            *[pl.BlockSpec((token_slots, BLOCK), lambda j: (0, 0)) for _ in xs[1:]],
             pl.BlockSpec((token_slots, features), lambda j: (0, 0)),
             pl.BlockSpec((token_slots, LANES), lambda j: (0, features // LANES)),
             pl.BlockSpec((token_slots, columns), lambda j: (0, 0)),
@@ -210,7 +216,7 @@
             bytes_accessed=2 * (2 * columns + token_slots) * (width + features),
             transcendentals=0,
         ),
-    )(received_input, received, received, backward_rows, adapter_down)
+    )(*xs, received, received, backward_rows, adapter_down)
 
 
 def finish_kernel(
@@ -302,9 +308,53 @@
         out_specs=whole,
         out_shape=jax.ShapeDtypeStruct((2 * share, features), jnp.bfloat16),
         cost_estimate=pl.CostEstimate(
-            flops=PAIR_FLOPS, bytes_accessed=10 * share * features, transcendentals=0
+            flops=EARLY_FLOPS, bytes_accessed=10 * share * features, transcendentals=0
         ),
     )(layer[None], below, above, over)
+
+
+def to_owners_kernel(rows, at_ref, *refs):
+    count = len(refs) // 2
+    for turn in range(count):
+        start = pl.multiple_of(lax.bitwise_xor(at_ref[0], turn) * rows, rows)
+        for block in range(count):
+            refs[count + turn][block * rows : (block + 1) * rows] = refs[block][
+                pl.ds(start, rows)
+            ]
+
+
+def to_owners(at, blocks):
+    whole = pl.BlockSpec(memory_space=pltpu.VMEM)
+    return pl.pallas_call(
+        functools.partial(to_owners_kernel, blocks[0].shape[0] // len(blocks)),
+        in_specs=[pl.BlockSpec(memory_space=pltpu.SMEM)] + [whole] * len(blocks),
+        out_specs=[whole] * len(blocks),
+        out_shape=[jax.ShapeDtypeStruct(b.shape, b.dtype) for b in blocks],
+        cost_estimate=pl.CostEstimate(
+            flops=EARLY_FLOPS, bytes_accessed=4 * len(blocks) * blocks[0].size, transcendentals=0
+        ),
+    )(at, *blocks)
+
+
+def by_sender_kernel(rows, at_ref, *refs):
+    count = len(refs) - 1
+    for turn in range(count):
+        for block in range(count):
+            layer = lax.bitwise_xor(at_ref[1], block)
+            sender = layer * count + lax.bitwise_xor(at_ref[0], turn)
+            start = pl.multiple_of(sender * rows, rows)
+            refs[count][pl.ds(start, rows)] = refs[turn][block * rows : (block + 1) * rows]
+
+
+def by_sender(at, blocks):
+    whole = pl.BlockSpec(memory_space=pltpu.VMEM)
+    slots, columns = blocks[0].shape
+    return pl.pallas_call(
+        functools.partial(by_sender_kernel, slots // len(blocks)),
+        in_specs=[pl.BlockSpec(memory_space=pltpu.SMEM)] + [whole] * len(blocks),
+        out_specs=whole,
+        out_shape=jax.ShapeDtypeStruct((slots * len(blocks), columns), jnp.bfloat16),
+    )(at, *blocks)
 
 
 def local(activations, cotangent, family, value_weight, adapter_down, adapter_up):
@@ -328,6 +378,10 @@
         pairs = [(j * inner + at, k * inner + at) for j, k in layers for at in range(inner)]
         return lax.ppermute(block, "adapter", pairs)
 
+    def turned(block, bits, step):
+        pairs = [(j, (j // step ^ bits) * step + j % step) for j in range(count)]
+        return lax.ppermute(block, "adapter", pairs)
+
     def pick(layer, *blocks):
         return lax.select_n(layer, *blocks)
 
@@ -353,7 +407,8 @@
 
     send, place, back_place = pack(family, cotangent, cap, token_slots)
     received = lax.all_to_all(send, "adapter", split_axis=0, concat_axis=0, tiled=True)
-    send_x = pack_x(place, activations)
+    split = deep == inner == 4 and width > BLOCK
+    send_x = pack_x(place, activations, width - BLOCK if split else None)
     received, own_share, cotangent, send_x = lax.optimization_barrier(
         (received, own_share, cotangent, send_x)
     )
@@ -368,6 +423,15 @@
 
     if deep == 4:
         hops.append(send_layers(make_pair(my_layer, *hops), ((1, 0), (2, 3))))
+    crossed = []
+    if split:
+        last = dot(place, activations[:, width - BLOCK :], ((1,), (0,))).astype(jnp.bfloat16)
+        last, backward_rows = lax.optimization_barrier((last, backward_rows))
+        slots = token_slots // deep
+        for k in range(deep):
+            start = lax.bitwise_xor(my_layer, jnp.int32(k)) * slots
+            block = lax.dynamic_slice_in_dim(last, start, slots, 0)
+            crossed.append(turned(block, k, inner) if k else block)
     received_input, adapter_rows, plane_dy, hops = lax.optimization_barrier(
         (received_input, adapter_rows, plane_dy, hops)
     )
@@ -395,15 +459,21 @@
 
     blocks = [dot(block, plane_weight, ((1,), (1,))).astype(jnp.bfloat16) for block in plane_dy]
     blocks = blocks[:1] + [around_groups(block, s) for s, block in enumerate(blocks) if s]
+    at = jnp.stack([my_inner, my_layer]).astype(jnp.int32)
+    xs = [received_input]
+    if split:
+        crossed = to_owners(at, crossed)
+        crossed = [turned(block, k, 1) if k else block for k, block in enumerate(crossed)]
+        xs.append(by_sender(at, crossed))
     base = []
     for shift in range(inner):
         for block in blocks:
             piece = block[shift * tok_rows : (shift + 1) * tok_rows]
             base.append(around_plane(piece, shift) if shift else piece)
     base = jnp.stack(base)
-    received_input, base = lax.optimization_barrier((received_input, base))
+    xs, base = lax.optimization_barrier((xs, base))
     grad_down, grad_up = make_grads(
-        received_input, received, backward_rows, adapter_up, adapter_down
+        xs, received, backward_rows, adapter_up, adapter_down
     )
     at = jnp.stack([my_inner, my_group]).astype(jnp.int32)
     input_gradient = finish(at, back_place, returned_rows, base, deep, groups)

time: 242 us -> 237 us (0.979)
  waiting for transfers between devices: 158 us -> 130 us
  starting transfers between devices: 42.2 us -> 49.9 us
  local copies, waits for them, and re-layouts: 3.96 us -> 11.6 us
  matrix products: 2.57 us -> 5.89 us
  Pallas kernels: 31.9 us -> 34.9 us
    all_to_all x1, waiting for transfers between devices: 29.1 us -> 2.02 us  [local(): lax.all_to_all(adapter_rows, 'adapter', split_axis=0, concat_axis=0, tile...]
    ppermute x2, waiting for transfers between devices: 26.9 us -> 0.01 us  [around_groups(): return lax.ppermute(block, 'groups', pairs)]
    ppermute x0 -> x6, waiting for transfers between devices: none -> 18.4 us  [turned(): return lax.ppermute(block, 'adapter', pairs)]
    all_to_all x1, waiting for transfers between devices: 15.9 us -> 21.4 us  [local(): lax.all_to_all(send_x, 'adapter', split_axis=0, concat_axis=0, tiled=True)]
    ppermute x9, starting transfers between devices: 12.7 us -> 16.9 us  [around_plane(): return lax.ppermute(block, 'adapter', pairs)]
    unnamed x35 -> x37, local copies, waits for them, and re-layouts: 2.33 us -> 6.51 us
    ppermute x9, waiting for transfers between devices: 51.6 us -> 55.7 us  [around_plane(): return lax.ppermute(block, 'adapter', pairs)]
    dot_general x2 -> x3, matrix products: 2.57 us -> 5.89 us  [dot(): lax.dot_general(a, b, (dims, ((), ())), preferred_element_type=jnp.float32)]
  transfers between devices with their start and end apart: 18 -> 24, of which waited for: 12 -> 13; matrix products, arithmetic and copies ran while one was open for 2% -> 6% of each run, Pallas kernels for 11% -> 12%
where the time goes in v6:
time: 237 us; the launch traced here: 236 us
  waiting for transfers between devices  130 us (55%)
  starting transfers between devices  49.9 us (21%)
  Pallas kernels  34.9 us (15%)
  local copies, waits for them, and re-layouts  11.6 us (5%)
  matrix products  5.89 us (2%)
    ppermute x9, waiting for transfers between devices, around_plane(): return lax.ppermute(block, 'adapter', pairs)  55.7 us
    ppermute x2, waiting for transfers between devices, next_layer(): return lax.ppermute(block, 'adapter', pairs)  26.1 us
    all_to_all x1, waiting for transfers between devices, local(): lax.all_to_all(send_x, 'adapter', split_axis=0, concat_axis=0, tiled=True)  21.4 us
    ppermute x6, waiting for transfers between devices, turned(): return lax.ppermute(block, 'adapter', pairs)  18.4 us
    ppermute x9, starting transfers between devices, around_plane(): return lax.ppermute(block, 'adapter', pairs)  16.9 us
    pallas_call x1, Pallas kernels, make_grads(): pl.pallas_call(functools.partial(grads_kernel, len(xs)), grid=(width // B...  11.2 us
    all_to_all x1, starting transfers between devices, local(): lax.all_to_all(send_x, 'adapter', split_axis=0, concat_axis=0, tiled=True)  8.64 us
    pallas_call x1, Pallas kernels, make_rows(): pl.pallas_call(rows_kernel, in_specs=[pl.BlockSpec(memory_space=pl.ANY)]...  7.39 us
  transfers between devices with their start and end apart: 24, of which 13 were waited for; matrix products, arithmetic and copies ran while one was open for 6% of the time, Pallas kernels for 12%

profile of v6, /device:TPU:15, one launch (start us, length us, event | category | flops | bytes accessed | tf_op | source)
XLA Modules:
  0.0 236.0 jit_solution(11786353680734057141)
XLA Ops:
  4.1 6.6 %all-to-all-start = ((bf16[16,16,1152]{2,1,0:T(8,128)(2,1)}), bf16[16,16,1152]{2,1,0:T(8,128)(2,1)S(1)}, u32[]{:S(2)}, u32[]{:S(2)}) async-start(bf16[16,16,1152]{2,1,0:T(8,128)(2,1)} %bitcast.55), calls=%async_computation | async-start | bytes 1179648 | tf_op jit(solution)/shard_map/all_to_all | solution.py:409
  10.7 3.1 %collective-permute-start.4 = (bf16[256,1024]{1,0:T(8,128)(2,1)S(1)}, bf16[256,1024]{1,0:T(8,128)(2,1)S(1)}, u32[]{:S(2)}, u32[]{:S(2)}) collective-permute-start(bf16[256,1024]{1,0:T(8,128)(2,1)S(1)} %constant_dynamic-slice_fusion.4), channel_id=1, source_target_pairs={{0,4},{1,5},{2,6},{3,7},{4,8},{5,9},{6,10},{7,11},{8,12},{9,13},{1... | collective-permute-start | bytes 1572872 | tf_op jit(solution)/shard_map/ppermute | solution.py:375
  16.0 3.7 %shard_map.86 = bf16[256,7168]{1,0:T(8,128)(2,1)} custom-call(bf16[256,128]{1,0:T(8,128)(2,1)} %get-tuple-element.39.place_ref, bf16[128,8192]{1,0:T(8,128)(2,1)} %x_ref.1), custom_call_target="tpu_custom_call" | custom-call | flops 469762048 | bytes 5505024 | tf_op jit(solution)/shard_map/pallas_call | solution.py:70
  19.7 6.8 %all-to-all-done = bf16[16,16,1152]{2,1,0:T(8,128)(2,1)S(1)} async-done(((bf16[16,16,1152]{2,1,0:T(8,128)(2,1)}), bf16[16,16,1152]{2,1,0:T(8,128)(2,1)S(1)}, u32[]{:S(2)}, u32[]{:S(2)}) %all-to-all-start) | async-done | bytes 589856 | tf_op jit(solution)/shard_map/all_to_all | solution.py:409
  27.8 8.6 %all-to-all-start.1 = ((bf16[16,16,7168]{2,1,0:T(8,128)(2,1)}), bf16[16,16,7168]{2,1,0:T(8,128)(2,1)}, u32[]{:S(2)}, u32[]{:S(2)}) async-start(bf16[16,16,7168]{2,1,0:T(8,128)(2,1)} %bitcast.52), calls=%async_computation.1 | async-start | bytes 7340032 | tf_op jit(solution)/shard_map/all_to_all | solution.py:417
  36.8 9.3 %collective-permute-done.4.below_ref = bf16[256,1024]{1,0:T(8,128)(2,1)S(1)} collective-permute-done((bf16[256,1024]{1,0:T(8,128)(2,1)S(1)}, bf16[256,1024]{1,0:T(8,128)(2,1)S(1)}, u32[]{:S(2)}, u32[]{:S(2)}) %collective-permute-start.4) | collective-permute-done | bytes 524320 | tf_op jit(solution)/shard_map/ppermute | solution.py:375
  46.1 16.8 %collective-permute-done.5.above_ref = bf16[256,1024]{1,0:T(8,128)(2,1)S(1)} collective-permute-done((bf16[256,1024]{1,0:T(8,128)(2,1)S(1)}, bf16[256,1024]{1,0:T(8,128)(2,1)S(1)}, u32[]{:S(2)}, u32[]{:S(2)}) %collective-permute-start.5) | collective-permute-done | bytes 524320 | tf_op jit(solution)/shard_map/ppermute | solution.py:375
  63.7 2.4 %shard_map.88 = bf16[512,1024]{1,0:T(8,128)(2,1)} custom-call(s32[1]{0:T(128)} %bitcast.9.layer_ref, bf16[256,1024]{1,0:T(8,128)(2,1)} %copy-done.8, bf16[256,1024]{1,0:T(8,128)(2,1)} %copy-done.10, bf16[256,1024]{1,0:T(8,128)(2,1)} %collective-permute-done.6.over_ref), custom_call_target="tpu_custom_call" | custom-call | flops 99999997952 | bytes 2621440 | tf_op jit(solution)/shard_map/pallas_call | solution.py:305
  66.1 2.3 collective-permute-start.7
  69.8 5.2 %collective-permute-start.2 = (bf16[2,128,1024]{2,1,0:T(8,128)(2,1)S(1)}, bf16[2,128,1024]{2,1,0:T(8,128)(2,1)}, u32[]{:S(2)}, u32[]{:S(2)}) collective-permute-start(bf16[2,128,1024]{2,1,0:T(8,128)(2,1)S(1)} %pad_maximum_fusion.1), channel_id=1, source_target_pairs={{0,2},{1,3},{2,0},{3,1},{4,6},{5,7},{6,4},{7,5},{8,10},{9,11},{10,... | collective-permute-start | bytes 1572872 | tf_op jit(solution)/shard_map/ppermute | solution.py:398
  77.4 7.4 %shard_map.87 = (bf16[256,8192]{1,0:T(8,128)(2,1)}, bf16[256,512]{1,0:T(8,128)(2,1)}) custom-call(bf16[256,1152]{1,0:T(8,128)(2,1)} %bitcast.49, bf16[512,1024]{1,0:T(8,128)(2,1)} %up_ref.1, bf16[8192,512]{1,0:T(8,128)(2,1)} %refs_5_.1), custom_call_target="tpu_custom_call" | custom-call | flops 2415919104 | bytes 14155776 | tf_op jit(solution)/shard_map/pallas_call | solution.py:137
  85.6 11.9 %collective-permute-done.1 = bf16[2,128,1024]{2,1,0:T(8,128)(2,1)S(1)} collective-permute-done((bf16[2,128,1024]{2,1,0:T(8,128)(2,1)S(1)}, bf16[2,128,1024]{2,1,0:T(8,128)(2,1)S(1)}, u32[]{:S(2)}, u32[]{:S(2)}) %collective-permute-start.1) | collective-permute-done | bytes 524320 | tf_op jit(solution)/shard_map/ppermute | solution.py:398
  97.5 14.3 %collective-permute-done.3 = bf16[2,128,1024]{2,1,0:T(8,128)(2,1)} collective-permute-done((bf16[2,128,1024]{2,1,0:T(8,128)(2,1)S(1)}, bf16[2,128,1024]{2,1,0:T(8,128)(2,1)}, u32[]{:S(2)}, u32[]{:S(2)}) %collective-permute-start.3) | collective-permute-done | bytes 524320 | tf_op jit(solution)/shard_map/ppermute | solution.py:398
  111.9 21.4 %all-to-all-done.1 = bf16[16,16,7168]{2,1,0:T(8,128)(2,1)} async-done(((bf16[16,16,7168]{2,1,0:T(8,128)(2,1)}), bf16[16,16,7168]{2,1,0:T(8,128)(2,1)}, u32[]{:S(2)}, u32[]{:S(2)}) %all-to-all-start.1) | async-done | bytes 3670048 | tf_op jit(solution)/shard_map/all_to_all | solution.py:417
  133.2 6.0 %all-to-all-start.2 = ((bf16[16,16,8192]{2,1,0:T(8,128)(2,1)}), bf16[16,16,8192]{2,1,0:T(8,128)(2,1)}, u32[]{:S(2)}, u32[]{:S(2)}) async-start(bf16[16,16,8192]{2,1,0:T(8,128)(2,1)} %bitcast.53), calls=%async_computation.2 | async-start | bytes 8388608 | tf_op jit(solution)/shard_map/all_to_all | solution.py:438
  150.8 14.9 %collective-permute-done.12.refs_2_ = bf16[64,1024]{1,0:T(8,128)(2,1)} collective-permute-done((bf16[64,1024]{1,0:T(8,128)(2,1)}, bf16[64,1024]{1,0:T(8,128)(2,1)}, u32[]{:S(2)}, u32[]{:S(2)}) %collective-permute-start.12) | collective-permute-done | bytes 131104 | tf_op jit(solution)/shard_map/ppermute | solution.py:383
  165.7 3.4 %collective-permute-done.13.refs_3_ = bf16[64,1024]{1,0:T(8,128)(2,1)} collective-permute-done((bf16[64,1024]{1,0:T(8,128)(2,1)}, bf16[64,1024]{1,0:T(8,128)(2,1)}, u32[]{:S(2)}, u32[]{:S(2)}) %collective-permute-start.13) | collective-permute-done | bytes 131104 | tf_op jit(solution)/shard_map/ppermute | solution.py:383
  171.1 2.4 %convolution_convert_fusion.1 = bf16[512,1024]{1,0:T(8,128)(2,1)S(1)} fusion(bf16[128,1024]{1,0:T(8,128)(2,1)S(1)} %get-tuple-element.84, bf16[128,1024]{1,0:T(8,128)(2,1)} %get-tuple-element.89, bf16[128,1024]{1,0:T(8,128)(2,1)} %get-tuple-element.80, bf16[128,1024]{1,0:T(8,128)(2,1)} %get-tuple-element.91, bf16[256,1024]{1,0:T(8,128)(2,1)S(1)} %copy-done.13, ...), kind=kOutput, calls=%fused_computation.2 | convolution fusion | flops 1086849024 | bytes 4194304 | tf_op jit(solution)/shard_map/dot_general | solution.py:23
  180.2 6.4 %collective-permute-start.20 = (bf16[128,1024]{1,0:T(8,128)(2,1)S(1)}, bf16[128,1024]{1,0:T(8,128)(2,1)S(1)}, u32[]{:S(2)}, u32[]{:S(2)}) collective-permute-start(bf16[128,1024]{1,0:T(8,128)(2,1)S(1)} %get-tuple-element.71), channel_id=1, source_target_pairs={{0,3},{1,0},{2,1},{3,2},{4,7},{5,4},{6,5},{7,6},{8,11},{9,8},{10,9... | collective-permute-start | bytes 786440 | tf_op jit(solution)/shard_map/ppermute | solution.py:398
  186.6 15.0 %collective-permute-done.16 = bf16[128,1024]{1,0:T(8,128)(2,1)S(1)} collective-permute-done((bf16[128,1024]{1,0:T(8,128)(2,1)S(1)}, bf16[128,1024]{1,0:T(8,128)(2,1)S(1)}, u32[]{:S(2)}, u32[]{:S(2)}) %collective-permute-start.16) | collective-permute-done | bytes 262176 | tf_op jit(solution)/shard_map/ppermute | solution.py:398
  201.7 12.3 %collective-permute-done.18 = bf16[128,1024]{1,0:T(8,128)(2,1)S(1)} collective-permute-done((bf16[128,1024]{1,0:T(8,128)(2,1)S(1)}, bf16[128,1024]{1,0:T(8,128)(2,1)S(1)}, u32[]{:S(2)}, u32[]{:S(2)}) %collective-permute-start.18) | collective-permute-done | bytes 262176 | tf_op jit(solution)/shard_map/ppermute | solution.py:398
  215.2 3.4 %copy-done.1 = bf16[8192,512]{1,0:T(8,128)(2,1)S(1)} copy-done((bf16[8192,512]{1,0:T(8,128)(2,1)S(1)}, bf16[8192,512]{1,0:T(8,128)(2,1)}, u32[]{:S(2)}) %copy-start.1) | copy-done | bytes 8388632
  218.6 11.2 %shard_map.92 = (bf16[8192,512]{1,0:T(8,128)(2,1)}, bf16[512,1024]{1,0:T(8,128)(2,1)}) custom-call(bf16[256,7168]{1,0:T(8,128)(2,1)} %bitcast.6.refs_0_, bf16[256,1024]{1,0:T(8,128)(2,1)S(1)} %copy-done.4, bf16[256,1152]{1,0:T(8,128)(2,1)S(1)} %bitcast.50, bf16[256,1152]{1,0:T(8,128)(2,1)S(1)} %bitcast.51, bf16[256,512]{1,0:T(8,128)(2,1)S(1)} %copy-done.6, ...), custom_call_target="tpu_custom_call" | custom-call | flops 4563402752 | bytes 23592960 | tf_op jit(solution)/shard_map/pallas_call | solution.py:193
  231.8 4.0 %shard_map.91 = bf16[128,8192]{1,0:T(8,128)(2,1)} custom-call(s32[2]{0:T(128)S(1)} %pad_add_fusion.at_ref, bf16[128,256]{1,0:T(8,128)(2,1)S(1)} %copy-done.5, bf16[256,8192]{1,0:T(8,128)(2,1)} %bitcast.11.rows_ref, bf16[8,128,1024]{2,1,0:T(8,128)(2,1)S(1)} %bitcast_dynamic-update-slice_fusion.base), custom_call_target="tpu_custom_call" | custom-call | flops 536870912 | bytes 8388608 | tf_op jit(solution)/shard_map/pallas_call | solution.py:264
  (83 shorter events, 36.1 us)
Async XLA Ops:
  4.1 22.4 %all-to-all-start = ((bf16[16,16,1152]{2,1,0:T(8,128)(2,1)}), bf16[16,16,1152]{2,1,0:T(8,128)(2,1)S(1)}, u32[]{:S(2)}, u32[]{:S(2)}) async-start(bf16[16,16,1152]{2,1,0:T(8,128)(2,1)} %bitcast.55), calls=%async_computation | async-start | bytes 1179648 | tf_op jit(solution)/shard_map/all_to_all | solution.py:409
  10.7 35.4 %collective-permute-start.4 = (bf16[256,1024]{1,0:T(8,128)(2,1)S(1)}, bf16[256,1024]{1,0:T(8,128)(2,1)S(1)}, u32[]{:S(2)}, u32[]{:S(2)}) collective-permute-start(bf16[256,1024]{1,0:T(8,128)(2,1)S(1)} %constant_dynamic-slice_fusion.4), channel_id=1, source_target_pairs={{0,4},{1,5},{2,6},{3,7},{4,8},{5,9},{6,10},{7,11},{8,12},{9,13},{1... | collective-permute-start | bytes 1572872 | tf_op jit(solution)/shard_map/ppermute | solution.py:375
  13.8 49.1 %collective-permute-start.5 = (bf16[256,1024]{1,0:T(8,128)(2,1)S(1)}, bf16[256,1024]{1,0:T(8,128)(2,1)S(1)}, u32[]{:S(2)}, u32[]{:S(2)}) collective-permute-start(bf16[256,1024]{1,0:T(8,128)(2,1)S(1)} %constant_dynamic-slice_fusion.4), channel_id=1, source_target_pairs={{4,0},{5,1},{6,2},{7,3},{8,4},{9,5},{10,6},{11,7},{12,8},{13,9},{1... | collective-permute-start | bytes 1572872 | tf_op jit(solution)/shard_map/ppermute | solution.py:375
  26.5 36.4 %collective-permute-start.6 = (bf16[256,1024]{1,0:T(8,128)(2,1)S(1)}, bf16[256,1024]{1,0:T(8,128)(2,1)}, u32[]{:S(2)}, u32[]{:S(2)}) collective-permute-start(bf16[256,1024]{1,0:T(8,128)(2,1)S(1)} %constant_dynamic-slice_fusion.4), channel_id=1, source_target_pairs={{0,8},{1,9},{2,10},{3,11},{12,4},{13,5},{14,6},{15,7},{16,24},{17,... | collective-permute-start | bytes 1572872 | tf_op jit(solution)/shard_map/ppermute | solution.py:379
  27.8 105.4 %all-to-all-start.1 = ((bf16[16,16,7168]{2,1,0:T(8,128)(2,1)}), bf16[16,16,7168]{2,1,0:T(8,128)(2,1)}, u32[]{:S(2)}, u32[]{:S(2)}) async-start(bf16[16,16,7168]{2,1,0:T(8,128)(2,1)} %bitcast.52), calls=%async_computation.1 | async-start | bytes 7340032 | tf_op jit(solution)/shard_map/all_to_all | solution.py:417
  36.5 31.9 %collective-permute-start = (bf16[128,1024]{1,0:T(8,128)(2,1)S(1)}, bf16[128,1024]{1,0:T(8,128)(2,1)S(1)}, u32[]{:S(2)}, u32[]{:S(2)}) collective-permute-start(bf16[128,1024]{1,0:T(8,128)(2,1)S(1)} %copy-done.7), channel_id=1, source_target_pairs={{0,16},{16,0},{1,17},{17,1},{2,18},{18,2},{3,19},{19,3},{4,20},{20... | collective-permute-start | bytes 786440 | tf_op jit(solution)/shard_map/ppermute | solution.py:390
  66.1 45.8 %collective-permute-start.7 = (bf16[512,1024]{1,0:T(8,128)(2,1)}, bf16[512,1024]{1,0:T(8,128)(2,1)}, u32[]{:S(2)}, u32[]{:S(2)}) collective-permute-start(bf16[512,1024]{1,0:T(8,128)(2,1)} %shard_map.88), channel_id=1, source_target_pairs={{4,0},{5,1},{6,2},{7,3},{8,12},{9,13},{10,14},{11,15},{20,16},{21,... | collective-permute-start | bytes 3145736 | tf_op jit(solution)/shard_map/ppermute | solution.py:379
  68.5 29.0 %collective-permute-start.1 = (bf16[2,128,1024]{2,1,0:T(8,128)(2,1)S(1)}, bf16[2,128,1024]{2,1,0:T(8,128)(2,1)S(1)}, u32[]{:S(2)}, u32[]{:S(2)}) collective-permute-start(bf16[2,128,1024]{2,1,0:T(8,128)(2,1)S(1)} %pad_maximum_fusion.1), channel_id=1, source_target_pairs={{0,3},{1,0},{2,1},{3,2},{4,7},{5,4},{6,5},{7,6},{8,11},{9,8},{10,9... | collective-permute-start | bytes 1572872 | tf_op jit(solution)/shard_map/ppermute | solution.py:398
  69.8 27.8 %collective-permute-start.2 = (bf16[2,128,1024]{2,1,0:T(8,128)(2,1)S(1)}, bf16[2,128,1024]{2,1,0:T(8,128)(2,1)}, u32[]{:S(2)}, u32[]{:S(2)}) collective-permute-start(bf16[2,128,1024]{2,1,0:T(8,128)(2,1)S(1)} %pad_maximum_fusion.1), channel_id=1, source_target_pairs={{0,2},{1,3},{2,0},{3,1},{4,6},{5,7},{6,4},{7,5},{8,10},{9,11},{10,... | collective-permute-start | bytes 1572872 | tf_op jit(solution)/shard_map/ppermute | solution.py:398
  74.9 36.9 %collective-permute-start.3 = (bf16[2,128,1024]{2,1,0:T(8,128)(2,1)S(1)}, bf16[2,128,1024]{2,1,0:T(8,128)(2,1)}, u32[]{:S(2)}, u32[]{:S(2)}) collective-permute-start(bf16[2,128,1024]{2,1,0:T(8,128)(2,1)S(1)} %pad_maximum_fusion.1), channel_id=1, source_target_pairs={{0,1},{1,2},{2,3},{3,0},{4,5},{5,6},{6,7},{7,4},{8,9},{9,10},{10,1... | collective-permute-start | bytes 1572872 | tf_op jit(solution)/shard_map/ppermute | solution.py:398
  85.6 60.7 %collective-permute-start.8 = (bf16[64,1024]{1,0:T(8,128)(2,1)}, bf16[64,1024]{1,0:T(8,128)(2,1)}, u32[]{:S(2)}, u32[]{:S(2)}) collective-permute-start(bf16[64,1024]{1,0:T(8,128)(2,1)} %get-tuple-element.87), channel_id=1, source_target_pairs={{0,4},{1,5},{2,6},{3,7},{4,0},{5,1},{6,2},{7,3},{8,12},{9,13},{10,... | collective-permute-start | bytes 393224 | tf_op jit(solution)/shard_map/ppermute | solution.py:383
  97.5 48.8 %collective-permute-start.9 = (bf16[64,1024]{1,0:T(8,128)(2,1)}, bf16[64,1024]{1,0:T(8,128)(2,1)}, u32[]{:S(2)}, u32[]{:S(2)}) collective-permute-start(bf16[64,1024]{1,0:T(8,128)(2,1)} %get-tuple-element.86), channel_id=1, source_target_pairs={{0,8},{1,9},{2,10},{3,11},{4,12},{5,13},{6,14},{7,15},{8,0},{9,1},... | collective-permute-start | bytes 393224 | tf_op jit(solution)/shard_map/ppermute | solution.py:383
  97.5 48.8 %collective-permute-start.10 = (bf16[64,1024]{1,0:T(8,128)(2,1)}, bf16[64,1024]{1,0:T(8,128)(2,1)}, u32[]{:S(2)}, u32[]{:S(2)}) collective-permute-start(bf16[64,1024]{1,0:T(8,128)(2,1)} %get-tuple-element.85), channel_id=1, source_target_pairs={{0,12},{1,13},{2,14},{3,15},{4,8},{5,9},{6,10},{7,11},{8,4},{9,5},... | collective-permute-start | bytes 393224 | tf_op jit(solution)/shard_map/ppermute | solution.py:383
  133.2 98.6 %all-to-all-start.2 = ((bf16[16,16,8192]{2,1,0:T(8,128)(2,1)}), bf16[16,16,8192]{2,1,0:T(8,128)(2,1)}, u32[]{:S(2)}, u32[]{:S(2)}) async-start(bf16[16,16,8192]{2,1,0:T(8,128)(2,1)} %bitcast.53), calls=%async_computation.2 | async-start | bytes 8388608 | tf_op jit(solution)/shard_map/all_to_all | solution.py:438
  146.1 28.8 %collective-permute-start.14 = (bf16[512,1024]{1,0:T(8,128)(2,1)}, bf16[512,1024]{1,0:T(8,128)(2,1)}, u32[]{:S(2)}, u32[]{:S(2)}) collective-permute-start(bf16[512,1024]{1,0:T(8,128)(2,1)} %convolution_convert_fusion), channel_id=1, source_target_pairs={{0,16},{16,0},{1,17},{17,1},{2,18},{18,2},{3,19},{19,3},{4,20},{20... | collective-permute-start | bytes 3145736 | tf_op jit(solution)/shard_map/ppermute | solution.py:390
  148.4 2.4 %collective-permute-start.11 = (bf16[64,1024]{1,0:T(8,128)(2,1)}, bf16[64,1024]{1,0:T(8,128)(2,1)}, u32[]{:S(2)}, u32[]{:S(2)}) collective-permute-start(bf16[64,1024]{1,0:T(8,128)(2,1)} %get-tuple-element.50), channel_id=1, source_target_pairs={{0,1},{1,0},{2,3},{3,2},{4,5},{5,4},{6,7},{7,6},{8,9},{9,8},{10,11... | collective-permute-start | bytes 393224 | tf_op jit(solution)/shard_map/ppermute | solution.py:383
  149.1 16.7 %collective-permute-start.12 = (bf16[64,1024]{1,0:T(8,128)(2,1)}, bf16[64,1024]{1,0:T(8,128)(2,1)}, u32[]{:S(2)}, u32[]{:S(2)}) collective-permute-start(bf16[64,1024]{1,0:T(8,128)(2,1)} %get-tuple-element.51), channel_id=1, source_target_pairs={{0,2},{1,3},{2,0},{3,1},{4,6},{5,7},{6,4},{7,5},{8,10},{9,11},{10,... | collective-permute-start | bytes 393224 | tf_op jit(solution)/shard_map/ppermute | solution.py:383
  149.3 19.8 %collective-permute-start.13 = (bf16[64,1024]{1,0:T(8,128)(2,1)}, bf16[64,1024]{1,0:T(8,128)(2,1)}, u32[]{:S(2)}, u32[]{:S(2)}) collective-permute-start(bf16[64,1024]{1,0:T(8,128)(2,1)} %get-tuple-element.52), channel_id=1, source_target_pairs={{0,3},{1,2},{2,1},{3,0},{4,7},{5,6},{6,5},{7,4},{8,11},{9,10},{10,... | collective-permute-start | bytes 393224 | tf_op jit(solution)/shard_map/ppermute | solution.py:383
  173.6 6.6 %collective-permute-start.15 = (bf16[128,1024]{1,0:T(8,128)(2,1)S(1)}, bf16[128,1024]{1,0:T(8,128)(2,1)S(1)}, u32[]{:S(2)}, u32[]{:S(2)}) collective-permute-start(bf16[128,1024]{1,0:T(8,128)(2,1)S(1)} %get-tuple-element.76), channel_id=1, source_target_pairs={{0,1},{1,2},{2,3},{3,0},{4,5},{5,6},{6,7},{7,4},{8,9},{9,10},{10,1... | collective-permute-start | bytes 786440 | tf_op jit(solution)/shard_map/ppermute | solution.py:398
  173.6 28.0 %collective-permute-start.17 = (bf16[128,1024]{1,0:T(8,128)(2,1)S(1)}, bf16[128,1024]{1,0:T(8,128)(2,1)S(1)}, u32[]{:S(2)}, u32[]{:S(2)}) collective-permute-start(bf16[128,1024]{1,0:T(8,128)(2,1)S(1)} %get-tuple-element.75), channel_id=1, source_target_pairs={{0,2},{1,3},{2,0},{3,1},{4,6},{5,7},{6,4},{7,5},{8,10},{9,11},{10,... | collective-permute-start | bytes 786440 | tf_op jit(solution)/shard_map/ppermute | solution.py:398
  174.9 39.1 %collective-permute-start.19 = (bf16[128,1024]{1,0:T(8,128)(2,1)S(1)}, bf16[128,1024]{1,0:T(8,128)(2,1)S(1)}, u32[]{:S(2)}, u32[]{:S(2)}) collective-permute-start(bf16[128,1024]{1,0:T(8,128)(2,1)S(1)} %get-tuple-element.74), channel_id=1, source_target_pairs={{0,3},{1,0},{2,1},{3,2},{4,7},{5,4},{6,5},{7,6},{8,11},{9,8},{10,9... | collective-permute-start | bytes 786440 | tf_op jit(solution)/shard_map/ppermute | solution.py:398
  176.1 25.5 %collective-permute-start.16 = (bf16[128,1024]{1,0:T(8,128)(2,1)S(1)}, bf16[128,1024]{1,0:T(8,128)(2,1)S(1)}, u32[]{:S(2)}, u32[]{:S(2)}) collective-permute-start(bf16[128,1024]{1,0:T(8,128)(2,1)S(1)} %get-tuple-element.73), channel_id=1, source_target_pairs={{0,1},{1,2},{2,3},{3,0},{4,5},{5,6},{6,7},{7,4},{8,9},{9,10},{10,1... | collective-permute-start | bytes 786440 | tf_op jit(solution)/shard_map/ppermute | solution.py:398
  177.9 36.1 %collective-permute-start.18 = (bf16[128,1024]{1,0:T(8,128)(2,1)S(1)}, bf16[128,1024]{1,0:T(8,128)(2,1)S(1)}, u32[]{:S(2)}, u32[]{:S(2)}) collective-permute-start(bf16[128,1024]{1,0:T(8,128)(2,1)S(1)} %get-tuple-element.72), channel_id=1, source_target_pairs={{0,2},{1,3},{2,0},{3,1},{4,6},{5,7},{6,4},{7,5},{8,10},{9,11},{10,... | collective-permute-start | bytes 786440 | tf_op jit(solution)/shard_map/ppermute | solution.py:398
  180.2 35.0 %collective-permute-start.20 = (bf16[128,1024]{1,0:T(8,128)(2,1)S(1)}, bf16[128,1024]{1,0:T(8,128)(2,1)S(1)}, u32[]{:S(2)}, u32[]{:S(2)}) collective-permute-start(bf16[128,1024]{1,0:T(8,128)(2,1)S(1)} %get-tuple-element.71), channel_id=1, source_target_pairs={{0,3},{1,0},{2,1},{3,2},{4,7},{5,4},{6,5},{7,6},{8,11},{9,8},{10,9... | collective-permute-start | bytes 786440 | tf_op jit(solution)/shard_map/ppermute | solution.py:398
  (15 other events, 207.7 us)

commit v7 on v6

--- a/solution.py
+++ b/solution.py
@@ -23,7 +23,7 @@
     return lax.dot_general(a, b, (dims, ((), ())), preferred_element_type=jnp.float32)
 
 
-def pack_kernel(cap, family_ref, dy_ref, out_ref, place_ref, back_place_ref):
+def pack_kernel(cap, family_ref, dy_ref, out_ref, place_ref):
     tok_rows, features = dy_ref.shape
     token_slots = out_ref.shape[0]
     square = (tok_rows, tok_rows)
@@ -32,28 +32,26 @@
     same = (along // FAM_DEV) == (down // FAM_DEV)
     row = lax.broadcasted_iota(jnp.int32, square, 0)
     column = lax.broadcasted_iota(jnp.int32, square, 1)
-    rank_down = jnp.sum((same & (column < row)).astype(jnp.int32), axis=1, keepdims=True)
-    rank_along = jnp.sum((same & (row < column)).astype(jnp.int32), axis=0, keepdims=True)
-    slot_down = (down[:, :1] // FAM_DEV) * cap + rank_down
-    slot_along = (along[:1] // FAM_DEV) * cap + rank_along
+    rank = jnp.sum((same & (row < column)).astype(jnp.int32), axis=0, keepdims=True)
+    slot = (along[:1] // FAM_DEV) * cap + rank
     slots = lax.broadcasted_iota(jnp.int32, (token_slots, tok_rows), 0)
-    place = jnp.where(slots == slot_along, 1.0, 0.0).astype(jnp.bfloat16)
+    place = jnp.where(slots == slot, 1.0, 0.0).astype(jnp.bfloat16)
     place_ref[...] = place
-    slots = lax.broadcasted_iota(jnp.int32, (tok_rows, token_slots), 1)
-    back_place_ref[...] = jnp.where(slots == slot_down, 1.0, 0.0).astype(jnp.bfloat16)
-    out_ref[:, :features] = dot(place, dy_ref[...], ((1,), (0,))).astype(jnp.bfloat16)
     families = (down % FAM_DEV).astype(jnp.float32)[:, :LANES].astype(jnp.bfloat16)
     out_ref[:, features:] = dot(place, families, ((1,), (0,))).astype(jnp.bfloat16)
+    out_ref[:, :features] = dot(place, dy_ref[...], ((1,), (0,))).astype(jnp.bfloat16)
 
 
 def pack(family, cotangent, cap, token_slots):
     tok_rows, features = cotangent.shape
+    whole = pl.BlockSpec(memory_space=pltpu.VMEM)
     return pl.pallas_call(
         functools.partial(pack_kernel, cap),
+        in_specs=[whole, whole],
+        out_specs=[whole, whole],
         out_shape=[
             jax.ShapeDtypeStruct((token_slots, features + LANES), jnp.bfloat16),
             jax.ShapeDtypeStruct((token_slots, tok_rows), jnp.bfloat16),
-            jax.ShapeDtypeStruct((tok_rows, token_slots), jnp.bfloat16),
         ],
         compiler_params=pltpu.CompilerParams(vmem_limit_bytes=VMEM),
     )(family.reshape(1, tok_rows), cotangent)
@@ -405,7 +403,7 @@
         for step in range(2, deep):
             hops += [next_layer(own_share, step * inner), next_layer(own_share, -step * inner)]
 
-    send, place, back_place = pack(family, cotangent, cap, token_slots)
+    send, place = pack(family, cotangent, cap, token_slots)
     received = lax.all_to_all(send, "adapter", split_axis=0, concat_axis=0, tiled=True)
     split = deep == inner == 4 and width > BLOCK
     send_x = pack_x(place, activations, width - BLOCK if split else None)
@@ -476,7 +474,7 @@
         xs, received, backward_rows, adapter_up, adapter_down
     )
     at = jnp.stack([my_inner, my_group]).astype(jnp.int32)
-    input_gradient = finish(at, back_place, returned_rows, base, deep, groups)
+    input_gradient = finish(at, place.T, returned_rows, base, deep, groups)
     return (input_gradient, grad_down, grad_up)
 
 

time: 237 us -> 237 us (level)
    unnamed x37 -> x41, local copies, waits for them, and re-layouts: 6.51 us -> 7.15 us
where the time goes in v7:
time: 237 us; the launch traced here: 236 us
  waiting for transfers between devices  130 us (55%)
  starting transfers between devices  50 us (21%)
  Pallas kernels  34.8 us (15%)
  local copies, waits for them, and re-layouts  11.6 us (5%)
  matrix products  5.97 us (3%)
  other arithmetic  2.37 us (1%)
    ppermute x9, waiting for transfers between devices, around_plane(): return lax.ppermute(block, 'adapter', pairs)  55.4 us
    ppermute x2, waiting for transfers between devices, next_layer(): return lax.ppermute(block, 'adapter', pairs)  26.1 us
    all_to_all x1, waiting for transfers between devices, local(): lax.all_to_all(send_x, 'adapter', split_axis=0, concat_axis=0, tiled=True)  21.3 us
    ppermute x6, waiting for transfers between devices, turned(): return lax.ppermute(block, 'adapter', pairs)  18.4 us
    ppermute x9, starting transfers between devices, around_plane(): return lax.ppermute(block, 'adapter', pairs)  17.1 us
    pallas_call x1, Pallas kernels, make_grads(): pl.pallas_call(functools.partial(grads_kernel, len(xs)), grid=(width // B...  11.2 us
    all_to_all x1, starting transfers between devices, local(): lax.all_to_all(send_x, 'adapter', split_axis=0, concat_axis=0, tiled=True)  8.63 us
    pallas_call x1, Pallas kernels, make_rows(): pl.pallas_call(rows_kernel, in_specs=[pl.BlockSpec(memory_space=pl.ANY)]...  7.43 us
  transfers between devices with their start and end apart: 24, of which 13 were waited for; matrix products, arithmetic and copies ran while one was open for 6% of the time, Pallas kernels for 12%

profile of v7, /device:TPU:15, one launch (start us, length us, event | category | flops | bytes accessed | tf_op | source)
XLA Modules:
  0.0 235.9 jit_solution(18352457173701772967)
XLA Ops:
  4.1 6.6 %all-to-all-start = ((bf16[16,16,1152]{2,1,0:T(8,128)(2,1)}), bf16[16,16,1152]{2,1,0:T(8,128)(2,1)S(1)}, u32[]{:S(2)}, u32[]{:S(2)}) async-start(bf16[16,16,1152]{2,1,0:T(8,128)(2,1)} %bitcast.57), calls=%async_computation | async-start | bytes 1179648 | tf_op jit(solution)/shard_map/all_to_all | solution.py:407
  10.7 3.1 %collective-permute-start.4 = (bf16[256,1024]{1,0:T(8,128)(2,1)S(1)}, bf16[256,1024]{1,0:T(8,128)(2,1)S(1)}, u32[]{:S(2)}, u32[]{:S(2)}) collective-permute-start(bf16[256,1024]{1,0:T(8,128)(2,1)S(1)} %constant_dynamic-slice_fusion.4), channel_id=1, source_target_pairs={{0,4},{1,5},{2,6},{3,7},{4,8},{5,9},{6,10},{7,11},{8,12},{9,13},{1... | collective-permute-start | bytes 1572872 | tf_op jit(solution)/shard_map/ppermute | solution.py:373
  16.0 3.7 %shard_map.86 = bf16[256,7168]{1,0:T(8,128)(2,1)} custom-call(bf16[256,128]{1,0:T(8,128)(2,1)} %get-tuple-element.35.place_ref, bf16[128,8192]{1,0:T(8,128)(2,1)} %x_ref.1), custom_call_target="tpu_custom_call" | custom-call | flops 469762048 | bytes 5505024 | tf_op jit(solution)/shard_map/pallas_call | solution.py:68
  19.7 6.8 %all-to-all-done = bf16[16,16,1152]{2,1,0:T(8,128)(2,1)S(1)} async-done(((bf16[16,16,1152]{2,1,0:T(8,128)(2,1)}), bf16[16,16,1152]{2,1,0:T(8,128)(2,1)S(1)}, u32[]{:S(2)}, u32[]{:S(2)}) %all-to-all-start) | async-done | bytes 589856 | tf_op jit(solution)/shard_map/all_to_all | solution.py:407
  27.8 8.6 %all-to-all-start.1 = ((bf16[16,16,7168]{2,1,0:T(8,128)(2,1)}), bf16[16,16,7168]{2,1,0:T(8,128)(2,1)}, u32[]{:S(2)}, u32[]{:S(2)}) async-start(bf16[16,16,7168]{2,1,0:T(8,128)(2,1)} %bitcast.54), calls=%async_computation.1 | async-start | bytes 7340032 | tf_op jit(solution)/shard_map/all_to_all | solution.py:415
  36.8 9.3 %collective-permute-done.4.below_ref = bf16[256,1024]{1,0:T(8,128)(2,1)S(1)} collective-permute-done((bf16[256,1024]{1,0:T(8,128)(2,1)S(1)}, bf16[256,1024]{1,0:T(8,128)(2,1)S(1)}, u32[]{:S(2)}, u32[]{:S(2)}) %collective-permute-start.4) | collective-permute-done | bytes 524320 | tf_op jit(solution)/shard_map/ppermute | solution.py:373
  46.1 16.8 %collective-permute-done.5.above_ref = bf16[256,1024]{1,0:T(8,128)(2,1)S(1)} collective-permute-done((bf16[256,1024]{1,0:T(8,128)(2,1)S(1)}, bf16[256,1024]{1,0:T(8,128)(2,1)S(1)}, u32[]{:S(2)}, u32[]{:S(2)}) %collective-permute-start.5) | collective-permute-done | bytes 524320 | tf_op jit(solution)/shard_map/ppermute | solution.py:373
  63.7 2.4 %shard_map.88 = bf16[512,1024]{1,0:T(8,128)(2,1)} custom-call(s32[1]{0:T(128)} %bitcast.10.layer_ref, bf16[256,1024]{1,0:T(8,128)(2,1)} %copy-done.8, bf16[256,1024]{1,0:T(8,128)(2,1)} %copy-done.10, bf16[256,1024]{1,0:T(8,128)(2,1)} %collective-permute-done.6.over_ref), custom_call_target="tpu_custom_call" | custom-call | flops 99999997952 | bytes 2621440 | tf_op jit(solution)/shard_map/pallas_call | solution.py:303
  66.1 2.3 collective-permute-start.7
  69.8 5.2 %collective-permute-start.2 = (bf16[2,128,1024]{2,1,0:T(8,128)(2,1)S(1)}, bf16[2,128,1024]{2,1,0:T(8,128)(2,1)}, u32[]{:S(2)}, u32[]{:S(2)}) collective-permute-start(bf16[2,128,1024]{2,1,0:T(8,128)(2,1)S(1)} %pad_maximum_fusion.1), channel_id=1, source_target_pairs={{0,2},{1,3},{2,0},{3,1},{4,6},{5,7},{6,4},{7,5},{8,10},{9,11},{10,... | collective-permute-start | bytes 1572872 | tf_op jit(solution)/shard_map/ppermute | solution.py:396
  77.5 7.4 %shard_map.87 = (bf16[256,8192]{1,0:T(8,128)(2,1)}, bf16[256,512]{1,0:T(8,128)(2,1)}) custom-call(bf16[256,1152]{1,0:T(8,128)(2,1)} %bitcast.50, bf16[512,1024]{1,0:T(8,128)(2,1)} %up_ref.1, bf16[8192,512]{1,0:T(8,128)(2,1)} %refs_5_.1), custom_call_target="tpu_custom_call" | custom-call | flops 2415919104 | bytes 14155776 | tf_op jit(solution)/shard_map/pallas_call | solution.py:135
  85.8 11.7 %collective-permute-done.1 = bf16[2,128,1024]{2,1,0:T(8,128)(2,1)S(1)} collective-permute-done((bf16[2,128,1024]{2,1,0:T(8,128)(2,1)S(1)}, bf16[2,128,1024]{2,1,0:T(8,128)(2,1)S(1)}, u32[]{:S(2)}, u32[]{:S(2)}) %collective-permute-start.1) | collective-permute-done | bytes 524320 | tf_op jit(solution)/shard_map/ppermute | solution.py:396
  97.5 14.3 %collective-permute-done.3 = bf16[2,128,1024]{2,1,0:T(8,128)(2,1)} collective-permute-done((bf16[2,128,1024]{2,1,0:T(8,128)(2,1)S(1)}, bf16[2,128,1024]{2,1,0:T(8,128)(2,1)}, u32[]{:S(2)}, u32[]{:S(2)}) %collective-permute-start.3) | collective-permute-done | bytes 524320 | tf_op jit(solution)/shard_map/ppermute | solution.py:396
  111.9 21.3 %all-to-all-done.1 = bf16[16,16,7168]{2,1,0:T(8,128)(2,1)} async-done(((bf16[16,16,7168]{2,1,0:T(8,128)(2,1)}), bf16[16,16,7168]{2,1,0:T(8,128)(2,1)}, u32[]{:S(2)}, u32[]{:S(2)}) %all-to-all-start.1) | async-done | bytes 3670048 | tf_op jit(solution)/shard_map/all_to_all | solution.py:415
  133.2 6.0 %all-to-all-start.2 = ((bf16[16,16,8192]{2,1,0:T(8,128)(2,1)}), bf16[16,16,8192]{2,1,0:T(8,128)(2,1)}, u32[]{:S(2)}, u32[]{:S(2)}) async-start(bf16[16,16,8192]{2,1,0:T(8,128)(2,1)} %bitcast.55), calls=%async_computation.2 | async-start | bytes 8388608 | tf_op jit(solution)/shard_map/all_to_all | solution.py:436
  150.8 14.9 %collective-permute-done.12.refs_2_ = bf16[64,1024]{1,0:T(8,128)(2,1)} collective-permute-done((bf16[64,1024]{1,0:T(8,128)(2,1)}, bf16[64,1024]{1,0:T(8,128)(2,1)}, u32[]{:S(2)}, u32[]{:S(2)}) %collective-permute-start.12) | collective-permute-done | bytes 131104 | tf_op jit(solution)/shard_map/ppermute | solution.py:381
  165.7 3.4 %collective-permute-done.13.refs_3_ = bf16[64,1024]{1,0:T(8,128)(2,1)} collective-permute-done((bf16[64,1024]{1,0:T(8,128)(2,1)}, bf16[64,1024]{1,0:T(8,128)(2,1)}, u32[]{:S(2)}, u32[]{:S(2)}) %collective-permute-start.13) | collective-permute-done | bytes 131104 | tf_op jit(solution)/shard_map/ppermute | solution.py:381
  171.1 2.5 %convolution_convert_fusion.1 = bf16[512,1024]{1,0:T(8,128)(2,1)S(1)} fusion(bf16[128,1024]{1,0:T(8,128)(2,1)S(1)} %get-tuple-element.82, bf16[128,1024]{1,0:T(8,128)(2,1)S(1)} %get-tuple-element.87, bf16[128,1024]{1,0:T(8,128)(2,1)} %get-tuple-element.78, bf16[128,1024]{1,0:T(8,128)(2,1)} %get-tuple-element.89, bf16[256,1024]{1,0:T(8,128)(2,1)} %copy-done.14, ...), kind=kOutput, calls=%fused_computation.2 | convolution fusion | flops 1086849024 | bytes 4194304 | tf_op jit(solution)/shard_map/dot_general | solution.py:23
  180.1 6.5 %collective-permute-start.20 = (bf16[128,1024]{1,0:T(8,128)(2,1)S(1)}, bf16[128,1024]{1,0:T(8,128)(2,1)S(1)}, u32[]{:S(2)}, u32[]{:S(2)}) collective-permute-start(bf16[128,1024]{1,0:T(8,128)(2,1)S(1)} %get-tuple-element.69), channel_id=1, source_target_pairs={{0,3},{1,0},{2,1},{3,2},{4,7},{5,4},{6,5},{7,6},{8,11},{9,8},{10,9... | collective-permute-start | bytes 786440 | tf_op jit(solution)/shard_map/ppermute | solution.py:396
  186.7 14.9 %collective-permute-done.16 = bf16[128,1024]{1,0:T(8,128)(2,1)S(1)} collective-permute-done((bf16[128,1024]{1,0:T(8,128)(2,1)S(1)}, bf16[128,1024]{1,0:T(8,128)(2,1)S(1)}, u32[]{:S(2)}, u32[]{:S(2)}) %collective-permute-start.16) | collective-permute-done | bytes 262176 | tf_op jit(solution)/shard_map/ppermute | solution.py:396
  201.6 12.5 %collective-permute-done.18 = bf16[128,1024]{1,0:T(8,128)(2,1)S(1)} collective-permute-done((bf16[128,1024]{1,0:T(8,128)(2,1)S(1)}, bf16[128,1024]{1,0:T(8,128)(2,1)S(1)}, u32[]{:S(2)}, u32[]{:S(2)}) %collective-permute-start.18) | collective-permute-done | bytes 262176 | tf_op jit(solution)/shard_map/ppermute | solution.py:396
  215.3 3.4 %copy-done.1 = bf16[8192,512]{1,0:T(8,128)(2,1)S(1)} copy-done((bf16[8192,512]{1,0:T(8,128)(2,1)S(1)}, bf16[8192,512]{1,0:T(8,128)(2,1)}, u32[]{:S(2)}) %copy-start.1) | copy-done | bytes 8388632
  218.7 11.2 %shard_map.92 = (bf16[8192,512]{1,0:T(8,128)(2,1)}, bf16[512,1024]{1,0:T(8,128)(2,1)}) custom-call(bf16[256,7168]{1,0:T(8,128)(2,1)} %bitcast.7.refs_0_, bf16[256,1024]{1,0:T(8,128)(2,1)S(1)} %copy-done.4, bf16[256,1152]{1,0:T(8,128)(2,1)S(1)} %bitcast.51, bf16[256,1152]{1,0:T(8,128)(2,1)S(1)} %bitcast.52, bf16[256,512]{1,0:T(8,128)(2,1)S(1)} %copy-done.5, ...), custom_call_target="tpu_custom_call" | custom-call | flops 4563402752 | bytes 23592960 | tf_op jit(solution)/shard_map/pallas_call | solution.py:191
  231.8 3.9 %shard_map.91 = bf16[128,8192]{1,0:T(8,128)(2,1)} custom-call(s32[2]{0:T(128)S(1)} %pad_add_fusion.at_ref, bf16[128,256]{1,0:T(8,128)(2,1)S(1)} %bitcast.53, bf16[256,8192]{1,0:T(8,128)(2,1)} %bitcast.12.rows_ref, bf16[8,128,1024]{2,1,0:T(8,128)(2,1)S(1)} %bitcast_dynamic-update-slice_fusion.base), custom_call_target="tpu_custom_call" | custom-call | flops 536870912 | bytes 8388608 | tf_op jit(solution)/shard_map/pallas_call | solution.py:262
  (88 shorter events, 36.0 us)
Async XLA Ops:
  4.1 22.4 %all-to-all-start = ((bf16[16,16,1152]{2,1,0:T(8,128)(2,1)}), bf16[16,16,1152]{2,1,0:T(8,128)(2,1)S(1)}, u32[]{:S(2)}, u32[]{:S(2)}) async-start(bf16[16,16,1152]{2,1,0:T(8,128)(2,1)} %bitcast.57), calls=%async_computation | async-start | bytes 1179648 | tf_op jit(solution)/shard_map/all_to_all | solution.py:407
  10.7 35.4 %collective-permute-start.4 = (bf16[256,1024]{1,0:T(8,128)(2,1)S(1)}, bf16[256,1024]{1,0:T(8,128)(2,1)S(1)}, u32[]{:S(2)}, u32[]{:S(2)}) collective-permute-start(bf16[256,1024]{1,0:T(8,128)(2,1)S(1)} %constant_dynamic-slice_fusion.4), channel_id=1, source_target_pairs={{0,4},{1,5},{2,6},{3,7},{4,8},{5,9},{6,10},{7,11},{8,12},{9,13},{1... | collective-permute-start | bytes 1572872 | tf_op jit(solution)/shard_map/ppermute | solution.py:373
  13.8 49.1 %collective-permute-start.5 = (bf16[256,1024]{1,0:T(8,128)(2,1)S(1)}, bf16[256,1024]{1,0:T(8,128)(2,1)S(1)}, u32[]{:S(2)}, u32[]{:S(2)}) collective-permute-start(bf16[256,1024]{1,0:T(8,128)(2,1)S(1)} %constant_dynamic-slice_fusion.4), channel_id=1, source_target_pairs={{4,0},{5,1},{6,2},{7,3},{8,4},{9,5},{10,6},{11,7},{12,8},{13,9},{1... | collective-permute-start | bytes 1572872 | tf_op jit(solution)/shard_map/ppermute | solution.py:373
  26.5 36.4 %collective-permute-start.6 = (bf16[256,1024]{1,0:T(8,128)(2,1)S(1)}, bf16[256,1024]{1,0:T(8,128)(2,1)}, u32[]{:S(2)}, u32[]{:S(2)}) collective-permute-start(bf16[256,1024]{1,0:T(8,128)(2,1)S(1)} %constant_dynamic-slice_fusion.4), channel_id=1, source_target_pairs={{0,8},{1,9},{2,10},{3,11},{12,4},{13,5},{14,6},{15,7},{16,24},{17,... | collective-permute-start | bytes 1572872 | tf_op jit(solution)/shard_map/ppermute | solution.py:377
  27.8 105.4 %all-to-all-start.1 = ((bf16[16,16,7168]{2,1,0:T(8,128)(2,1)}), bf16[16,16,7168]{2,1,0:T(8,128)(2,1)}, u32[]{:S(2)}, u32[]{:S(2)}) async-start(bf16[16,16,7168]{2,1,0:T(8,128)(2,1)} %bitcast.54), calls=%async_computation.1 | async-start | bytes 7340032 | tf_op jit(solution)/shard_map/all_to_all | solution.py:415
  36.5 32.0 %collective-permute-start = (bf16[128,1024]{1,0:T(8,128)(2,1)S(1)}, bf16[128,1024]{1,0:T(8,128)(2,1)S(1)}, u32[]{:S(2)}, u32[]{:S(2)}) collective-permute-start(bf16[128,1024]{1,0:T(8,128)(2,1)S(1)} %copy-done.6), channel_id=1, source_target_pairs={{0,16},{16,0},{1,17},{17,1},{2,18},{18,2},{3,19},{19,3},{4,20},{20... | collective-permute-start | bytes 786440 | tf_op jit(solution)/shard_map/ppermute | solution.py:388
  66.1 45.8 %collective-permute-start.7 = (bf16[512,1024]{1,0:T(8,128)(2,1)}, bf16[512,1024]{1,0:T(8,128)(2,1)}, u32[]{:S(2)}, u32[]{:S(2)}) collective-permute-start(bf16[512,1024]{1,0:T(8,128)(2,1)} %shard_map.88), channel_id=1, source_target_pairs={{4,0},{5,1},{6,2},{7,3},{8,12},{9,13},{10,14},{11,15},{20,16},{21,... | collective-permute-start | bytes 3145736 | tf_op jit(solution)/shard_map/ppermute | solution.py:377
  68.5 29.0 %collective-permute-start.1 = (bf16[2,128,1024]{2,1,0:T(8,128)(2,1)S(1)}, bf16[2,128,1024]{2,1,0:T(8,128)(2,1)S(1)}, u32[]{:S(2)}, u32[]{:S(2)}) collective-permute-start(bf16[2,128,1024]{2,1,0:T(8,128)(2,1)S(1)} %pad_maximum_fusion.1), channel_id=1, source_target_pairs={{0,3},{1,0},{2,1},{3,2},{4,7},{5,4},{6,5},{7,6},{8,11},{9,8},{10,9... | collective-permute-start | bytes 1572872 | tf_op jit(solution)/shard_map/ppermute | solution.py:396
  69.8 27.8 %collective-permute-start.2 = (bf16[2,128,1024]{2,1,0:T(8,128)(2,1)S(1)}, bf16[2,128,1024]{2,1,0:T(8,128)(2,1)}, u32[]{:S(2)}, u32[]{:S(2)}) collective-permute-start(bf16[2,128,1024]{2,1,0:T(8,128)(2,1)S(1)} %pad_maximum_fusion.1), channel_id=1, source_target_pairs={{0,2},{1,3},{2,0},{3,1},{4,6},{5,7},{6,4},{7,5},{8,10},{9,11},{10,... | collective-permute-start | bytes 1572872 | tf_op jit(solution)/shard_map/ppermute | solution.py:396
  74.9 36.9 %collective-permute-start.3 = (bf16[2,128,1024]{2,1,0:T(8,128)(2,1)S(1)}, bf16[2,128,1024]{2,1,0:T(8,128)(2,1)}, u32[]{:S(2)}, u32[]{:S(2)}) collective-permute-start(bf16[2,128,1024]{2,1,0:T(8,128)(2,1)S(1)} %pad_maximum_fusion.1), channel_id=1, source_target_pairs={{0,1},{1,2},{2,3},{3,0},{4,5},{5,6},{6,7},{7,4},{8,9},{9,10},{10,1... | collective-permute-start | bytes 1572872 | tf_op jit(solution)/shard_map/ppermute | solution.py:396
  85.8 59.8 %collective-permute-start.8 = (bf16[64,1024]{1,0:T(8,128)(2,1)}, bf16[64,1024]{1,0:T(8,128)(2,1)S(1)}, u32[]{:S(2)}, u32[]{:S(2)}) collective-permute-start(bf16[64,1024]{1,0:T(8,128)(2,1)} %get-tuple-element.85), channel_id=1, source_target_pairs={{0,4},{1,5},{2,6},{3,7},{4,0},{5,1},{6,2},{7,3},{8,12},{9,13},{10,... | collective-permute-start | bytes 393224 | tf_op jit(solution)/shard_map/ppermute | solution.py:381
  97.5 48.1 %collective-permute-start.9 = (bf16[64,1024]{1,0:T(8,128)(2,1)}, bf16[64,1024]{1,0:T(8,128)(2,1)}, u32[]{:S(2)}, u32[]{:S(2)}) collective-permute-start(bf16[64,1024]{1,0:T(8,128)(2,1)} %get-tuple-element.84), channel_id=1, source_target_pairs={{0,8},{1,9},{2,10},{3,11},{4,12},{5,13},{6,14},{7,15},{8,0},{9,1},... | collective-permute-start | bytes 393224 | tf_op jit(solution)/shard_map/ppermute | solution.py:381
  97.5 48.1 %collective-permute-start.10 = (bf16[64,1024]{1,0:T(8,128)(2,1)}, bf16[64,1024]{1,0:T(8,128)(2,1)}, u32[]{:S(2)}, u32[]{:S(2)}) collective-permute-start(bf16[64,1024]{1,0:T(8,128)(2,1)} %get-tuple-element.83), channel_id=1, source_target_pairs={{0,12},{1,13},{2,14},{3,15},{4,8},{5,9},{6,10},{7,11},{8,4},{9,5},... | collective-permute-start | bytes 393224 | tf_op jit(solution)/shard_map/ppermute | solution.py:381
  133.2 98.6 %all-to-all-start.2 = ((bf16[16,16,8192]{2,1,0:T(8,128)(2,1)}), bf16[16,16,8192]{2,1,0:T(8,128)(2,1)}, u32[]{:S(2)}, u32[]{:S(2)}) async-start(bf16[16,16,8192]{2,1,0:T(8,128)(2,1)} %bitcast.55), calls=%async_computation.2 | async-start | bytes 8388608 | tf_op jit(solution)/shard_map/all_to_all | solution.py:436
  145.4 29.6 %collective-permute-start.14 = (bf16[512,1024]{1,0:T(8,128)(2,1)}, bf16[512,1024]{1,0:T(8,128)(2,1)}, u32[]{:S(2)}, u32[]{:S(2)}) collective-permute-start(bf16[512,1024]{1,0:T(8,128)(2,1)} %convolution_convert_fusion), channel_id=1, source_target_pairs={{0,16},{16,0},{1,17},{17,1},{2,18},{18,2},{3,19},{19,3},{4,20},{20... | collective-permute-start | bytes 3145736 | tf_op jit(solution)/shard_map/ppermute | solution.py:388
  148.3 2.5 %collective-permute-start.11 = (bf16[64,1024]{1,0:T(8,128)(2,1)}, bf16[64,1024]{1,0:T(8,128)(2,1)S(1)}, u32[]{:S(2)}, u32[]{:S(2)}) collective-permute-start(bf16[64,1024]{1,0:T(8,128)(2,1)} %get-tuple-element.48), channel_id=1, source_target_pairs={{0,1},{1,0},{2,3},{3,2},{4,5},{5,4},{6,7},{7,6},{8,9},{9,8},{10,11... | collective-permute-start | bytes 393224 | tf_op jit(solution)/shard_map/ppermute | solution.py:381
  148.9 16.8 %collective-permute-start.12 = (bf16[64,1024]{1,0:T(8,128)(2,1)}, bf16[64,1024]{1,0:T(8,128)(2,1)}, u32[]{:S(2)}, u32[]{:S(2)}) collective-permute-start(bf16[64,1024]{1,0:T(8,128)(2,1)} %get-tuple-element.49), channel_id=1, source_target_pairs={{0,2},{1,3},{2,0},{3,1},{4,6},{5,7},{6,4},{7,5},{8,10},{9,11},{10,... | collective-permute-start | bytes 393224 | tf_op jit(solution)/shard_map/ppermute | solution.py:381
  149.2 19.9 %collective-permute-start.13 = (bf16[64,1024]{1,0:T(8,128)(2,1)}, bf16[64,1024]{1,0:T(8,128)(2,1)}, u32[]{:S(2)}, u32[]{:S(2)}) collective-permute-start(bf16[64,1024]{1,0:T(8,128)(2,1)} %get-tuple-element.50), channel_id=1, source_target_pairs={{0,3},{1,2},{2,1},{3,0},{4,7},{5,6},{6,5},{7,4},{8,11},{9,10},{10,... | collective-permute-start | bytes 393224 | tf_op jit(solution)/shard_map/ppermute | solution.py:381
  173.7 6.5 %collective-permute-start.15 = (bf16[128,1024]{1,0:T(8,128)(2,1)S(1)}, bf16[128,1024]{1,0:T(8,128)(2,1)S(1)}, u32[]{:S(2)}, u32[]{:S(2)}) collective-permute-start(bf16[128,1024]{1,0:T(8,128)(2,1)S(1)} %get-tuple-element.74), channel_id=1, source_target_pairs={{0,1},{1,2},{2,3},{3,0},{4,5},{5,6},{6,7},{7,4},{8,9},{9,10},{10,1... | collective-permute-start | bytes 786440 | tf_op jit(solution)/shard_map/ppermute | solution.py:396
  173.7 27.8 %collective-permute-start.17 = (bf16[128,1024]{1,0:T(8,128)(2,1)S(1)}, bf16[128,1024]{1,0:T(8,128)(2,1)S(1)}, u32[]{:S(2)}, u32[]{:S(2)}) collective-permute-start(bf16[128,1024]{1,0:T(8,128)(2,1)S(1)} %get-tuple-element.73), channel_id=1, source_target_pairs={{0,2},{1,3},{2,0},{3,1},{4,6},{5,7},{6,4},{7,5},{8,10},{9,11},{10,... | collective-permute-start | bytes 786440 | tf_op jit(solution)/shard_map/ppermute | solution.py:396
  175.0 39.1 %collective-permute-start.19 = (bf16[128,1024]{1,0:T(8,128)(2,1)S(1)}, bf16[128,1024]{1,0:T(8,128)(2,1)S(1)}, u32[]{:S(2)}, u32[]{:S(2)}) collective-permute-start(bf16[128,1024]{1,0:T(8,128)(2,1)S(1)} %get-tuple-element.72), channel_id=1, source_target_pairs={{0,3},{1,0},{2,1},{3,2},{4,7},{5,4},{6,5},{7,6},{8,11},{9,8},{10,9... | collective-permute-start | bytes 786440 | tf_op jit(solution)/shard_map/ppermute | solution.py:396
  176.2 25.3 %collective-permute-start.16 = (bf16[128,1024]{1,0:T(8,128)(2,1)S(1)}, bf16[128,1024]{1,0:T(8,128)(2,1)S(1)}, u32[]{:S(2)}, u32[]{:S(2)}) collective-permute-start(bf16[128,1024]{1,0:T(8,128)(2,1)S(1)} %get-tuple-element.71), channel_id=1, source_target_pairs={{0,1},{1,2},{2,3},{3,0},{4,5},{5,6},{6,7},{7,4},{8,9},{9,10},{10,1... | collective-permute-start | bytes 786440 | tf_op jit(solution)/shard_map/ppermute | solution.py:396
  178.0 36.1 %collective-permute-start.18 = (bf16[128,1024]{1,0:T(8,128)(2,1)S(1)}, bf16[128,1024]{1,0:T(8,128)(2,1)S(1)}, u32[]{:S(2)}, u32[]{:S(2)}) collective-permute-start(bf16[128,1024]{1,0:T(8,128)(2,1)S(1)} %get-tuple-element.70), channel_id=1, source_target_pairs={{0,2},{1,3},{2,0},{3,1},{4,6},{5,7},{6,4},{7,5},{8,10},{9,11},{10,... | collective-permute-start | bytes 786440 | tf_op jit(solution)/shard_map/ppermute | solution.py:396
  180.1 35.1 %collective-permute-start.20 = (bf16[128,1024]{1,0:T(8,128)(2,1)S(1)}, bf16[128,1024]{1,0:T(8,128)(2,1)S(1)}, u32[]{:S(2)}, u32[]{:S(2)}) collective-permute-start(bf16[128,1024]{1,0:T(8,128)(2,1)S(1)} %get-tuple-element.69), channel_id=1, source_target_pairs={{0,3},{1,0},{2,1},{3,2},{4,7},{5,4},{6,5},{7,6},{8,11},{9,8},{10,9... | collective-permute-start | bytes 786440 | tf_op jit(solution)/shard_map/ppermute | solution.py:396
  (17 other events, 214.4 us)
